TPU v7x, 512 devices: a whole 4x8x8 slice. The times are simulated.
512 devices in a mesh: pixel: 16 (over x, z_hi), trow: 8 (over y), tcol: 4 (over z_lo, core).
Axes of the slice: x: 4, y: 8, z: 8 (z_hi: 4, z_lo: 2; z = z_hi * 2 + z_lo), core: 2. Of those that a mesh axis runs over, the one named last changes fastest.
Arguments:
- counts: int32 [512, 65536], P(('trow', 'tcol'), 'pixel'), may hold values from 2 to 62
- labels: int32 [65536, 1], P('pixel'), may hold values from 0 to 63, as said below
- pixel_mask: int32 [65536], P('pixel'), may hold values from 0 to 1, as said below
- dark_level: float32 [65536], P('pixel'), may hold values from 0 to 3.5
- flat_field: float32 [65536], P('pixel'), may hold values from 0.3 to 3
Outputs:
- two_time: float32 [64, 512, 512], P('pixel', 'trow', 'tcol')
- lag_means: float32 [64, 512], P('pixel')
Inputs may be any that keep to these rules, and one draw needn't show every extreme that they name: `labels`: among the pixels of one index of pixel (aligned blocks of 4096 pixels), no cycle holds more than 128 pixels, and some cycle holds exactly 128; every cycle has pixels in every block. `pixel_mask`: all pixels of one cycle are 0.
All inputs are finite; a program needn't handle non-finite values.
Results may differ from a plain program's by a relative error of at most 0.0003.
Values may be sent and summed in bfloat16 or wider, within the bound.
No kernel may reach another device: no remote copies, remote signals or barrier semaphores. Data moves between devices by JAX's collectives and lax.ppermute only.
A program may use at most 64 MiB of HBM per device.

v0:
```python
import jax
import jax.numpy as jnp
from jax import lax
from jax.sharding import PartitionSpec as P

CYCLES = 64
FRAMES = 512
CAP = 128


def slot_table(block_labels):
    pixels = block_labels.shape[0]
    ordering = jnp.argsort(block_labels, stable=True)
    member = block_labels[:, None] == jnp.arange(CYCLES, dtype=jnp.int32)[None, :]
    cycle_sizes = jnp.sum(member.astype(jnp.int32), axis=0)
    starts = jnp.cumsum(cycle_sizes) - cycle_sizes
    offset = jnp.arange(CAP, dtype=jnp.int32)
    places = jnp.minimum(starts[:, None] + offset[None, :], pixels - 1)
    return (ordering[places].reshape(-1), (offset[None, :] < cycle_sizes[:, None]).reshape(-1))


def per_device(counts, labels, pixel_mask, dark_level, flat_field):
    sub_frames = counts.shape[0]
    n_trow = lax.axis_size("trow")
    n_tcol = lax.axis_size("tcol")
    owned = CYCLES // lax.axis_size("pixel")
    corrected = (
        flat_field * pixel_mask.astype(jnp.float32) * (counts.astype(jnp.float32) - dark_level)
    ).astype(jnp.bfloat16)
    slot_index, usable = slot_table(labels[:, 0])
    live = jnp.where(usable, pixel_mask[slot_index], 0).astype(jnp.float32)
    cycle_sizes = jnp.sum(live.reshape(CYCLES, CAP), axis=1)
    slotted = jnp.where(
        usable[None, :], jnp.take(corrected, slot_index, axis=1), jnp.zeros((), jnp.bfloat16)
    )
    row_block = lax.all_gather(slotted, "tcol", axis=0, tiled=True)
    rows_here = row_block.shape[0]
    row_slots = row_block.reshape(rows_here, CYCLES, CAP)
    row_sums = jnp.sum(row_slots, axis=2, dtype=jnp.float32).T
    anchor = jnp.zeros((), jnp.int32)
    arrived = lax.all_gather(slotted, "trow", axis=0, tiled=True)
    slots = arrived.reshape(arrived.shape[0], CYCLES, CAP)
    product = jnp.einsum("arc,brc->rab", row_slots, slots, preferred_element_type=jnp.float32)
    gram_tile = product
    block_sums = jnp.sum(slots, axis=2, dtype=jnp.float32).T
    column_sums = block_sums
    gram_tile, column_sums = (gram_tile, column_sums)
    gram_tile, row_sums, column_sums, cycle_sizes = lax.psum(
        (gram_tile, row_sums, column_sums, cycle_sizes), "pixel"
    )
    first_cycle = lax.axis_index("pixel") * owned
    gram_tile = lax.dynamic_slice_in_dim(gram_tile, first_cycle, owned, 0)
    row_sums = lax.dynamic_slice_in_dim(row_sums, first_cycle, owned, 0)
    column_sums = lax.dynamic_slice_in_dim(column_sums, first_cycle, owned, 0)
    cycle_sizes = lax.dynamic_slice_in_dim(cycle_sizes, first_cycle, owned, 0)
    correlation = (
        cycle_sizes[:, None, None]
        * gram_tile
        / (jnp.maximum(row_sums, 1.0)[:, :, None] * jnp.maximum(column_sums, 1.0)[:, None, :])
    )
    placed = jnp.zeros((owned, rows_here, n_trow, n_tcol, sub_frames), jnp.float32)
    update = correlation.reshape(owned, rows_here, n_trow, 1, sub_frames)
    placed = lax.dynamic_update_slice(
        placed, update, (anchor, anchor, anchor, lax.axis_index("tcol"), anchor)
    )
    natural = placed.reshape(owned, rows_here, FRAMES)
    widened = jnp.pad(natural, ((0, 0), (0, 0), (0, FRAMES)))
    shifted = lax.dynamic_slice_in_dim(
        widened, lax.axis_index("trow") * rows_here, FRAMES + rows_here, 2
    )
    skewed = jnp.pad(shifted.reshape(owned, -1), ((0, 0), (0, rows_here)))
    skewed = skewed.reshape(owned, rows_here, FRAMES + rows_here + 1)
    partial_lags = jnp.sum(skewed[:, :, :FRAMES], axis=1)
    summed = lax.psum(partial_lags, ("trow", "tcol"))
    lag_means = summed / (FRAMES - jnp.arange(FRAMES)).astype(jnp.float32)
    return (correlation, lag_means)


def solution(mesh):
    placed = (P(("trow", "tcol"), "pixel"), P("pixel", None), P("pixel"), P("pixel"), P("pixel"))
    return jax.shard_map(
        per_device,
        mesh=mesh,
        in_specs=placed,
        out_specs=(P("pixel", "trow", "tcol"), P("pixel", None)),
        check_vma=False,
    )
```

profile of v0, /device:TPU:1, one launch (start us, length us, event | category | flops | bytes accessed | tf_op | source)
XLA Modules:
  0.0 431.5 jit_solution(1267022783187305772)
XLA Ops:
  7.2 0.9 convert_reduce_fusion.2
  8.2 0.1 copy.56
  8.4 0.1 reduce
  8.6 6.5 %sort.17 = (s32[4096]{0:T(1024)}, s32[4096]{0:T(1024)S(1)}) sort(s32[4096]{0:T(1024)} %bitcast.46, s32[4096]{0:T(1024)S(1)} %iota.21), dimensions={0}, to_apply=%region_1.2 | sort | flops 49152 | bytes 65536 | tf_op jit(solution)/shard_map/jit(argsort)/sort | solution.py:13
  15.2 45.5 %gather_fusion = s32[8192]{0:T(1024)S(1)} fusion(s32[4096]{0:T(1024)S(1)} %get-tuple-element.3, s32[8192]{0:T(1024)S(1)} %fusion.4), kind=kCustom, calls=%fused_computation | custom fusion | bytes 98304 | tf_op jit(solution)/shard_map/gather | solution.py:19
  60.9 0.5 copy.57
  61.4 29.2 %gather_fusion.2 = bf16[8192,16]{1,0:T(8,128)(2,1)} fusion(bf16[16,4096]{0,1:T(8,128)(2,1)S(1)} %copy.57, s32[8192]{0:T(1024)S(1)} %broadcast_clamp_fusion), kind=kCustom, calls=%fused_computation.2 | custom fusion | bytes 557056 | tf_op jit(solution)/shard_map/jit(_take)/gather | solution.py:34
  90.6 7.0 %select_bitcast_fusion = bf16[16,8192]{0,1:T(8,128)(2,1)S(1)} fusion(bf16[8192,16]{1,0:T(8,128)(2,1)} %gather_fusion.2, pred[8192]{0:T(1024)(128)(4,1)S(1)} %fusion.7, pred[8192]{0:T(1024)(128)(4,1)S(1)} %compare_and_fusion), kind=kLoop, calls=%fused_computation.4 | loop fusion | flops 262144 | bytes 540672 | tf_op jit(solution)/shard_map/jit(_where)/select_n | solution.py:33
  97.6 1.4 copy.58
  99.1 0.7 all-gather.3.cloned.1.call-update
  99.8 44.8 %all-gather.5.cloned.1.call-done = bf16[128,8192]{1,0:T(8,128)(2,1)} async-done(((bf16[16,8192]{1,0:T(8,128)(2,1)}), bf16[128,8192]{1,0:T(8,128)(2,1)}) %all-gather.5.cloned.1.call-update) | async-done | bytes 2097168 | tf_op jit(solution)/shard_map/all_gather | solution.py:41
  144.6 3.2 copy.60
  147.8 28.3 %all-gather.3.cloned.1.call-done = bf16[64,8192]{1,0:T(8,128)(2,1)} async-done(((bf16[16,8192]{1,0:T(8,128)(2,1)}), bf16[64,8192]{1,0:T(8,128)(2,1)}) %all-gather.3.cloned.1.call-update) | async-done | bytes 1048592 | tf_op jit(solution)/shard_map/all_gather | solution.py:36
  176.2 3.2 fusion
  179.4 45.5 %gather_fusion.1 = s32[8192]{0:T(1024)S(1)} fusion(s32[4096]{0:T(1024)S(1)} %copy-done, s32[8192]{0:T(1024)S(1)} %broadcast_clamp_fusion), kind=kCustom, calls=%fused_computation.1 | custom fusion | bytes 98304 | tf_op jit(solution)/shard_map/gather | solution.py:31
  225.0 0.2 fusion.6
  225.1 0.3 copy.69
  225.4 0.6 convert_reduce_fusion.1
  226.1 0.5 convert_reduce_fusion
  226.6 74.1 %all-reduce.2 = (f32[64,128]{1,0:T(8,128)S(1)}, f32[64,64]{1,0:T(8,128)S(1)}, f32[64]{0:T(128)S(1)}) all-reduce(f32[64,128]{1,0:T(8,128)S(1)} %bitcast.42, f32[64,64]{1,0:T(8,128)S(1)} %bitcast.43, f32[64]{0:T(128)S(1)} %fusion.6), channel_id=1, replica_groups=mesh['pixel'=16,'trow'=8,'tcol'=4] {'pixel'}, use_global_device_ids=true, to_apply=%region_9.10 | all-reduce | flops 12352 | bytes 98816 | tf_op jit(solution)/shard_map/psum | solution.py:48
  300.9 55.9 %all-reduce.5.cloned.1.call-done = f32[64,64,128]{2,1,0:T(8,128)} async-done(((f32[64,64,128]{2,1,0:T(8,128)}), f32[64,64,128]{2,1,0:T(8,128)}) %all-reduce.5.cloned.1.call-update) | async-done | bytes 2097168 | tf_op jit(solution)/shard_map/psum | solution.py:48
  356.8 1.0 multiply_divide_fusion
  357.8 0.1 copy.64
  357.9 0.1 broadcast_in_dim.44
  358.1 0.1 pad_dynamic-slice_fusion
  358.2 0.2 copy-done.2
  358.4 0.4 copy.66
  358.8 0.5 reshape.167
  359.3 0.1 pad.9
  359.4 0.7 reshape.168
  360.2 64.2 %psum.39 = f32[4,512]{1,0:T(4,128)S(1)} all-reduce(f32[4,512]{1,0:T(4,128)S(1)} %slice_reduce_fusion), channel_id=1, replica_groups=mesh['pixel'=16,'trow'=8,'tcol'=4] {'trow','tcol'}, use_global_device_ids=true, to_apply=%region_11.12 | all-reduce | flops 2048 | bytes 16384 | tf_op jit(solution)/shard_map/psum | solution.py:74
  424.4 0.6 broadcast_divide_fusion
  (33 shorter events, 0.8 us)
Async XLA Ops:
  7.2 137.4 %all-gather.5.cloned.1.call-start = ((), (), s32[]{:S(2)}) async-start(), calls=%async_computation.1 | async-start | bytes 2359296 | tf_op jit(solution)/shard_map/all_gather | solution.py:41
  15.1 45.6 %copy-start = (s32[4096]{0:T(1024)S(1)}, s32[4096]{0:T(1024)}, u32[]{:S(2)}) copy-start(s32[4096]{0:T(1024)} %param.7) | copy-start | bytes 49156
  15.1 45.6 %copy-start.4 = (f32[4096]{0:T(1024)S(1)}, f32[4096]{0:T(1024)}, u32[]{:S(2)}) copy-start(f32[4096]{0:T(1024)} %param.9) | copy-start | bytes 49156
  15.1 45.7 %copy-start.3 = (s32[16,4096]{1,0:T(8,128)S(1)}, s32[16,4096]{1,0:T(8,128)}, u32[]{:S(2)}) copy-start(s32[16,4096]{1,0:T(8,128)} %param.5) | copy-start | bytes 786436
  15.2 45.7 %copy-start.5 = (f32[4096]{0:T(1024)S(1)}, f32[4096]{0:T(1024)}, u32[]{:S(2)}) copy-start(f32[4096]{0:T(1024)} %param.8) | copy-start | bytes 49156
  99.0 77.1 %all-gather.3.cloned.1.call-start = ((), (), s32[]{:S(2)}) async-start(), calls=%async_computation | async-start | bytes 1310720 | tf_op jit(solution)/shard_map/all_gather | solution.py:36
  99.8 257.0 %all-reduce.5.cloned.1.call-start = ((), (), s32[]{:S(2)}) async-start(), calls=%async_computation.2 | async-start | bytes 4194304 | tf_op jit(solution)/shard_map/psum | solution.py:48
  179.4 45.7 %copy-start.1 = (bf16[64,8192]{1,0:T(8,128)(2,1)S(1)}, bf16[64,8192]{1,0:T(8,128)(2,1)}, u32[]{:S(2)}) copy-start(bf16[64,8192]{1,0:T(8,128)(2,1)} %all-gather.3.cloned.1.call-done) | copy-start | bytes 3145732
  357.8 0.7 copy-start.2
Sparse Core Ops, SparseCore 0:
  99.2 45.3 all-gather.4
  146.7 29.4 all-gather.2
  179.5 177.2 all-reduce.4
where the time goes:
time: 432 us
  blocking collectives  138 us (32%)
  waiting for transfers between devices  130 us (30%)
  local copies, waits for them, and re-layouts  128 us (30%)
  other arithmetic  17.9 us (4%)
  between operations  14 us (3%)
    psum x1, blocking collectives, per_device(): lax.psum((gram_tile, row_sums, column_sums, cycle_sizes), 'pixel')  74.1 us
    psum x1, blocking collectives, per_device(): summed = lax.psum(partial_lags, ('trow', 'tcol'))  64.2 us
    psum x1, waiting for transfers between devices, per_device(): lax.psum((gram_tile, row_sums, column_sums, cycle_sizes), 'pixel')  55.9 us
    gather x1, local copies, waits for them, and re-layouts, per_device(): live = jnp.where(usable, pixel_mask[slot_index], 0).astype(jnp.float32)  45.5 us
    gather x1, local copies, waits for them, and re-layouts, slot_table(): ordering[places].reshape(-1)  45.5 us
    all_gather x1, waiting for transfers between devices, per_device(): arrived = lax.all_gather(slotted, 'trow', axis=0, tiled=True)  44.8 us
    gather x1, local copies, waits for them, and re-layouts, per_device(): jnp.take(corrected, slot_index, axis=1)  29.2 us
    all_gather x1, waiting for transfers between devices, per_device(): row_block = lax.all_gather(slotted, 'tcol', axis=0, tiled=True)  28.3 us
  transfers between devices with their start and end apart: 3, of which 3 were waited for; matrix products, arithmetic and copies ran while one was open for 12% of the time, Pallas kernels for 0%

commit v1 on v0

v1 whole, which is shorter than its diff:
```python
import jax
import jax.numpy as jnp
from jax import lax
from jax.experimental import pallas as pl
from jax.experimental.pallas import tpu as pltpu
from jax.sharding import PartitionSpec as P

CYCLES = 64
FRAMES = 512
CAP = 128
HALF = CAP // 2
PIX = 4096
N_PIXEL = 16
N_TROW = 8
N_TCOL = 4
SUB = 16
OWNED = CYCLES // N_PIXEL
COLS = N_TROW * SUB
PAIRS = N_PIXEL // 2
ROWS = N_TCOL * SUB
LANES = 128
CHUNK = 512
RANK = 256
F32 = jnp.float32
BF16 = jnp.bfloat16


def dot_t(a, b):
    return lax.dot_general(a, b, (((1,), (1,)), ((), ())), preferred_element_type=F32)


def dot_n(a, b):
    return jnp.dot(a, b, preferred_element_type=F32)


def three_parts(x):
    hi = x.astype(BF16).astype(F32)
    rest = x - hi
    mid = rest.astype(BF16).astype(F32)
    return hi, mid, rest - mid


def slot_kernel(odd_ref, counts_ref, labels_ref, mask_ref, dark_ref, flat_ref, out_ref):
    odd = odd_ref[0] == 1
    live = mask_ref[...].astype(F32)
    frames = (
        flat_ref[...] * live * (counts_ref[...].astype(F32) - dark_ref[...])
    ).astype(BF16)
    labels = labels_ref[...]

    before = lax.broadcasted_iota(jnp.int32, (RANK, RANK + LANES), 0)
    at = lax.broadcasted_iota(jnp.int32, (RANK, RANK + LANES), 1)
    ahead = jnp.where((before < at) | (at >= RANK), 1.0, 0.0).astype(BF16)
    cycle_of_row = lax.broadcasted_iota(jnp.int32, (CYCLES, RANK), 0)
    offset = jnp.zeros((CYCLES, LANES), F32)
    usable = jnp.zeros((CYCLES, LANES), F32)
    ranks = []
    for c in range(PIX // RANK):
        span = slice(c * RANK, (c + 1) * RANK)
        member = jnp.where(labels[:, span] == cycle_of_row, 1.0, 0.0)
        counted = dot_n(member.astype(BF16), ahead)
        place = counted[:, :RANK] + jnp.concatenate([offset] * (RANK // LANES), axis=1)
        ranks.append(jnp.sum(member * place, axis=0, keepdims=True))
        offset = offset + counted[:, RANK:]
        usable = usable + dot_n(
            (member * live[:, span]).astype(BF16), jnp.ones((RANK, LANES), BF16)
        )
    rank = jnp.concatenate(ranks, axis=1).astype(BF16)
    label16 = labels.astype(F32).astype(BF16)

    slots = jnp.zeros((CYCLES * SUB, CAP), F32)
    slot_of_row = lax.broadcasted_iota(jnp.int32, (CAP, CHUNK), 0).astype(F32).astype(BF16)
    one = jnp.ones((CAP, CHUNK), BF16)
    none = jnp.zeros((SUB, CHUNK), BF16)
    for c in range(PIX // CHUNK):
        span = slice(c * CHUNK, (c + 1) * CHUNK)
        here = jnp.broadcast_to(label16[:, span], (SUB, CHUNK))
        chunk = frames[:, span]
        left = jnp.concatenate(
            [jnp.where(here == jnp.array(r, BF16), chunk, none) for r in range(CYCLES)], axis=0
        )
        right = jnp.where(
            jnp.broadcast_to(rank[:, span], (CAP, CHUNK)) == slot_of_row, one, jnp.zeros_like(one)
        )
        slots = slots + dot_t(left, right)

    sums = dot_n(slots.astype(BF16), jnp.ones((CAP, LANES), BF16))
    hi, mid, lo = three_parts(sums)
    lane = lax.broadcasted_iota(jnp.int32, (CYCLES * SUB, LANES), 1)
    first = jnp.where(odd, 0, HALF)
    extra = jnp.where(lane == first, hi, 0.0)
    extra = jnp.where(lane == first + 1, mid, extra)
    extra = jnp.where(lane == first + 2, lo, extra)
    extra = extra.reshape(CYCLES, SUB, LANES)
    lane = lane.reshape(CYCLES, SUB, LANES)
    extra = jnp.where(lane == first + 3, usable[:, None, :], extra)
    turned = pltpu.roll(slots, HALF, axis=1)
    in_place = jnp.where(odd, turned, slots).reshape(CYCLES, SUB, LANES)
    moved = jnp.where(odd, slots, turned).reshape(CYCLES, SUB, LANES)
    data = (lane >= HALF) == odd
    out_ref[:, 0] = jnp.where(data, in_place, extra).astype(BF16)
    out_ref[:, 1] = jnp.where(data, moved, extra).astype(BF16)


def pack_kernel(in_ref, out_ref):
    low = lax.broadcasted_iota(jnp.int32, (N_TROW, SUB, LANES), 2) < HALF
    total = jnp.zeros((COLS, LANES), F32)
    for pair in range(PAIRS):
        even = in_ref[2 * pair].astype(F32)
        odd = in_ref[2 * pair + 1].astype(F32)
        out_ref[pair * COLS : (pair + 1) * COLS] = (
            jnp.where(low, even, odd).reshape(COLS, LANES).astype(BF16)
        )
        total = total + jnp.where(low, odd, even).reshape(COLS, LANES)
    lane = lax.broadcasted_iota(jnp.int32, (COLS, LANES), 1) % HALF
    sums = jnp.sum(jnp.where(lane < 3, total, 0.0), axis=1, keepdims=True)
    usable = jnp.sum(jnp.where(lane == 3, total, 0.0), axis=1, keepdims=True)
    hi, mid, lo = three_parts(jnp.broadcast_to(sums, (COLS, LANES)).T[:SUB])
    n_hi, n_lo, _ = three_parts(jnp.broadcast_to(usable, (COLS, LANES)).T[:SUB])
    row = lax.broadcasted_iota(jnp.int32, (SUB, COLS), 0)
    tail = jnp.where(row == 0, hi, 0.0)
    tail = jnp.where(row == 1, mid, tail)
    tail = jnp.where(row == 2, lo, tail)
    tail = jnp.where(row == 3, n_hi, tail)
    tail = jnp.where(row == 4, n_lo, tail)
    out_ref[PAIRS * COLS :] = tail.astype(BF16)


def gram_kernel(me_ref, x0_ref, x1_ref, x2_ref, x3_ref, out_ref, all_ref, own_ref):
    me = me_ref[0]
    depth = PAIRS * LANES
    t_row = lax.broadcasted_iota(jnp.int32, (COLS, FRAMES), 0)
    t_col = lax.broadcasted_iota(jnp.int32, (COLS, FRAMES), 1)
    stats = jnp.zeros((SUB, FRAMES), F32)
    for d, ref in enumerate((x0_ref, x1_ref, x2_ref, x3_ref)):
        k = me ^ d
        for j in range(N_TROW):
            rows = pl.ds(pl.multiple_of(j * ROWS + k * SUB, SUB), SUB)
            for pair in range(PAIRS):
                at = pair * COLS + j * SUB
                all_ref[rows, pair * LANES : (pair + 1) * LANES] = ref[at : at + SUB]
        goes_to = (t_row // SUB) * ROWS + k * SUB + t_row % SUB
        spread = jnp.where(goes_to == t_col, 1.0, 0.0).astype(BF16)
        stats = stats + dot_n(ref[PAIRS * COLS :], spread)
    for pair in range(PAIRS):
        own_ref[:, pair * LANES : (pair + 1) * LANES] = x0_ref[pair * COLS : (pair + 1) * COLS]

    own = x0_ref[PAIRS * COLS :].astype(F32)
    own_inv = 1.0 / jnp.maximum(own[0:1] + own[1:2] + own[2:3], 1.0)
    usable = (own[3:4] + own[4:5])[:, 0:1]
    inv = 1.0 / jnp.maximum(stats[0:1] + stats[1:2] + stats[2:3], 1.0)
    inv_col = jnp.broadcast_to(inv, (LANES, FRAMES)).T

    tile = dot_t(all_ref[...], own_ref[...])
    tile = tile * (inv_col * (own_inv * usable))

    lags = jnp.zeros((1, FRAMES), F32)
    flip_row = lax.broadcasted_iota(jnp.int32, (LANES, LANES), 0)
    flip_col = lax.broadcasted_iota(jnp.int32, (LANES, LANES), 1)
    flip = jnp.where(flip_row + flip_col == LANES - 1, 1.0, 0.0).astype(BF16)
    for b in range(FRAMES // LANES):
        start = b * LANES
        width = FRAMES - start
        back = dot_n(flip, all_ref[start : start + LANES]).astype(BF16)
        back_stats = dot_n(stats[:, start : start + LANES].astype(BF16), flip)
        back_sums = back_stats[0:1] + back_stats[1:2] + back_stats[2:3]
        back_inv = jnp.broadcast_to(1.0 / jnp.maximum(back_sums, 1.0), (LANES, LANES)).T[:, 0:1]
        block = dot_t(back, all_ref[start:])
        row = lax.broadcasted_iota(jnp.int32, (LANES, width), 0)
        col = lax.broadcasted_iota(jnp.int32, (LANES, width), 1)
        block = jnp.where(row + col >= LANES - 1, block * (back_inv * inv[:, start:]), 0.0)
        block = pltpu.roll(block, width - LANES + 1, axis=1, stride=1, stride_axis=0)
        part = jnp.sum(block, axis=0, keepdims=True)
        if width < FRAMES:
            part = jnp.concatenate([part, jnp.zeros((1, start), F32)], axis=1)
        lags = lags + part
    remaining = (FRAMES - lax.broadcasted_iota(jnp.int32, (1, FRAMES), 1)).astype(F32)
    lags = lags * usable / remaining

    for i in range(N_TROW):
        out_ref[i, :ROWS] = tile[i * ROWS : (i + 1) * ROWS]
        for b in range(FRAMES // LANES):
            out_ref[i, ROWS + b : ROWS + b + 1] = lags[:, b * LANES : (b + 1) * LANES]
        out_ref[i, ROWS + 4 :] = jnp.zeros((4, LANES), F32)


def join_kernel(in_ref, tile_ref, lag_ref):
    for c in range(OWNED):
        both = in_ref[2 * c] + in_ref[2 * c + 1]
        tile_ref[c] = both[:ROWS]
        for b in range(FRAMES // LANES):
            lag_ref[c : c + 1, b * LANES : (b + 1) * LANES] = both[ROWS + b : ROWS + b + 1]


def call(body, out_shape, n_in, scalars=0, scratch=(), flops=0, size=0):
    vmem = pl.BlockSpec(memory_space=pltpu.VMEM)
    smem = pl.BlockSpec(memory_space=pltpu.SMEM)
    many = isinstance(out_shape, tuple)
    return pl.pallas_call(
        body,
        out_shape=out_shape,
        in_specs=[smem] * scalars + [vmem] * n_in,
        out_specs=(vmem,) * len(out_shape) if many else vmem,
        scratch_shapes=list(scratch),
        compiler_params=pltpu.CompilerParams(vmem_limit_bytes=32 * 1024 * 1024),
        cost_estimate=pl.CostEstimate(flops=flops, bytes_accessed=size, transcendentals=0),
    )


def per_device(counts, labels, pixel_mask, dark_level, flat_field):
    odd = (lax.axis_index("pixel") % 2).astype(jnp.int32).reshape(1)
    me = lax.axis_index("tcol").astype(jnp.int32).reshape(1)
    payload = call(
        slot_kernel,
        jax.ShapeDtypeStruct((CYCLES, 2, SUB, LANES), BF16),
        5,
        scalars=1,
        flops=2 * CYCLES * SUB * CAP * PIX,
        size=1 << 20,
    )(
        odd,
        counts,
        labels.reshape(1, PIX),
        pixel_mask.reshape(1, PIX),
        dark_level.reshape(1, PIX),
        flat_field.reshape(1, PIX),
    )
    arrived = lax.all_to_all(
        payload.reshape(2 * CYCLES, SUB, LANES), ("pixel", "trow"), 0, 0, tiled=True
    )
    packed = call(
        pack_kernel,
        jax.ShapeDtypeStruct((PAIRS * COLS + SUB, LANES), BF16),
        1,
        flops=1 << 20,
        size=3 << 18,
    )(arrived.reshape(N_PIXEL, N_TROW, SUB, LANES))
    beside = lax.ppermute(packed, "tcol", [(k, k ^ 1) for k in range(N_TCOL)])
    across = lax.ppermute(packed, "tcol", [(k, k ^ 2) for k in range(N_TCOL)])
    corner = lax.ppermute(across, "tcol", [(k, k ^ 1) for k in range(N_TCOL)])
    depth = PAIRS * LANES
    sends = call(
        gram_kernel,
        jax.ShapeDtypeStruct((N_TROW, ROWS + 8, LANES), F32),
        4,
        scalars=1,
        scratch=[pltpu.VMEM((FRAMES, depth), BF16), pltpu.VMEM((COLS, depth), BF16)],
        flops=2 * FRAMES * FRAMES * depth,
        size=3 << 19,
    )(me, packed, beside, across, corner)
    gets = lax.all_to_all(sends, "trow", 0, 0, tiled=True)
    return call(
        join_kernel,
        (
            jax.ShapeDtypeStruct((OWNED, ROWS, COLS), F32),
            jax.ShapeDtypeStruct((OWNED, FRAMES), F32),
        ),
        1,
        flops=1 << 16,
        size=1 << 19,
    )(gets)


def solution(mesh):
    placed = (P(("trow", "tcol"), "pixel"), P("pixel", None), P("pixel"), P("pixel"), P("pixel"))
    return jax.shard_map(
        per_device,
        mesh=mesh,
        in_specs=placed,
        out_specs=(P("pixel", "trow", "tcol"), P("pixel", None)),
        check_vma=False,
    )
```

time: 432 us -> 80.9 us (0.19)
  waiting for transfers between devices: 130 us -> 1.14 us
  local copies, waits for them, and re-layouts: 128 us -> 3.1 us
  blocking collectives: 138 us -> 56.5 us
  other arithmetic: 17.9 us -> 0 us
  between operations: 14 us -> 0.72 us
  starting transfers between devices: 0.12 us -> 12.8 us
  Pallas kernels: 0 us -> 6.05 us
    psum x2 -> x0, blocking collectives: 138 us -> none  [the longest x1 74.1 us: per_device(): lax.psum((gram_tile, row_sums, column_sums, cycle_sizes), 'pixel')]
    gather x3 -> x0, local copies, waits for them, and re-layouts: 120 us -> none  [the longest x1 45.5 us: per_device(): live = jnp.where(usable, pixel_mask[slot_index], 0).astype(jnp.float32)]
    all_gather x2 -> x0, waiting for transfers between devices: 73.1 us -> none  [the longest x1 44.8 us: per_device(): arrived = lax.all_gather(slotted, 'trow', axis=0, tiled=True)]
    all_to_all x0 -> x2, blocking collectives: none -> 56.5 us  [the longest x1 40.5 us: per_device(): lax.all_to_all(payload.reshape(2 * CYCLES, SUB, LANES), ('pixel', 'trow')...]
    psum x1 -> x0, waiting for transfers between devices: 55.9 us -> none  [per_device(): lax.psum((gram_tile, row_sums, column_sums, cycle_sizes), 'pixel')]
    ppermute x0 -> x3, starting transfers between devices: none -> 12.8 us  [the longest x1 4.89 us: per_device(): corner = lax.ppermute(across, 'tcol', [(k, k ^ 1) for k in range(N_TCOL)])]
    select_n x2 -> x0, other arithmetic: 7.02 us -> none  [the longest x1 6.98 us: per_device(): jnp.where(usable[None, :], jnp.take(corrected, slot_index, axis=1), jnp.z...]
    sort x1 -> x0, other arithmetic: 6.5 us -> none  [slot_table(): ordering = jnp.argsort(block_labels, stable=True)]
  transfers between devices with their start and end apart: 3 -> 3, of which waited for: 3 -> 1; matrix products, arithmetic and copies ran while one was open for 12% -> 0% of each run, Pallas kernels for 0% -> 0%
where the time goes in v1:
time: 80.9 us; the launch traced here: 80.3 us
  blocking collectives  56.5 us (70%)
  starting transfers between devices  12.8 us (16%)
  Pallas kernels  6.05 us (7%)
  local copies, waits for them, and re-layouts  3.1 us (4%)
  waiting for transfers between devices  1.14 us (1%)
    all_to_all x1, blocking collectives, per_device(): lax.all_to_all(payload.reshape(2 * CYCLES, SUB, LANES), ('pixel', 'trow')...  40.5 us
    all_to_all x1, blocking collectives, per_device(): gets = lax.all_to_all(sends, 'trow', 0, 0, tiled=True)  16 us
    ppermute x1, starting transfers between devices, per_device(): corner = lax.ppermute(across, 'tcol', [(k, k ^ 1) for k in range(N_TCOL)])  4.89 us
    ppermute x1, starting transfers between devices, per_device(): beside = lax.ppermute(packed, 'tcol', [(k, k ^ 1) for k in range(N_TCOL)])  4.8 us
    pallas_call x1, Pallas kernels, per_device(): call(slot_kernel, jax.ShapeDtypeStruct((CYCLES, 2, SUB, LANES), BF16), 5,...  3.18 us
    ppermute x1, starting transfers between devices, per_device(): across = lax.ppermute(packed, 'tcol', [(k, k ^ 2) for k in range(N_TCOL)])  3.1 us
    unnamed x10, local copies, waits for them, and re-layouts  3.1 us
    pallas_call x1, Pallas kernels, per_device(): call(gram_kernel, jax.ShapeDtypeStruct((N_TROW, ROWS + 8, LANES), F32), 4...  1.99 us
  transfers between devices with their start and end apart: 3, of which 1 were waited for; matrix products, arithmetic and copies ran while one was open for 0% of the time, Pallas kernels for 0%

profile of v1, /device:TPU:1, one launch (start us, length us, event | category | flops | bytes accessed | tf_op | source)
XLA Modules:
  0.0 80.3 jit_solution(13698019888726940831)
XLA Ops:
  0.6 0.0 copy-start.1
  0.6 0.0 copy-start.2
  0.7 0.7 copy-done.1
  1.4 0.0 copy-done.2
  1.4 0.0 copy-start
  1.4 0.9 %copy-done = s32[16,4096]{1,0:T(8,128)S(1)} copy-done((s32[16,4096]{1,0:T(8,128)S(1)}, s32[16,4096]{1,0:T(8,128)}, u32[]{:S(2)}) %copy-start) | copy-done | bytes 262168
  2.3 0.0 copy-start.3
  2.3 0.7 copy-done.3
  3.0 0.0 copy-start.4
  3.0 0.7 copy-done.4
  3.8 3.2 %shard_map.68 = bf16[64,2,16,128]{3,2,1,0:T(8,128)(2,1)S(1)} custom-call(s32[1]{0:T(128)} %bitcast.1.odd_ref, s32[16,4096]{1,0:T(8,128)S(1)} %copy-done, s32[1,4096]{1,0:T(1,128)S(1)} %bitcast.10, s32[1,4096]{1,0:T(1,128)S(1)} %bitcast.11, f32[1,4096]{1,0:T(1,128)S(1)} %bitcast.12, f32[1,4096]{1,0:T(1,128)S(1)} %bitcast.13), custom_call_target="tpu_custom_call" | custom-call | flops 1073741824 | bytes 1048576 | tf_op jit(solution)/shard_map/pallas_call | solution.py:213
  6.9 40.5 %all_to_all.10 = bf16[128,16,128]{2,1,0:T(8,128)(2,1)S(1)} all-to-all(bf16[128,16,128]{2,1,0:T(8,128)(2,1)S(1)} %bitcast.9), channel_id=1, replica_groups=mesh['pixel'=16,'trow'=8,'tcol'=4] {'pixel','trow'}, dimensions={0} | all-to-all | bytes 1048576 | tf_op jit(solution)/shard_map/all_to_all | solution.py:228
  47.5 0.2 shard_map.69.x0_ref
  47.7 3.1 %collective-permute-start.1 = (bf16[1040,128]{1,0:T(8,128)(2,1)S(1)}, bf16[1040,128]{1,0:T(8,128)(2,1)S(1)}, u32[]{:S(2)}, u32[]{:S(2)}) collective-permute-start(bf16[1040,128]{1,0:T(8,128)(2,1)S(1)} %shard_map.69.x0_ref), channel_id=1, source_target_pairs={{0,2},{1,3},{2,0},{3,1},{4,6},{5,7},{6,4},{7,5},{8,10},{9,11},{10,... | collective-permute-start | bytes 798728 | tf_op jit(solution)/shard_map/ppermute | solution.py:239
  50.8 4.8 %collective-permute-start = (bf16[1040,128]{1,0:T(8,128)(2,1)S(1)}, bf16[1040,128]{1,0:T(8,128)(2,1)S(1)}, u32[]{:S(2)}, u32[]{:S(2)}) collective-permute-start(bf16[1040,128]{1,0:T(8,128)(2,1)S(1)} %shard_map.69.x0_ref), channel_id=1, source_target_pairs={{0,1},{1,0},{2,3},{3,2},{4,5},{5,4},{6,7},{7,6},{8,9},{9,8},{10,11... | collective-permute-start | bytes 798728 | tf_op jit(solution)/shard_map/ppermute | solution.py:238
  55.6 0.0 collective-permute-done.1.x2_ref
  55.6 4.9 %collective-permute-start.2 = (bf16[1040,128]{1,0:T(8,128)(2,1)S(1)}, bf16[1040,128]{1,0:T(8,128)(2,1)S(1)}, u32[]{:S(2)}, u32[]{:S(2)}) collective-permute-start(bf16[1040,128]{1,0:T(8,128)(2,1)S(1)} %collective-permute-done.1.x2_ref), channel_id=1, source_target_pairs={{0,1},{1,0},{2,3},{3,2},{4,5},{5,4},{6,7},{7,6},{8,9},{9,8},{10,11... | collective-permute-start | bytes 798728 | tf_op jit(solution)/shard_map/ppermute | solution.py:240
  60.5 0.0 collective-permute-done.x1_ref
  60.5 1.1 %collective-permute-done.2.x3_ref = bf16[1040,128]{1,0:T(8,128)(2,1)S(1)} collective-permute-done((bf16[1040,128]{1,0:T(8,128)(2,1)S(1)}, bf16[1040,128]{1,0:T(8,128)(2,1)S(1)}, u32[]{:S(2)}, u32[]{:S(2)}) %collective-permute-start.2) | collective-permute-done | bytes 266272 | tf_op jit(solution)/shard_map/ppermute | solution.py:240
  61.7 2.0 %shard_map.70 = f32[8,72,128]{2,1,0:T(8,128)S(1)} custom-call(s32[1]{0:T(128)} %bitcast.me_ref, bf16[1040,128]{1,0:T(8,128)(2,1)S(1)} %shard_map.69.x0_ref, bf16[1040,128]{1,0:T(8,128)(2,1)S(1)} %collective-permute-done.x1_ref, bf16[1040,128]{1,0:T(8,128)(2,1)S(1)} %collective-permute-done.1.x2_ref, bf16[1040,128]{1,0:T(8,128)(2,1)S(1)} %collective-permute-done.2.x3_ref), custom_call_target="tpu_custom_call" | custom-call | flops 536870912 | bytes 1572864 | tf_op jit(solution)/shard_map/pallas_call | solution.py:242
  63.7 16.0 %all_to_all.11.in_ref = f32[8,72,128]{2,1,0:T(8,128)S(1)} all-to-all(f32[8,72,128]{2,1,0:T(8,128)S(1)} %shard_map.70), channel_id=1, replica_groups=mesh['pixel'=16,'trow'=8,'tcol'=4] {'trow'}, dimensions={0} | all-to-all | bytes 589824 | tf_op jit(solution)/shard_map/all_to_all | solution.py:251
  79.6 0.7 shard_map.71
Async XLA Ops:
  0.6 0.7 copy-start.1
  0.6 0.7 copy-start.2
  1.4 0.9 %copy-start = (s32[16,4096]{1,0:T(8,128)S(1)}, s32[16,4096]{1,0:T(8,128)}, u32[]{:S(2)}) copy-start(s32[16,4096]{1,0:T(8,128)} %counts_ref.1) | copy-start | bytes 786436
  2.3 0.7 copy-start.3
  3.0 0.7 copy-start.4
  47.7 7.9 %collective-permute-start.1 = (bf16[1040,128]{1,0:T(8,128)(2,1)S(1)}, bf16[1040,128]{1,0:T(8,128)(2,1)S(1)}, u32[]{:S(2)}, u32[]{:S(2)}) collective-permute-start(bf16[1040,128]{1,0:T(8,128)(2,1)S(1)} %shard_map.69.x0_ref), channel_id=1, source_target_pairs={{0,2},{1,3},{2,0},{3,1},{4,6},{5,7},{6,4},{7,5},{8,10},{9,11},{10,... | collective-permute-start | bytes 798728 | tf_op jit(solution)/shard_map/ppermute | solution.py:239
  50.8 9.7 %collective-permute-start = (bf16[1040,128]{1,0:T(8,128)(2,1)S(1)}, bf16[1040,128]{1,0:T(8,128)(2,1)S(1)}, u32[]{:S(2)}, u32[]{:S(2)}) collective-permute-start(bf16[1040,128]{1,0:T(8,128)(2,1)S(1)} %shard_map.69.x0_ref), channel_id=1, source_target_pairs={{0,1},{1,0},{2,3},{3,2},{4,5},{5,4},{6,7},{7,6},{8,9},{9,8},{10,11... | collective-permute-start | bytes 798728 | tf_op jit(solution)/shard_map/ppermute | solution.py:238
  55.6 6.0 %collective-permute-start.2 = (bf16[1040,128]{1,0:T(8,128)(2,1)S(1)}, bf16[1040,128]{1,0:T(8,128)(2,1)S(1)}, u32[]{:S(2)}, u32[]{:S(2)}) collective-permute-start(bf16[1040,128]{1,0:T(8,128)(2,1)S(1)} %collective-permute-done.1.x2_ref), channel_id=1, source_target_pairs={{0,1},{1,0},{2,3},{3,2},{4,5},{5,4},{6,7},{7,6},{8,9},{9,8},{10,11... | collective-permute-start | bytes 798728 | tf_op jit(solution)/shard_map/ppermute | solution.py:240

commit v2 on v1

v2 whole, which is shorter than its diff:
```python
import jax
import jax.numpy as jnp
from jax import lax
from jax.experimental import pallas as pl
from jax.experimental.pallas import tpu as pltpu
from jax.sharding import Mesh
from jax.sharding import PartitionSpec as P

CYCLES = 64
FRAMES = 512
CAP = 128
SPLIT = 4
PART = CAP // SPLIT
PIX = 4096
N_PIXEL = 16
N_TROW = 8
N_TCOL = 4
N_Z = 2
SUB = 16
OWNED = CYCLES // N_PIXEL
COLS = N_TROW * SUB
QUADS = N_PIXEL // SPLIT
SEEN = N_TROW * N_Z * SUB
ROWS = N_TCOL * SUB
LANES = 128
CHUNK = 512
RANK = 256
F32 = jnp.float32
BF16 = jnp.bfloat16


def dot_t(a, b):
    return lax.dot_general(a, b, (((1,), (1,)), ((), ())), preferred_element_type=F32)


def dot_n(a, b):
    return jnp.dot(a, b, preferred_element_type=F32)


def three_parts(x):
    hi = x.astype(BF16).astype(F32)
    rest = x - hi
    mid = rest.astype(BF16).astype(F32)
    return hi, mid, rest - mid


def slot_kernel(turn_ref, counts_ref, labels_ref, mask_ref, dark_ref, flat_ref, out_ref):
    turn = turn_ref[0]
    live = mask_ref[...].astype(F32)
    frames = (
        flat_ref[...] * live * (counts_ref[...].astype(F32) - dark_ref[...])
    ).astype(BF16)
    labels = labels_ref[...]

    before = lax.broadcasted_iota(jnp.int32, (RANK, RANK + LANES), 0)
    at = lax.broadcasted_iota(jnp.int32, (RANK, RANK + LANES), 1)
    ahead = jnp.where((before < at) | (at >= RANK), 1.0, 0.0).astype(BF16)
    cycle_of_row = lax.broadcasted_iota(jnp.int32, (CYCLES, RANK), 0)
    offset = jnp.zeros((CYCLES, LANES), F32)
    usable = jnp.zeros((CYCLES, LANES), F32)
    ranks = []
    for c in range(PIX // RANK):
        span = slice(c * RANK, (c + 1) * RANK)
        member = jnp.where(labels[:, span] == cycle_of_row, 1.0, 0.0)
        counted = dot_n(member.astype(BF16), ahead)
        place = counted[:, :RANK] + jnp.concatenate([offset] * (RANK // LANES), axis=1)
        ranks.append(jnp.sum(member * place, axis=0, keepdims=True))
        offset = offset + counted[:, RANK:]
        usable = usable + dot_n(
            (member * live[:, span]).astype(BF16), jnp.ones((RANK, LANES), BF16)
        )
    rank = jnp.concatenate(ranks, axis=1).astype(jnp.int32) + turn * PART
    rank = (rank & (CAP - 1)).astype(F32).astype(BF16)
    label16 = labels.astype(F32).astype(BF16)

    slots = jnp.zeros((CYCLES * SUB, CAP), F32)
    slot_of_row = lax.broadcasted_iota(jnp.int32, (CAP, CHUNK), 0).astype(F32).astype(BF16)
    one = jnp.ones((CAP, CHUNK), BF16)
    none = jnp.zeros((SUB, CHUNK), BF16)
    for c in range(PIX // CHUNK):
        span = slice(c * CHUNK, (c + 1) * CHUNK)
        here = jnp.broadcast_to(label16[:, span], (SUB, CHUNK))
        chunk = frames[:, span]
        left = jnp.concatenate(
            [jnp.where(here == jnp.array(r, BF16), chunk, none) for r in range(CYCLES)], axis=0
        )
        right = jnp.where(
            jnp.broadcast_to(rank[:, span], (CAP, CHUNK)) == slot_of_row, one, jnp.zeros_like(one)
        )
        slots = slots + dot_t(left, right)

    sums = dot_n(slots.astype(BF16), jnp.ones((CAP, LANES), BF16))
    hi, mid, lo = three_parts(sums)
    lane = lax.broadcasted_iota(jnp.int32, (CYCLES * SUB, LANES), 1) % PART
    extra = jnp.where(lane == 0, hi, jnp.where(lane == 1, mid, jnp.where(lane == 2, lo, 0.0)))
    extra = extra.reshape(CYCLES, SUB, LANES)
    extra = jnp.where(lane.reshape(CYCLES, SUB, LANES) == 3, usable[:, None, :], extra)
    slots = slots.reshape(CYCLES, SUB, LANES)
    early, late = slots[:, : SUB // 2], slots[:, SUB // 2 :]
    block = lax.broadcasted_iota(jnp.int32, (CYCLES, SUB // 2, LANES), 2) // PART
    block = (block - turn) & (SPLIT - 1)
    rest = jnp.where(block == 1, extra[:, : SUB // 2], extra[:, SUB // 2 :])
    for part in range(SPLIT):
        first = pltpu.roll(early, (CAP - part * PART) % CAP, axis=2)
        second = pltpu.roll(late, (CAP - part * PART + CAP // 2) % CAP, axis=2)
        tile = jnp.where(block == 0, first, jnp.where(block == 2, second, rest))
        tiles = [tile] if part % 2 == 0 else tiles + [tile]
        if part % 2 == 1:
            rows = slice((part - 1) * SUB // 2, (part + 1) * SUB // 2)
            out_ref[:, rows] = jnp.concatenate(tiles, axis=1).astype(BF16)


def pick(tiles, ahead):
    block = lax.broadcasted_iota(jnp.int32, tiles[0].shape, 2) // PART
    out = tiles[(SPLIT - 1 + ahead) % SPLIT]
    for b in range(SPLIT - 1):
        out = jnp.where(block == b, tiles[(b + ahead) % SPLIT], out)
    return out


def by_frame(early, late):
    half = SUB // 2
    pieces = [x[:, z * half : (z + 1) * half] for z in range(N_Z) for x in (early, late)]
    return jnp.concatenate(pieces, axis=1).reshape(SEEN, LANES)


def pack_kernel(in_ref, out_ref):
    total = jnp.zeros((SEEN, LANES), F32)
    for quad in range(QUADS):
        tiles = [in_ref[SPLIT * quad + s].astype(F32) for s in range(SPLIT)]
        late = pltpu.roll(pick(tiles, 2), CAP // 2, axis=2)
        out_ref[quad * SEEN : (quad + 1) * SEEN] = by_frame(pick(tiles, 0), late).astype(BF16)
        total = total + by_frame(pick(tiles, 3), pick(tiles, 1))
    lane = lax.broadcasted_iota(jnp.int32, (SEEN, LANES), 1) % PART
    sums = jnp.sum(jnp.where(lane < 3, total, 0.0), axis=1, keepdims=True)
    usable = jnp.sum(jnp.where(lane == 3, total, 0.0), axis=1, keepdims=True)
    sums = jnp.broadcast_to(sums, (SEEN, LANES)).T[: SUB // 2]
    usable = jnp.broadcast_to(usable, (SEEN, LANES)).T[: SUB // 2]
    hi, mid, lo = three_parts(sums)
    n_hi, n_lo, _ = three_parts(usable)
    row = lax.broadcasted_iota(jnp.int32, (SUB // 2, SEEN), 0)
    tail = jnp.zeros((SUB // 2, SEEN), F32)
    for i, x in enumerate((hi, mid, lo, n_hi, n_lo)):
        tail = jnp.where(row == i, x, tail)
    tail = jnp.concatenate([tail[:, :LANES], tail[:, LANES:]], axis=0)
    out_ref[QUADS * SEEN :] = tail.astype(BF16)


def gram_kernel(me_ref, x0_ref, x1_ref, out_ref, all_ref, own_ref):
    me = me_ref[0]
    t_row = lax.broadcasted_iota(jnp.int32, (LANES, FRAMES), 0)
    t_col = lax.broadcasted_iota(jnp.int32, (LANES, FRAMES), 1)
    stats = jnp.zeros((SUB // 2, FRAMES), F32)
    for d, ref in enumerate((x0_ref, x1_ref)):
        core = me ^ d
        for j in range(N_TROW):
            for z in range(N_Z):
                first = j * ROWS + z * 2 * SUB + core * SUB
                rows = pl.ds(pl.multiple_of(first, SUB), SUB)
                for quad in range(QUADS):
                    at = quad * SEEN + (j * N_Z + z) * SUB
                    here = ref[at : at + SUB]
                    all_ref[rows, quad * LANES : (quad + 1) * LANES] = here
                    if d == 0:
                        own_ref[z, j * SUB : (j + 1) * SUB, quad * LANES : (quad + 1) * LANES] = here
        tail = ref[QUADS * SEEN :]
        for part in range(SEEN // LANES):
            group = t_row // SUB + part * LANES // SUB
            goes_to = group * 2 * SUB + core * SUB + t_row % SUB
            spread = jnp.where(goes_to == t_col, 1.0, 0.0).astype(BF16)
            stats = stats + dot_n(tail, spread)[part * SUB // 2 : (part + 1) * SUB // 2]

    inv = 1.0 / jnp.maximum(stats[0:1] + stats[1:2] + stats[2:3], 1.0)
    inv_col = jnp.broadcast_to(inv, (LANES, FRAMES)).T
    usable = (stats[3:4] + stats[4:5])[:, 0:1]

    lags = jnp.zeros((1, FRAMES), F32)
    flip_row = lax.broadcasted_iota(jnp.int32, (LANES, LANES), 0)
    flip_col = lax.broadcasted_iota(jnp.int32, (LANES, LANES), 1)
    flip = jnp.where(flip_row + flip_col == LANES - 1, 1.0, 0.0).astype(BF16)
    for b in range(FRAMES // LANES):
        start = b * LANES
        width = FRAMES - start
        back = dot_n(flip, all_ref[start : start + LANES]).astype(BF16)
        back_stats = dot_n(stats[:, start : start + LANES].astype(BF16), flip)
        back_sums = back_stats[0:1] + back_stats[1:2] + back_stats[2:3]
        back_inv = jnp.broadcast_to(1.0 / jnp.maximum(back_sums, 1.0), (LANES, LANES)).T[:, 0:1]
        block = dot_t(back, all_ref[start:])
        row = lax.broadcasted_iota(jnp.int32, (LANES, width), 0)
        col = lax.broadcasted_iota(jnp.int32, (LANES, width), 1)
        block = jnp.where(row + col >= LANES - 1, block * (back_inv * inv[:, start:]), 0.0)
        block = pltpu.roll(block, width - LANES + 1, axis=1, stride=1, stride_axis=0)
        part = jnp.sum(block, axis=0, keepdims=True)
        if width < FRAMES:
            part = jnp.concatenate([part, jnp.zeros((1, start), F32)], axis=1)
        lags = lags + part
    remaining = (FRAMES - lax.broadcasted_iota(jnp.int32, (1, FRAMES), 1)).astype(F32)
    lags = lags * usable / remaining
    tail = jnp.concatenate(
        [lags[:, b * LANES : (b + 1) * LANES] for b in range(FRAMES // LANES)]
        + [jnp.zeros((4, LANES), F32)],
        axis=0,
    )

    own_sums = x0_ref[QUADS * SEEN :].astype(F32)
    for z in range(N_Z):
        pieces = []
        for j in range(N_TROW):
            at = (j * N_Z + z) * SUB
            half = at // LANES * (SUB // 2)
            pieces.append(own_sums[half : half + SUB // 2, at % LANES : at % LANES + SUB])
        own = jnp.concatenate(pieces, axis=1)
        own_inv = usable / jnp.maximum(own[0:1] + own[1:2] + own[2:3], 1.0)
        tile = dot_t(all_ref[...], own_ref[z]) * (inv_col * own_inv)
        for i in range(N_TROW):
            out_ref[i, z, :ROWS] = tile[i * ROWS : (i + 1) * ROWS]
            out_ref[i, z, ROWS:] = tail


def join_kernel(in_ref, tile_ref, lag_ref):
    for c in range(OWNED):
        parts = [in_ref[SPLIT * c + part] for part in range(SPLIT)]
        both = (parts[0] + parts[1]) + (parts[2] + parts[3])
        tile_ref[c] = both[:ROWS]
        for b in range(FRAMES // LANES):
            lag_ref[c : c + 1, b * LANES : (b + 1) * LANES] = both[ROWS + b : ROWS + b + 1]


def call(body, out_shape, n_in, scalars=0, scratch=(), flops=0, size=0):
    vmem = pl.BlockSpec(memory_space=pltpu.VMEM)
    smem = pl.BlockSpec(memory_space=pltpu.SMEM)
    many = isinstance(out_shape, tuple)
    return pl.pallas_call(
        body,
        out_shape=out_shape,
        in_specs=[smem] * scalars + [vmem] * n_in,
        out_specs=(vmem,) * len(out_shape) if many else vmem,
        scratch_shapes=list(scratch),
        compiler_params=pltpu.CompilerParams(vmem_limit_bytes=32 * 1024 * 1024),
        cost_estimate=pl.CostEstimate(flops=flops, bytes_accessed=size, transcendentals=0),
    )


def per_device(counts, labels, pixel_mask, dark_level, flat_field):
    turn = (lax.axis_index("pixel") & (SPLIT - 1)).astype(jnp.int32).reshape(1)
    me = lax.axis_index("core").astype(jnp.int32).reshape(1)
    payload = call(
        slot_kernel,
        jax.ShapeDtypeStruct((CYCLES, SPLIT * SUB // 2, LANES), BF16),
        5,
        scalars=1,
        flops=2 * CYCLES * SUB * CAP * PIX,
        size=1 << 20,
    )(
        turn,
        counts,
        labels.reshape(1, PIX),
        pixel_mask.reshape(1, PIX),
        dark_level.reshape(1, PIX),
        flat_field.reshape(1, PIX),
    )
    arrived = lax.all_to_all(
        payload.reshape(SPLIT * CYCLES, SUB // 2, LANES), ("pixel", "trow", "z"), 0, 0, tiled=True
    )
    packed = call(
        pack_kernel,
        jax.ShapeDtypeStruct((QUADS * SEEN + SUB, LANES), BF16),
        1,
        flops=1 << 20,
        size=3 << 18,
    )(arrived.reshape(N_PIXEL, N_TROW, SUB, LANES))
    beside = lax.ppermute(packed, "core", [(0, 1), (1, 0)])
    depth = QUADS * LANES
    sends = call(
        gram_kernel,
        jax.ShapeDtypeStruct((N_TROW, N_Z, ROWS + 8, LANES), F32),
        2,
        scalars=1,
        scratch=[pltpu.VMEM((FRAMES, depth), BF16), pltpu.VMEM((N_Z, COLS, depth), BF16)],
        flops=2 * FRAMES * FRAMES * depth,
        size=3 << 19,
    )(me, packed, beside)
    gets = lax.all_to_all(
        sends.reshape(N_TROW * N_Z, ROWS + 8, LANES), ("trow", "z"), 0, 0, tiled=True
    )
    return call(
        join_kernel,
        (
            jax.ShapeDtypeStruct((OWNED, ROWS, COLS), F32),
            jax.ShapeDtypeStruct((OWNED, FRAMES), F32),
        ),
        1,
        flops=1 << 16,
        size=1 << 19,
    )(gets)


def solution(mesh):
    fine = Mesh(
        mesh.devices.reshape(N_PIXEL, N_TROW, N_Z, 2), ("pixel", "trow", "z", "core")
    )
    frames = ("trow", "z", "core")
    placed = (P(frames, "pixel"), P("pixel", None), P("pixel"), P("pixel"), P("pixel"))
    return jax.shard_map(
        per_device,
        mesh=fine,
        in_specs=placed,
        out_specs=(P("pixel", "trow", ("z", "core")), P("pixel", None)),
        check_vma=False,
    )
```

time: 80.9 us -> 80.3 us (level)
  starting transfers between devices: 12.8 us -> 5.05 us
  blocking collectives: 56.5 us -> 63.5 us
    ppermute x3 -> x1, starting transfers between devices: 12.8 us -> 5.05 us  [per_device(): beside = lax.ppermute(packed, 'core', [(0, 1), (1, 0)])]
    all_to_all x2, blocking collectives: 56.5 us -> 63.5 us  [the longest x1 42.1 us: per_device(): lax.all_to_all(payload.reshape(SPLIT * CYCLES, SUB // 2, LANES), ('pixel'...]
  transfers between devices with their start and end apart: 3 -> 1, of which waited for: 1 -> 1; matrix products, arithmetic and copies ran while one was open for 0% -> 0% of each run, Pallas kernels for 0% -> 0%
where the time goes in v2:
time: 80.3 us; the launch traced here: 79.7 us
  blocking collectives  63.5 us (79%)
  Pallas kernels  5.53 us (7%)
  starting transfers between devices  5.05 us (6%)
  local copies, waits for them, and re-layouts  3.8 us (5%)
  waiting for transfers between devices  1.14 us (1%)
    all_to_all x1, blocking collectives, per_device(): lax.all_to_all(payload.reshape(SPLIT * CYCLES, SUB // 2, LANES), ('pixel'...  42.1 us
    all_to_all x1, blocking collectives, per_device(): lax.all_to_all(sends.reshape(N_TROW * N_Z, ROWS + 8, LANES), ('trow', 'z'...  21.5 us
    ppermute x1, starting transfers between devices, per_device(): beside = lax.ppermute(packed, 'core', [(0, 1), (1, 0)])  5.05 us
    unnamed x10, local copies, waits for them, and re-layouts  3.8 us
    pallas_call x1, Pallas kernels, per_device(): call(slot_kernel, jax.ShapeDtypeStruct((CYCLES, SPLIT * SUB // 2, LANES),...  3.27 us
  transfers between devices with their start and end apart: 1, of which 1 were waited for; matrix products, arithmetic and copies ran while one was open for 0% of the time, Pallas kernels for 0%

profile of v2, /device:TPU:1, one launch (start us, length us, event | category | flops | bytes accessed | tf_op | source)
XLA Modules:
  0.0 79.7 jit_solution(7019403549175046122)
XLA Ops:
  0.6 0.0 copy-start.1
  0.6 0.7 copy-done.1
  1.3 0.0 copy-start
  1.4 0.9 %copy-done = s32[16,4096]{1,0:T(8,128)S(1)} copy-done((s32[16,4096]{1,0:T(8,128)S(1)}, s32[16,4096]{1,0:T(8,128)}, u32[]{:S(2)}) %copy-start) | copy-done | bytes 262168
  2.3 0.0 copy-start.2
  2.3 0.7 copy-done.2
  3.0 0.0 copy-start.3
  3.0 0.7 copy-done.3
  3.7 0.0 copy-start.4
  3.7 0.7 copy-done.4
  4.5 3.3 %shard_map.68 = bf16[64,32,128]{2,1,0:T(8,128)(2,1)S(1)} custom-call(s32[1]{0:T(128)} %bitcast.1.turn_ref, s32[16,4096]{1,0:T(8,128)S(1)} %copy-done, s32[1,4096]{1,0:T(1,128)S(1)} %bitcast.12, s32[1,4096]{1,0:T(1,128)S(1)} %bitcast.13, f32[1,4096]{1,0:T(1,128)S(1)} %bitcast.14, f32[1,4096]{1,0:T(1,128)S(1)} %bitcast.15), custom_call_target="tpu_custom_call" | custom-call | flops 1073741824 | bytes 1048576 | tf_op jit(solution)/shard_map/pallas_call | solution.py:247
  7.7 42.1 %all_to_all.10 = bf16[256,8,128]{2,1,0:T(8,128)(2,1)S(1)} all-to-all(bf16[256,8,128]{2,1,0:T(8,128)(2,1)S(1)} %bitcast.11), channel_id=1, replica_groups=mesh['pixel'=16,'trow'=8,'z'=2,'core'=2] {'pixel','trow','z'}, dimensions={0} | all-to-all | bytes 1048576 | tf_op jit(solution)/shard_map/all_to_all | solution.py:262
  49.8 0.3 shard_map.69.x0_ref
  50.1 5.0 %collective-permute-start = (bf16[1040,128]{1,0:T(8,128)(2,1)S(1)}, bf16[1040,128]{1,0:T(8,128)(2,1)S(1)}, u32[]{:S(2)}, u32[]{:S(2)}) collective-permute-start(bf16[1040,128]{1,0:T(8,128)(2,1)S(1)} %shard_map.69.x0_ref), channel_id=1, source_target_pairs={{0,1},{1,0},{2,3},{3,2},{4,5},{5,4},{6,7},{7,6},{8,9},{9,8},{10,11... | collective-permute-start | bytes 798728 | tf_op jit(solution)/shard_map/ppermute | solution.py:272
  55.2 1.1 %collective-permute-done.x1_ref = bf16[1040,128]{1,0:T(8,128)(2,1)S(1)} collective-permute-done((bf16[1040,128]{1,0:T(8,128)(2,1)S(1)}, bf16[1040,128]{1,0:T(8,128)(2,1)S(1)}, u32[]{:S(2)}, u32[]{:S(2)}) %collective-permute-start) | collective-permute-done | bytes 266272 | tf_op jit(solution)/shard_map/ppermute | solution.py:272
  56.3 1.3 %shard_map.70 = f32[8,2,72,128]{3,2,1,0:T(8,128)S(1)} custom-call(s32[1]{0:T(128)} %bitcast.me_ref, bf16[1040,128]{1,0:T(8,128)(2,1)S(1)} %shard_map.69.x0_ref, bf16[1040,128]{1,0:T(8,128)(2,1)S(1)} %collective-permute-done.x1_ref), custom_call_target="tpu_custom_call" | custom-call | flops 268435456 | bytes 1572864 | tf_op jit(solution)/shard_map/pallas_call | solution.py:274
  57.6 21.5 %all_to_all.11.in_ref = f32[16,72,128]{2,1,0:T(8,128)S(1)} all-to-all(f32[16,72,128]{2,1,0:T(8,128)S(1)} %bitcast.9), channel_id=1, replica_groups=mesh['pixel'=16,'trow'=8,'z'=2,'core'=2] {'trow','z'}, dimensions={0} | all-to-all | bytes 1179648 | tf_op jit(solution)/shard_map/all_to_all | solution.py:283
  79.0 0.7 shard_map.71
Async XLA Ops:
  0.6 0.7 copy-start.1
  1.3 0.9 %copy-start = (s32[16,4096]{1,0:T(8,128)S(1)}, s32[16,4096]{1,0:T(8,128)}, u32[]{:S(2)}) copy-start(s32[16,4096]{1,0:T(8,128)} %counts_ref.1) | copy-start | bytes 786436
  2.3 0.7 copy-start.2
  3.0 0.7 copy-start.3
  3.7 0.7 copy-start.4
  50.1 6.2 %collective-permute-start = (bf16[1040,128]{1,0:T(8,128)(2,1)S(1)}, bf16[1040,128]{1,0:T(8,128)(2,1)S(1)}, u32[]{:S(2)}, u32[]{:S(2)}) collective-permute-start(bf16[1040,128]{1,0:T(8,128)(2,1)S(1)} %shard_map.69.x0_ref), channel_id=1, source_target_pairs={{0,1},{1,0},{2,3},{3,2},{4,5},{5,4},{6,7},{7,6},{8,9},{9,8},{10,11... | collective-permute-start | bytes 798728 | tf_op jit(solution)/shard_map/ppermute | solution.py:272

commit v3 on v2

--- a/solution.py
+++ b/solution.py
@@ -44,13 +44,37 @@
     return hi, mid, rest - mid
 
 
-def slot_kernel(turn_ref, counts_ref, labels_ref, mask_ref, dark_ref, flat_ref, out_ref):
+def slot_kernel(
+    turn_ref,
+    labels_hbm,
+    mask_hbm,
+    dark_hbm,
+    flat_hbm,
+    counts_hbm,
+    out_ref,
+    labels_ref,
+    mask_ref,
+    dark_ref,
+    flat_ref,
+    counts_ref,
+    labels_sem,
+    mask_sem,
+    dark_sem,
+    flat_sem,
+    counts_sem,
+):
+    get_labels = pltpu.make_async_copy(labels_hbm, labels_ref, labels_sem)
+    get_mask = pltpu.make_async_copy(mask_hbm, mask_ref, mask_sem)
+    get_dark = pltpu.make_async_copy(dark_hbm, dark_ref, dark_sem)
+    get_flat = pltpu.make_async_copy(flat_hbm, flat_ref, flat_sem)
+    get_counts = pltpu.make_async_copy(counts_hbm, counts_ref, counts_sem)
+    for get in (get_labels, get_mask, get_dark, get_flat, get_counts):
+        get.start()
     turn = turn_ref[0]
+    get_labels.wait()
+    get_mask.wait()
+    labels = labels_ref[...]
     live = mask_ref[...].astype(F32)
-    frames = (
-        flat_ref[...] * live * (counts_ref[...].astype(F32) - dark_ref[...])
-    ).astype(BF16)
-    labels = labels_ref[...]
 
     before = lax.broadcasted_iota(jnp.int32, (RANK, RANK + LANES), 0)
     at = lax.broadcasted_iota(jnp.int32, (RANK, RANK + LANES), 1)
@@ -72,6 +96,12 @@
     rank = jnp.concatenate(ranks, axis=1).astype(jnp.int32) + turn * PART
     rank = (rank & (CAP - 1)).astype(F32).astype(BF16)
     label16 = labels.astype(F32).astype(BF16)
+    get_dark.wait()
+    get_flat.wait()
+    get_counts.wait()
+    frames = (
+        flat_ref[...] * live * (counts_ref[...].astype(F32) - dark_ref[...])
+    ).astype(BF16)
 
     slots = jnp.zeros((CYCLES * SUB, CAP), F32)
     slot_of_row = lax.broadcasted_iota(jnp.int32, (CAP, CHUNK), 0).astype(F32).astype(BF16)
@@ -226,17 +256,18 @@
             lag_ref[c : c + 1, b * LANES : (b + 1) * LANES] = both[ROWS + b : ROWS + b + 1]
 
 
-def call(body, out_shape, n_in, scalars=0, scratch=(), flops=0, size=0):
+def call(body, out_shape, n_in, scalars=0, scratch=(), flops=0, size=0, source=pltpu.VMEM, limit=32 << 20):
     vmem = pl.BlockSpec(memory_space=pltpu.VMEM)
+    given = pl.BlockSpec(memory_space=source)
     smem = pl.BlockSpec(memory_space=pltpu.SMEM)
     many = isinstance(out_shape, tuple)
     return pl.pallas_call(
         body,
         out_shape=out_shape,
-        in_specs=[smem] * scalars + [vmem] * n_in,
+        in_specs=[smem] * scalars + [given] * n_in,
         out_specs=(vmem,) * len(out_shape) if many else vmem,
         scratch_shapes=list(scratch),
-        compiler_params=pltpu.CompilerParams(vmem_limit_bytes=32 * 1024 * 1024),
+        compiler_params=pltpu.CompilerParams(vmem_limit_bytes=limit),
         cost_estimate=pl.CostEstimate(flops=flops, bytes_accessed=size, transcendentals=0),
     )
 
@@ -249,15 +280,25 @@
         jax.ShapeDtypeStruct((CYCLES, SPLIT * SUB // 2, LANES), BF16),
         5,
         scalars=1,
+        scratch=[
+            pltpu.VMEM((1, PIX), jnp.int32),
+            pltpu.VMEM((1, PIX), jnp.int32),
+            pltpu.VMEM((1, PIX), F32),
+            pltpu.VMEM((1, PIX), F32),
+            pltpu.VMEM((SUB, PIX), jnp.int32),
+        ]
+        + [pltpu.SemaphoreType.DMA] * 5,
         flops=2 * CYCLES * SUB * CAP * PIX,
         size=1 << 20,
+        source=pltpu.HBM,
+        limit=63 << 20,
     )(
         turn,
-        counts,
         labels.reshape(1, PIX),
         pixel_mask.reshape(1, PIX),
         dark_level.reshape(1, PIX),
         flat_field.reshape(1, PIX),
+        counts,
     )
     arrived = lax.all_to_all(
         payload.reshape(SPLIT * CYCLES, SUB // 2, LANES), ("pixel", "trow", "z"), 0, 0, tiled=True

time: 80.3 us -> 78.2 us (0.974)
  local copies, waits for them, and re-layouts: 3.8 us -> 0 us
  Pallas kernels: 5.53 us -> 7.26 us
    unnamed x10 -> x0, local copies, waits for them, and re-layouts: 3.8 us -> none
    pallas_call x1, Pallas kernels: 3.27 us -> 5 us  [per_device(): call(slot_kernel, jax.ShapeDtypeStruct((CYCLES, SPLIT * SUB // 2, LANES),...]
where the time goes in v3:
time: 78.2 us; the launch traced here: 77.9 us
  blocking collectives  63.7 us (81%)
  Pallas kernels  7.26 us (9%)
  starting transfers between devices  5.05 us (6%)
  waiting for transfers between devices  1.14 us (1%)
    all_to_all x1, blocking collectives, per_device(): lax.all_to_all(payload.reshape(SPLIT * CYCLES, SUB // 2, LANES), ('pixel'...  42.3 us
    all_to_all x1, blocking collectives, per_device(): lax.all_to_all(sends.reshape(N_TROW * N_Z, ROWS + 8, LANES), ('trow', 'z'...  21.5 us
    ppermute x1, starting transfers between devices, per_device(): beside = lax.ppermute(packed, 'core', [(0, 1), (1, 0)])  5.05 us
    pallas_call x1, Pallas kernels, per_device(): call(slot_kernel, jax.ShapeDtypeStruct((CYCLES, SPLIT * SUB // 2, LANES),...  5 us
  transfers between devices with their start and end apart: 1, of which 1 were waited for; matrix products, arithmetic and copies ran while one was open for 0% of the time, Pallas kernels for 0%

profile of v3, /device:TPU:1, one launch (start us, length us, event | category | flops | bytes accessed | tf_op | source)
XLA Modules:
  0.0 77.9 jit_solution(13834481887070598347)
XLA Ops:
  0.6 5.0 %shard_map.68 = bf16[64,32,128]{2,1,0:T(8,128)(2,1)} custom-call(s32[1]{0:T(128)} %bitcast.1.turn_ref, s32[1,4096]{1,0:T(1,128)} %bitcast.12, s32[1,4096]{1,0:T(1,128)} %bitcast.13, f32[1,4096]{1,0:T(1,128)} %bitcast.14, f32[1,4096]{1,0:T(1,128)} %bitcast.15, s32[16,4096]{1,0:T(8,128)} %counts_hbm.1), custom_call_target="tpu_custom_call" | custom-call | flops 1073741824 | bytes 1048576 | tf_op jit(solution)/shard_map/pallas_call | solution.py:278
  5.6 42.3 %all_to_all.10 = bf16[256,8,128]{2,1,0:T(8,128)(2,1)S(1)} all-to-all(bf16[256,8,128]{2,1,0:T(8,128)(2,1)} %bitcast.11), channel_id=1, replica_groups=mesh['pixel'=16,'trow'=8,'z'=2,'core'=2] {'pixel','trow','z'}, dimensions={0} | all-to-all | bytes 1048576 | tf_op jit(solution)/shard_map/all_to_all | solution.py:303
  47.9 0.3 shard_map.69.x0_ref
  48.2 5.1 %collective-permute-start = (bf16[1040,128]{1,0:T(8,128)(2,1)S(1)}, bf16[1040,128]{1,0:T(8,128)(2,1)S(1)}, u32[]{:S(2)}, u32[]{:S(2)}) collective-permute-start(bf16[1040,128]{1,0:T(8,128)(2,1)S(1)} %shard_map.69.x0_ref), channel_id=1, source_target_pairs={{0,1},{1,0},{2,3},{3,2},{4,5},{5,4},{6,7},{7,6},{8,9},{9,8},{10,11... | collective-permute-start | bytes 798728 | tf_op jit(solution)/shard_map/ppermute | solution.py:313
  53.3 1.1 %collective-permute-done.x1_ref = bf16[1040,128]{1,0:T(8,128)(2,1)S(1)} collective-permute-done((bf16[1040,128]{1,0:T(8,128)(2,1)S(1)}, bf16[1040,128]{1,0:T(8,128)(2,1)S(1)}, u32[]{:S(2)}, u32[]{:S(2)}) %collective-permute-start) | collective-permute-done | bytes 266272 | tf_op jit(solution)/shard_map/ppermute | solution.py:313
  54.5 1.3 %shard_map.70 = f32[8,2,72,128]{3,2,1,0:T(8,128)S(1)} custom-call(s32[1]{0:T(128)} %bitcast.me_ref, bf16[1040,128]{1,0:T(8,128)(2,1)S(1)} %shard_map.69.x0_ref, bf16[1040,128]{1,0:T(8,128)(2,1)S(1)} %collective-permute-done.x1_ref), custom_call_target="tpu_custom_call" | custom-call | flops 268435456 | bytes 1572864 | tf_op jit(solution)/shard_map/pallas_call | solution.py:315
  55.7 21.5 %all_to_all.11.in_ref = f32[16,72,128]{2,1,0:T(8,128)S(1)} all-to-all(f32[16,72,128]{2,1,0:T(8,128)S(1)} %bitcast.9), channel_id=1, replica_groups=mesh['pixel'=16,'trow'=8,'z'=2,'core'=2] {'trow','z'}, dimensions={0} | all-to-all | bytes 1179648 | tf_op jit(solution)/shard_map/all_to_all | solution.py:324
  77.2 0.7 shard_map.71
Async XLA Ops:
  48.2 6.2 %collective-permute-start = (bf16[1040,128]{1,0:T(8,128)(2,1)S(1)}, bf16[1040,128]{1,0:T(8,128)(2,1)S(1)}, u32[]{:S(2)}, u32[]{:S(2)}) collective-permute-start(bf16[1040,128]{1,0:T(8,128)(2,1)S(1)} %shard_map.69.x0_ref), channel_id=1, source_target_pairs={{0,1},{1,0},{2,3},{3,2},{4,5},{5,4},{6,7},{7,6},{8,9},{9,8},{10,11... | collective-permute-start | bytes 798728 | tf_op jit(solution)/shard_map/ppermute | solution.py:313

commit v4 on v1

--- a/solution.py
+++ b/solution.py
@@ -19,6 +19,7 @@
 PAIRS = N_PIXEL // 2
 ROWS = N_TCOL * SUB
 LANES = 128
+MESSAGE = 10
 CHUNK = 512
 RANK = 256
 F32 = jnp.float32
@@ -40,20 +41,43 @@
     return hi, mid, rest - mid
 
 
-def slot_kernel(odd_ref, counts_ref, labels_ref, mask_ref, dark_ref, flat_ref, out_ref):
-    odd = odd_ref[0] == 1
+def slot_kernel(
+    turn_ref,
+    labels_hbm,
+    mask_hbm,
+    dark_hbm,
+    flat_hbm,
+    counts_hbm,
+    out_ref,
+    labels_ref,
+    mask_ref,
+    dark_ref,
+    flat_ref,
+    counts_ref,
+    labels_sem,
+    mask_sem,
+    dark_sem,
+    flat_sem,
+    counts_sem,
+):
+    get_labels = pltpu.make_async_copy(labels_hbm, labels_ref, labels_sem)
+    get_mask = pltpu.make_async_copy(mask_hbm, mask_ref, mask_sem)
+    get_dark = pltpu.make_async_copy(dark_hbm, dark_ref, dark_sem)
+    get_flat = pltpu.make_async_copy(flat_hbm, flat_ref, flat_sem)
+    get_counts = pltpu.make_async_copy(counts_hbm, counts_ref, counts_sem)
+    for get in (get_labels, get_mask, get_dark, get_flat, get_counts):
+        get.start()
+    turn = turn_ref[0]
+    get_labels.wait()
+    get_mask.wait()
+    labels = labels_ref[...]
     live = mask_ref[...].astype(F32)
-    frames = (
-        flat_ref[...] * live * (counts_ref[...].astype(F32) - dark_ref[...])
-    ).astype(BF16)
-    labels = labels_ref[...]
 
     before = lax.broadcasted_iota(jnp.int32, (RANK, RANK + LANES), 0)
     at = lax.broadcasted_iota(jnp.int32, (RANK, RANK + LANES), 1)
     ahead = jnp.where((before < at) | (at >= RANK), 1.0, 0.0).astype(BF16)
     cycle_of_row = lax.broadcasted_iota(jnp.int32, (CYCLES, RANK), 0)
     offset = jnp.zeros((CYCLES, LANES), F32)
-    usable = jnp.zeros((CYCLES, LANES), F32)
     ranks = []
     for c in range(PIX // RANK):
         span = slice(c * RANK, (c + 1) * RANK)
@@ -62,68 +86,123 @@
         place = counted[:, :RANK] + jnp.concatenate([offset] * (RANK // LANES), axis=1)
         ranks.append(jnp.sum(member * place, axis=0, keepdims=True))
         offset = offset + counted[:, RANK:]
-        usable = usable + dot_n(
-            (member * live[:, span]).astype(BF16), jnp.ones((RANK, LANES), BF16)
-        )
-    rank = jnp.concatenate(ranks, axis=1).astype(BF16)
+    rank = jnp.concatenate(ranks, axis=1).astype(jnp.int32)
+    slot = ((rank + turn * HALF) & (CAP - 1)) + (labels & 1) * CAP
+    slot16 = slot.astype(F32).astype(BF16)
     label16 = labels.astype(F32).astype(BF16)
-
-    slots = jnp.zeros((CYCLES * SUB, CAP), F32)
-    slot_of_row = lax.broadcasted_iota(jnp.int32, (CAP, CHUNK), 0).astype(F32).astype(BF16)
-    one = jnp.ones((CAP, CHUNK), BF16)
+    pair16 = (labels >> 1).astype(F32).astype(BF16)
+
+    get_dark.wait()
+    get_flat.wait()
+    get_counts.wait()
+    frames = (
+        flat_ref[...] * live * (counts_ref[...].astype(F32) - dark_ref[...])
+    ).astype(BF16)
+    live16 = jnp.broadcast_to(live, (SUB, PIX)).astype(BF16)
+
+    slots = jnp.zeros((CYCLES // 2 * SUB, 2 * CAP), F32)
+    sums = jnp.zeros((CYCLES, LANES), F32)
+    slot_of_row = lax.broadcasted_iota(jnp.int32, (2 * CAP, CHUNK), 0).astype(F32).astype(BF16)
+    row = lax.broadcasted_iota(jnp.int32, (CYCLES, CHUNK), 0)
+    even_first = ((row & (CYCLES // 2 - 1)) * 2 + row // (CYCLES // 2)).astype(F32).astype(BF16)
+    one = jnp.ones((2 * CAP, CHUNK), BF16)
     none = jnp.zeros((SUB, CHUNK), BF16)
     for c in range(PIX // CHUNK):
         span = slice(c * CHUNK, (c + 1) * CHUNK)
-        here = jnp.broadcast_to(label16[:, span], (SUB, CHUNK))
+        here = jnp.broadcast_to(pair16[:, span], (SUB, CHUNK))
         chunk = frames[:, span]
         left = jnp.concatenate(
-            [jnp.where(here == jnp.array(r, BF16), chunk, none) for r in range(CYCLES)], axis=0
+            [jnp.where(here == jnp.array(r, BF16), chunk, none) for r in range(CYCLES // 2)],
+            axis=0,
         )
         right = jnp.where(
-            jnp.broadcast_to(rank[:, span], (CAP, CHUNK)) == slot_of_row, one, jnp.zeros_like(one)
+            jnp.broadcast_to(slot16[:, span], (2 * CAP, CHUNK)) == slot_of_row,
+            one,
+            jnp.zeros_like(one),
         )
         slots = slots + dot_t(left, right)
-
-    sums = dot_n(slots.astype(BF16), jnp.ones((CAP, LANES), BF16))
+        member = jnp.where(
+            jnp.broadcast_to(label16[:, span], (CYCLES, CHUNK)) == even_first,
+            one[:CYCLES],
+            jnp.zeros_like(one[:CYCLES]),
+        )
+        stack = jnp.concatenate([chunk, chunk, chunk, live16[:, span]] * 2, axis=0)
+        sums = sums + dot_t(member, stack)
+
     hi, mid, lo = three_parts(sums)
-    lane = lax.broadcasted_iota(jnp.int32, (CYCLES * SUB, LANES), 1)
-    first = jnp.where(odd, 0, HALF)
-    extra = jnp.where(lane == first, hi, 0.0)
-    extra = jnp.where(lane == first + 1, mid, extra)
-    extra = jnp.where(lane == first + 2, lo, extra)
-    extra = extra.reshape(CYCLES, SUB, LANES)
-    lane = lane.reshape(CYCLES, SUB, LANES)
-    extra = jnp.where(lane == first + 3, usable[:, None, :], extra)
-    turned = pltpu.roll(slots, HALF, axis=1)
-    in_place = jnp.where(odd, turned, slots).reshape(CYCLES, SUB, LANES)
-    moved = jnp.where(odd, slots, turned).reshape(CYCLES, SUB, LANES)
-    data = (lane >= HALF) == odd
-    out_ref[:, 0] = jnp.where(data, in_place, extra).astype(BF16)
-    out_ref[:, 1] = jnp.where(data, moved, extra).astype(BF16)
+    part = lax.broadcasted_iota(jnp.int32, (CYCLES, LANES), 1) // SUB
+    extra = jnp.where(part == 0, hi, jnp.where(part == 1, mid, jnp.where(part == 2, lo, sums)))
+    shape = (CYCLES // 2, SUB // 2, LANES)
+    extras = [
+        jnp.broadcast_to(extra[b * shape[0] : (b + 1) * shape[0]][:, None, :], shape)
+        for b in range(2)
+    ]
+    data = (lax.broadcasted_iota(jnp.int32, shape, 2) >= HALF) == (turn == 1)
+    row = lax.broadcasted_iota(jnp.int32, shape, 1)
+    slots = slots.reshape(CYCLES // 2, SUB, 2 * CAP)
+    tiles = []
+    for b in range(2):
+        early = slots[:, : SUB // 2, b * CAP : (b + 1) * CAP]
+        late = slots[:, SUB // 2 :, b * CAP : (b + 1) * CAP]
+        tiles.append(jnp.where(data, early, pltpu.roll(late, HALF, axis=2)))
+        tiles.append(jnp.where(data, pltpu.roll(early, HALF, axis=2), late))
+    second, third, fourth = (pltpu.roll(tiles[m], 2 * m, axis=1) for m in (1, 2, 3))
+    groups = [
+        tiles[0],
+        jnp.where(row < 2, extras[0], second),
+        jnp.where(row < 2, second, jnp.where(row < 4, extras[0], third)),
+        jnp.where(row < 4, third, jnp.where(row < 6, extras[1], fourth)),
+        jnp.where(row < 6, fourth, extras[1]),
+    ]
+    out_ref[...] = (
+        jnp.concatenate(groups, axis=1).reshape(2 * CYCLES * MESSAGE, LANES).astype(BF16)
+    )
 
 
 def pack_kernel(in_ref, out_ref):
-    low = lax.broadcasted_iota(jnp.int32, (N_TROW, SUB, LANES), 2) < HALF
-    total = jnp.zeros((COLS, LANES), F32)
+    per_shard = N_TROW * MESSAGE
+    shape = (N_TROW, SUB // 2, LANES)
+    low = lax.broadcasted_iota(jnp.int32, shape, 2) < HALF
+    row = lax.broadcasted_iota(jnp.int32, (SUB // 2, LANES), 0)
+    lane = lax.broadcasted_iota(jnp.int32, (SUB // 2, LANES), 1)
+    total = jnp.zeros((per_shard, LANES), F32)
     for pair in range(PAIRS):
-        even = in_ref[2 * pair].astype(F32)
-        odd = in_ref[2 * pair + 1].astype(F32)
+        halves = []
+        for shard in (2 * pair, 2 * pair + 1):
+            rows = in_ref[shard * per_shard : (shard + 1) * per_shard].astype(F32)
+            total = total + rows
+            group = [rows[8 * i : 8 * i + 8] for i in range(per_shard // 8)]
+            tiles = []
+            for first in (0, 5):
+                g = group[first : first + 5]
+                tiles.append(g[0])
+                tiles.append(pltpu.roll(jnp.where(row < 2, g[2], g[1]), 6, axis=0))
+                tiles.append(pltpu.roll(jnp.where(row < 4, g[3], g[2]), 4, axis=0))
+                tiles.append(pltpu.roll(jnp.where(row < 6, g[4], g[3]), 2, axis=0))
+            halves.append(jnp.concatenate(tiles, axis=0).reshape(shape))
+        even, odd = halves
+        early = jnp.where(low, even, odd)
+        late = pltpu.roll(jnp.where(low, odd, even), HALF, axis=2)
         out_ref[pair * COLS : (pair + 1) * COLS] = (
-            jnp.where(low, even, odd).reshape(COLS, LANES).astype(BF16)
+            jnp.concatenate([early, late], axis=1).reshape(COLS, LANES).astype(BF16)
         )
-        total = total + jnp.where(low, odd, even).reshape(COLS, LANES)
-    lane = lax.broadcasted_iota(jnp.int32, (COLS, LANES), 1) % HALF
-    sums = jnp.sum(jnp.where(lane < 3, total, 0.0), axis=1, keepdims=True)
-    usable = jnp.sum(jnp.where(lane == 3, total, 0.0), axis=1, keepdims=True)
-    hi, mid, lo = three_parts(jnp.broadcast_to(sums, (COLS, LANES)).T[:SUB])
-    n_hi, n_lo, _ = three_parts(jnp.broadcast_to(usable, (COLS, LANES)).T[:SUB])
-    row = lax.broadcasted_iota(jnp.int32, (SUB, COLS), 0)
-    tail = jnp.where(row == 0, hi, 0.0)
-    tail = jnp.where(row == 1, mid, tail)
-    tail = jnp.where(row == 2, lo, tail)
-    tail = jnp.where(row == 3, n_hi, tail)
-    tail = jnp.where(row == 4, n_lo, tail)
-    out_ref[PAIRS * COLS :] = tail.astype(BF16)
+    sums = jnp.zeros((SUB // 2, LANES), F32)
+    usable = jnp.zeros((SUB // 2, LANES), F32)
+    for j in range(N_TROW):
+        at = j * MESSAGE + SUB // 2
+        extra = jnp.broadcast_to(total[at : at + 1], (SUB // 2, LANES))
+        added = extra + pltpu.roll(extra, LANES - SUB, axis=1)
+        added = added + pltpu.roll(extra, LANES - 2 * SUB, axis=1)
+        here = lane // SUB == j
+        sums = jnp.where(here, pltpu.roll(added, j * SUB, axis=1), sums)
+        count = pltpu.roll(extra, (LANES - 3 * SUB + j * SUB) % LANES, axis=1)
+        usable = jnp.where(here, count, usable)
+    hi, mid, lo = three_parts(sums)
+    n_hi, n_lo, _ = three_parts(usable)
+    tail = jnp.zeros((SUB // 2, LANES), F32)
+    for i, x in enumerate((hi, mid, lo, n_hi, n_lo)):
+        tail = jnp.where(row == i, x, tail)
+    out_ref[PAIRS * COLS :] = jnp.concatenate([tail, jnp.zeros_like(tail)], axis=0).astype(BF16)
 
 
 def gram_kernel(me_ref, x0_ref, x1_ref, x2_ref, x3_ref, out_ref, all_ref, own_ref):
@@ -192,41 +271,52 @@
             lag_ref[c : c + 1, b * LANES : (b + 1) * LANES] = both[ROWS + b : ROWS + b + 1]
 
 
-def call(body, out_shape, n_in, scalars=0, scratch=(), flops=0, size=0):
+def call(body, out_shape, n_in, scalars=0, scratch=(), flops=0, size=0, source=pltpu.VMEM, limit=32 << 20):
     vmem = pl.BlockSpec(memory_space=pltpu.VMEM)
+    given = pl.BlockSpec(memory_space=source)
     smem = pl.BlockSpec(memory_space=pltpu.SMEM)
     many = isinstance(out_shape, tuple)
     return pl.pallas_call(
         body,
         out_shape=out_shape,
-        in_specs=[smem] * scalars + [vmem] * n_in,
+        in_specs=[smem] * scalars + [given] * n_in,
         out_specs=(vmem,) * len(out_shape) if many else vmem,
         scratch_shapes=list(scratch),
-        compiler_params=pltpu.CompilerParams(vmem_limit_bytes=32 * 1024 * 1024),
+        compiler_params=pltpu.CompilerParams(vmem_limit_bytes=limit),
         cost_estimate=pl.CostEstimate(flops=flops, bytes_accessed=size, transcendentals=0),
     )
 
 
 def per_device(counts, labels, pixel_mask, dark_level, flat_field):
-    odd = (lax.axis_index("pixel") % 2).astype(jnp.int32).reshape(1)
+    turn = (lax.axis_index("pixel") & 1).astype(jnp.int32).reshape(1)
     me = lax.axis_index("tcol").astype(jnp.int32).reshape(1)
     payload = call(
         slot_kernel,
-        jax.ShapeDtypeStruct((CYCLES, 2, SUB, LANES), BF16),
+        jax.ShapeDtypeStruct((2 * CYCLES * MESSAGE, LANES), BF16),
         5,
         scalars=1,
+        scratch=[
+            pltpu.VMEM((1, PIX), jnp.int32),
+            pltpu.VMEM((1, PIX), jnp.int32),
+            pltpu.VMEM((1, PIX), F32),
+            pltpu.VMEM((1, PIX), F32),
+            pltpu.VMEM((SUB, PIX), jnp.int32),
+        ]
+        + [pltpu.SemaphoreType.DMA] * 5,
         flops=2 * CYCLES * SUB * CAP * PIX,
         size=1 << 20,
+        source=pltpu.HBM,
+        limit=63 << 20,
     )(
-        odd,
-        counts,
+        turn,
         labels.reshape(1, PIX),
         pixel_mask.reshape(1, PIX),
         dark_level.reshape(1, PIX),
         flat_field.reshape(1, PIX),
+        counts,
     )
     arrived = lax.all_to_all(
-        payload.reshape(2 * CYCLES, SUB, LANES), ("pixel", "trow"), 0, 0, tiled=True
+        payload.reshape(2 * CYCLES, MESSAGE // 2, 2, LANES), ("pixel", "trow"), 0, 0, tiled=True
     )
     packed = call(
         pack_kernel,
@@ -234,7 +324,7 @@
         1,
         flops=1 << 20,
         size=3 << 18,
-    )(arrived.reshape(N_PIXEL, N_TROW, SUB, LANES))
+    )(arrived.reshape(2 * CYCLES * MESSAGE, LANES))
     beside = lax.ppermute(packed, "tcol", [(k, k ^ 1) for k in range(N_TCOL)])
     across = lax.ppermute(packed, "tcol", [(k, k ^ 2) for k in range(N_TCOL)])
     corner = lax.ppermute(across, "tcol", [(k, k ^ 1) for k in range(N_TCOL)])

time: 80.9 us -> 74.2 us (0.917)
  blocking collectives: 56.5 us -> 52.7 us
  local copies, waits for them, and re-layouts: 3.1 us -> 0 us
    all_to_all x1, blocking collectives: 40.5 us -> 36.9 us  [per_device(): lax.all_to_all(payload.reshape(2 * CYCLES, MESSAGE // 2, 2, LANES), ('pix...]
    unnamed x10 -> x0, local copies, waits for them, and re-layouts: 3.1 us -> none
where the time goes in v4:
time: 74.2 us; the launch traced here: 73.9 us
  blocking collectives  52.7 us (71%)
  starting transfers between devices  12.6 us (17%)
  Pallas kernels  6.72 us (9%)
  waiting for transfers between devices  1.14 us (2%)
    all_to_all x1, blocking collectives, per_device(): lax.all_to_all(payload.reshape(2 * CYCLES, MESSAGE // 2, 2, LANES), ('pix...  36.9 us
    all_to_all x1, blocking collectives, per_device(): gets = lax.all_to_all(sends, 'trow', 0, 0, tiled=True)  15.9 us
    ppermute x1, starting transfers between devices, per_device(): corner = lax.ppermute(across, 'tcol', [(k, k ^ 1) for k in range(N_TCOL)])  4.9 us
    ppermute x1, starting transfers between devices, per_device(): beside = lax.ppermute(packed, 'tcol', [(k, k ^ 1) for k in range(N_TCOL)])  4.66 us
    pallas_call x1, Pallas kernels, per_device(): call(slot_kernel, jax.ShapeDtypeStruct((2 * CYCLES * MESSAGE, LANES), BF1...  3.86 us
    ppermute x1, starting transfers between devices, per_device(): across = lax.ppermute(packed, 'tcol', [(k, k ^ 2) for k in range(N_TCOL)])  3.07 us
    pallas_call x1, Pallas kernels, per_device(): call(gram_kernel, jax.ShapeDtypeStruct((N_TROW, ROWS + 8, LANES), F32), 4...  1.99 us
  transfers between devices with their start and end apart: 3, of which 1 were waited for; matrix products, arithmetic and copies ran while one was open for 0% of the time, Pallas kernels for 0%

profile of v4, /device:TPU:1, one launch (start us, length us, event | category | flops | bytes accessed | tf_op | source)
XLA Modules:
  0.0 73.9 jit_solution(837842560406257301)
XLA Ops:
  0.6 3.9 %shard_map.68 = bf16[1280,128]{1,0:T(8,128)(2,1)} custom-call(s32[1]{0:T(128)} %bitcast.1.turn_ref, s32[1,4096]{1,0:T(1,128)} %bitcast.10, s32[1,4096]{1,0:T(1,128)} %bitcast.11, f32[1,4096]{1,0:T(1,128)} %bitcast.12, f32[1,4096]{1,0:T(1,128)} %bitcast.13, s32[16,4096]{1,0:T(8,128)} %counts_hbm.1), custom_call_target="tpu_custom_call" | custom-call | flops 1073741824 | bytes 1048576 | tf_op jit(solution)/shard_map/pallas_call | solution.py:293
  4.5 36.9 %all_to_all.10 = bf16[128,5,2,128]{3,2,1,0:T(2,128)(2,1)S(1)} all-to-all(bf16[128,5,2,128]{3,2,1,0:T(2,128)(2,1)} %bitcast.9), channel_id=1, replica_groups=mesh['pixel'=16,'trow'=8,'tcol'=4] {'pixel','trow'}, dimensions={0} | all-to-all | bytes 655360 | tf_op jit(solution)/shard_map/all_to_all | solution.py:318
  41.4 0.2 shard_map.69.x0_ref
  41.6 3.1 %collective-permute-start.1 = (bf16[1040,128]{1,0:T(8,128)(2,1)S(1)}, bf16[1040,128]{1,0:T(8,128)(2,1)S(1)}, u32[]{:S(2)}, u32[]{:S(2)}) collective-permute-start(bf16[1040,128]{1,0:T(8,128)(2,1)S(1)} %shard_map.69.x0_ref), channel_id=1, source_target_pairs={{0,2},{1,3},{2,0},{3,1},{4,6},{5,7},{6,4},{7,5},{8,10},{9,11},{10,... | collective-permute-start | bytes 798728 | tf_op jit(solution)/shard_map/ppermute | solution.py:329
  44.6 4.7 %collective-permute-start = (bf16[1040,128]{1,0:T(8,128)(2,1)S(1)}, bf16[1040,128]{1,0:T(8,128)(2,1)S(1)}, u32[]{:S(2)}, u32[]{:S(2)}) collective-permute-start(bf16[1040,128]{1,0:T(8,128)(2,1)S(1)} %shard_map.69.x0_ref), channel_id=1, source_target_pairs={{0,1},{1,0},{2,3},{3,2},{4,5},{5,4},{6,7},{7,6},{8,9},{9,8},{10,11... | collective-permute-start | bytes 798728 | tf_op jit(solution)/shard_map/ppermute | solution.py:328
  49.3 0.0 collective-permute-done.1.x2_ref
  49.3 4.9 %collective-permute-start.2 = (bf16[1040,128]{1,0:T(8,128)(2,1)S(1)}, bf16[1040,128]{1,0:T(8,128)(2,1)S(1)}, u32[]{:S(2)}, u32[]{:S(2)}) collective-permute-start(bf16[1040,128]{1,0:T(8,128)(2,1)S(1)} %collective-permute-done.1.x2_ref), channel_id=1, source_target_pairs={{0,1},{1,0},{2,3},{3,2},{4,5},{5,4},{6,7},{7,6},{8,9},{9,8},{10,11... | collective-permute-start | bytes 798728 | tf_op jit(solution)/shard_map/ppermute | solution.py:330
  54.2 0.0 collective-permute-done.x1_ref
  54.2 1.1 %collective-permute-done.2.x3_ref = bf16[1040,128]{1,0:T(8,128)(2,1)S(1)} collective-permute-done((bf16[1040,128]{1,0:T(8,128)(2,1)S(1)}, bf16[1040,128]{1,0:T(8,128)(2,1)S(1)}, u32[]{:S(2)}, u32[]{:S(2)}) %collective-permute-start.2) | collective-permute-done | bytes 266272 | tf_op jit(solution)/shard_map/ppermute | solution.py:330
  55.4 2.0 %shard_map.70 = f32[8,72,128]{2,1,0:T(8,128)S(1)} custom-call(s32[1]{0:T(128)} %bitcast.me_ref, bf16[1040,128]{1,0:T(8,128)(2,1)S(1)} %shard_map.69.x0_ref, bf16[1040,128]{1,0:T(8,128)(2,1)S(1)} %collective-permute-done.x1_ref, bf16[1040,128]{1,0:T(8,128)(2,1)S(1)} %collective-permute-done.1.x2_ref, bf16[1040,128]{1,0:T(8,128)(2,1)S(1)} %collective-permute-done.2.x3_ref), custom_call_target="tpu_custom_call" | custom-call | flops 536870912 | bytes 1572864 | tf_op jit(solution)/shard_map/pallas_call | solution.py:332
  57.4 15.9 %all_to_all.11.in_ref = f32[8,72,128]{2,1,0:T(8,128)S(1)} all-to-all(f32[8,72,128]{2,1,0:T(8,128)S(1)} %shard_map.70), channel_id=1, replica_groups=mesh['pixel'=16,'trow'=8,'tcol'=4] {'trow'}, dimensions={0} | all-to-all | bytes 589824 | tf_op jit(solution)/shard_map/all_to_all | solution.py:341
  73.2 0.7 shard_map.71
Async XLA Ops:
  41.6 7.7 %collective-permute-start.1 = (bf16[1040,128]{1,0:T(8,128)(2,1)S(1)}, bf16[1040,128]{1,0:T(8,128)(2,1)S(1)}, u32[]{:S(2)}, u32[]{:S(2)}) collective-permute-start(bf16[1040,128]{1,0:T(8,128)(2,1)S(1)} %shard_map.69.x0_ref), channel_id=1, source_target_pairs={{0,2},{1,3},{2,0},{3,1},{4,6},{5,7},{6,4},{7,5},{8,10},{9,11},{10,... | collective-permute-start | bytes 798728 | tf_op jit(solution)/shard_map/ppermute | solution.py:329
  44.6 9.6 %collective-permute-start = (bf16[1040,128]{1,0:T(8,128)(2,1)S(1)}, bf16[1040,128]{1,0:T(8,128)(2,1)S(1)}, u32[]{:S(2)}, u32[]{:S(2)}) collective-permute-start(bf16[1040,128]{1,0:T(8,128)(2,1)S(1)} %shard_map.69.x0_ref), channel_id=1, source_target_pairs={{0,1},{1,0},{2,3},{3,2},{4,5},{5,4},{6,7},{7,6},{8,9},{9,8},{10,11... | collective-permute-start | bytes 798728 | tf_op jit(solution)/shard_map/ppermute | solution.py:328
  49.3 6.0 %collective-permute-start.2 = (bf16[1040,128]{1,0:T(8,128)(2,1)S(1)}, bf16[1040,128]{1,0:T(8,128)(2,1)S(1)}, u32[]{:S(2)}, u32[]{:S(2)}) collective-permute-start(bf16[1040,128]{1,0:T(8,128)(2,1)S(1)} %collective-permute-done.1.x2_ref), channel_id=1, source_target_pairs={{0,1},{1,0},{2,3},{3,2},{4,5},{5,4},{6,7},{7,6},{8,9},{9,8},{10,11... | collective-permute-start | bytes 798728 | tf_op jit(solution)/shard_map/ppermute | solution.py:330

commit v5 on v4

--- a/solution.py
+++ b/solution.py
@@ -3,6 +3,7 @@
 from jax import lax
 from jax.experimental import pallas as pl
 from jax.experimental.pallas import tpu as pltpu
+from jax.sharding import Mesh
 from jax.sharding import PartitionSpec as P
 
 CYCLES = 64
@@ -13,10 +14,12 @@
 N_PIXEL = 16
 N_TROW = 8
 N_TCOL = 4
+N_Z = 2
 SUB = 16
 OWNED = CYCLES // N_PIXEL
 COLS = N_TROW * SUB
 PAIRS = N_PIXEL // 2
+SEEN = N_TROW * N_Z * SUB
 ROWS = N_TCOL * SUB
 LANES = 128
 MESSAGE = 10
@@ -146,22 +149,27 @@
         late = slots[:, SUB // 2 :, b * CAP : (b + 1) * CAP]
         tiles.append(jnp.where(data, early, pltpu.roll(late, HALF, axis=2)))
         tiles.append(jnp.where(data, pltpu.roll(early, HALF, axis=2), late))
-    second, third, fourth = (pltpu.roll(tiles[m], 2 * m, axis=1) for m in (1, 2, 3))
-    groups = [
-        tiles[0],
-        jnp.where(row < 2, extras[0], second),
-        jnp.where(row < 2, second, jnp.where(row < 4, extras[0], third)),
-        jnp.where(row < 4, third, jnp.where(row < 6, extras[1], fourth)),
-        jnp.where(row < 6, fourth, extras[1]),
-    ]
+    groups = []
+    for b in range(2):
+        extra, (lower, upper) = extras[b], tiles[2 * b : 2 * b + 2]
+        second, third, fourth = (
+            pltpu.roll(x, 2 * m, axis=1) for m, x in ((1, lower), (2, upper), (3, upper))
+        )
+        groups += [
+            lower,
+            jnp.where(row < 2, extra, second),
+            jnp.where(row < 2, second, jnp.where(row < 4, extra, third)),
+            jnp.where(row < 4, third, jnp.where(row < 6, extra, fourth)),
+            jnp.where(row < 6, fourth, extra),
+        ]
     out_ref[...] = (
-        jnp.concatenate(groups, axis=1).reshape(2 * CYCLES * MESSAGE, LANES).astype(BF16)
+        jnp.concatenate(groups, axis=1).reshape(4 * CYCLES * MESSAGE, LANES).astype(BF16)
     )
 
 
 def pack_kernel(in_ref, out_ref):
-    per_shard = N_TROW * MESSAGE
-    shape = (N_TROW, SUB // 2, LANES)
+    per_shard = N_TROW * N_Z * MESSAGE
+    shape = (N_TROW * N_Z, SUB // 2, LANES)
     low = lax.broadcasted_iota(jnp.int32, shape, 2) < HALF
     row = lax.broadcasted_iota(jnp.int32, (SUB // 2, LANES), 0)
     lane = lax.broadcasted_iota(jnp.int32, (SUB // 2, LANES), 1)
@@ -173,7 +181,7 @@
             total = total + rows
             group = [rows[8 * i : 8 * i + 8] for i in range(per_shard // 8)]
             tiles = []
-            for first in (0, 5):
+            for first in range(0, len(group), 5):
                 g = group[first : first + 5]
                 tiles.append(g[0])
                 tiles.append(pltpu.roll(jnp.where(row < 2, g[2], g[1]), 6, axis=0))
@@ -183,55 +191,57 @@
         even, odd = halves
         early = jnp.where(low, even, odd)
         late = pltpu.roll(jnp.where(low, odd, even), HALF, axis=2)
-        out_ref[pair * COLS : (pair + 1) * COLS] = (
-            jnp.concatenate([early, late], axis=1).reshape(COLS, LANES).astype(BF16)
-        )
-    sums = jnp.zeros((SUB // 2, LANES), F32)
-    usable = jnp.zeros((SUB // 2, LANES), F32)
-    for j in range(N_TROW):
-        at = j * MESSAGE + SUB // 2
-        extra = jnp.broadcast_to(total[at : at + 1], (SUB // 2, LANES))
-        added = extra + pltpu.roll(extra, LANES - SUB, axis=1)
-        added = added + pltpu.roll(extra, LANES - 2 * SUB, axis=1)
-        here = lane // SUB == j
-        sums = jnp.where(here, pltpu.roll(added, j * SUB, axis=1), sums)
-        count = pltpu.roll(extra, (LANES - 3 * SUB + j * SUB) % LANES, axis=1)
-        usable = jnp.where(here, count, usable)
-    hi, mid, lo = three_parts(sums)
-    n_hi, n_lo, _ = three_parts(usable)
-    tail = jnp.zeros((SUB // 2, LANES), F32)
-    for i, x in enumerate((hi, mid, lo, n_hi, n_lo)):
-        tail = jnp.where(row == i, x, tail)
-    out_ref[PAIRS * COLS :] = jnp.concatenate([tail, jnp.zeros_like(tail)], axis=0).astype(BF16)
-
-
-def gram_kernel(me_ref, x0_ref, x1_ref, x2_ref, x3_ref, out_ref, all_ref, own_ref):
-    me = me_ref[0]
-    depth = PAIRS * LANES
-    t_row = lax.broadcasted_iota(jnp.int32, (COLS, FRAMES), 0)
-    t_col = lax.broadcasted_iota(jnp.int32, (COLS, FRAMES), 1)
-    stats = jnp.zeros((SUB, FRAMES), F32)
-    for d, ref in enumerate((x0_ref, x1_ref, x2_ref, x3_ref)):
-        k = me ^ d
+        out_ref[pair * SEEN : (pair + 1) * SEEN] = (
+            jnp.concatenate([early, late], axis=1).reshape(SEEN, LANES).astype(BF16)
+        )
+    tails = []
+    for half in range(SEEN // LANES):
+        sums = jnp.zeros((SUB // 2, LANES), F32)
+        usable = jnp.zeros((SUB // 2, LANES), F32)
+        for i in range(LANES // SUB):
+            at = (half * LANES // SUB + i) * MESSAGE + SUB // 2
+            extra = jnp.broadcast_to(total[at : at + 1], (SUB // 2, LANES))
+            added = extra + pltpu.roll(extra, LANES - SUB, axis=1)
+            added = added + pltpu.roll(extra, LANES - 2 * SUB, axis=1)
+            here = lane // SUB == i
+            sums = jnp.where(here, pltpu.roll(added, i * SUB, axis=1), sums)
+            count = pltpu.roll(extra, (LANES - 3 * SUB + i * SUB) % LANES, axis=1)
+            usable = jnp.where(here, count, usable)
+        hi, mid, lo = three_parts(sums)
+        n_hi, n_lo, _ = three_parts(usable)
+        tail = jnp.zeros((SUB // 2, LANES), F32)
+        for i, x in enumerate((hi, mid, lo, n_hi, n_lo)):
+            tail = jnp.where(row == i, x, tail)
+        tails.append(tail)
+    out_ref[PAIRS * SEEN :] = jnp.concatenate(tails, axis=0).astype(BF16)
+
+
+def gram_kernel(core_ref, z_ref, x0_ref, x1_ref, out_ref, all_ref, own_ref):
+    me = core_ref[0]
+    my_z = z_ref[0]
+    t_row = lax.broadcasted_iota(jnp.int32, (LANES, FRAMES), 0)
+    t_col = lax.broadcasted_iota(jnp.int32, (LANES, FRAMES), 1)
+    stats = jnp.zeros((SUB // 2, FRAMES), F32)
+    for d, ref in enumerate((x0_ref, x1_ref)):
+        core = me ^ d
         for j in range(N_TROW):
-            rows = pl.ds(pl.multiple_of(j * ROWS + k * SUB, SUB), SUB)
-            for pair in range(PAIRS):
-                at = pair * COLS + j * SUB
-                all_ref[rows, pair * LANES : (pair + 1) * LANES] = ref[at : at + SUB]
-        goes_to = (t_row // SUB) * ROWS + k * SUB + t_row % SUB
-        spread = jnp.where(goes_to == t_col, 1.0, 0.0).astype(BF16)
-        stats = stats + dot_n(ref[PAIRS * COLS :], spread)
-    for pair in range(PAIRS):
-        own_ref[:, pair * LANES : (pair + 1) * LANES] = x0_ref[pair * COLS : (pair + 1) * COLS]
-
-    own = x0_ref[PAIRS * COLS :].astype(F32)
-    own_inv = 1.0 / jnp.maximum(own[0:1] + own[1:2] + own[2:3], 1.0)
-    usable = (own[3:4] + own[4:5])[:, 0:1]
+            for z in range(N_Z):
+                first = j * ROWS + z * 2 * SUB + core * SUB
+                rows = pl.ds(pl.multiple_of(first, SUB), SUB)
+                for pair in range(PAIRS):
+                    at = pair * SEEN + (j * N_Z + z) * SUB
+                    here = ref[at : at + SUB]
+                    all_ref[rows, pair * LANES : (pair + 1) * LANES] = here
+        tail = ref[PAIRS * SEEN :]
+        for part in range(SEEN // LANES):
+            group = t_row // SUB + part * LANES // SUB
+            goes_to = group * 2 * SUB + core * SUB + t_row % SUB
+            spread = jnp.where(goes_to == t_col, 1.0, 0.0).astype(BF16)
+            stats = stats + dot_n(tail, spread)[part * SUB // 2 : (part + 1) * SUB // 2]
+
     inv = 1.0 / jnp.maximum(stats[0:1] + stats[1:2] + stats[2:3], 1.0)
     inv_col = jnp.broadcast_to(inv, (LANES, FRAMES)).T
-
-    tile = dot_t(all_ref[...], own_ref[...])
-    tile = tile * (inv_col * (own_inv * usable))
+    usable = (stats[3:4] + stats[4:5])[:, 0:1]
 
     lags = jnp.zeros((1, FRAMES), F32)
     flip_row = lax.broadcasted_iota(jnp.int32, (LANES, LANES), 0)
@@ -255,12 +265,30 @@
         lags = lags + part
     remaining = (FRAMES - lax.broadcasted_iota(jnp.int32, (1, FRAMES), 1)).astype(F32)
     lags = lags * usable / remaining
-
+    tail = jnp.concatenate(
+        [lags[:, b * LANES : (b + 1) * LANES] for b in range(FRAMES // LANES)]
+        + [jnp.zeros((4, LANES), F32)],
+        axis=0,
+    )
+
+    own_sums = x0_ref[PAIRS * SEEN :].astype(F32)
+    own = jnp.zeros((SUB // 2, LANES), F32)
+    for z in range(N_Z):
+        pieces = []
+        for j in range(N_TROW):
+            at = (j * N_Z + z) * SUB
+            half = at // LANES * (SUB // 2)
+            pieces.append(own_sums[half : half + SUB // 2, at % LANES : at % LANES + SUB])
+        own = jnp.where(my_z == z, jnp.concatenate(pieces, axis=1), own)
+    own_inv = usable / jnp.maximum(own[0:1] + own[1:2] + own[2:3], 1.0)
+    for j in range(N_TROW):
+        for pair in range(PAIRS):
+            at = pl.ds(pl.multiple_of(pair * SEEN + j * N_Z * SUB + my_z * SUB, SUB), SUB)
+            own_ref[j * SUB : (j + 1) * SUB, pair * LANES : (pair + 1) * LANES] = x0_ref[at]
+    tile = dot_t(all_ref[...], own_ref[...]) * (inv_col * own_inv)
     for i in range(N_TROW):
         out_ref[i, :ROWS] = tile[i * ROWS : (i + 1) * ROWS]
-        for b in range(FRAMES // LANES):
-            out_ref[i, ROWS + b : ROWS + b + 1] = lags[:, b * LANES : (b + 1) * LANES]
-        out_ref[i, ROWS + 4 :] = jnp.zeros((4, LANES), F32)
+        out_ref[i, ROWS:] = tail
 
 
 def join_kernel(in_ref, tile_ref, lag_ref):
@@ -289,10 +317,11 @@
 
 def per_device(counts, labels, pixel_mask, dark_level, flat_field):
     turn = (lax.axis_index("pixel") & 1).astype(jnp.int32).reshape(1)
-    me = lax.axis_index("tcol").astype(jnp.int32).reshape(1)
+    core = lax.axis_index("core").astype(jnp.int32).reshape(1)
+    z = lax.axis_index("z").astype(jnp.int32).reshape(1)
     payload = call(
         slot_kernel,
-        jax.ShapeDtypeStruct((2 * CYCLES * MESSAGE, LANES), BF16),
+        jax.ShapeDtypeStruct((4 * CYCLES * MESSAGE, LANES), BF16),
         5,
         scalars=1,
         scratch=[
@@ -316,28 +345,30 @@
         counts,
     )
     arrived = lax.all_to_all(
-        payload.reshape(2 * CYCLES, MESSAGE // 2, 2, LANES), ("pixel", "trow"), 0, 0, tiled=True
+        payload.reshape(4 * CYCLES, MESSAGE // 2, 2, LANES),
+        ("pixel", "trow", "z"),
+        0,
+        0,
+        tiled=True,
     )
     packed = call(
         pack_kernel,
-        jax.ShapeDtypeStruct((PAIRS * COLS + SUB, LANES), BF16),
+        jax.ShapeDtypeStruct((PAIRS * SEEN + SUB, LANES), BF16),
         1,
         flops=1 << 20,
-        size=3 << 18,
-    )(arrived.reshape(2 * CYCLES * MESSAGE, LANES))
-    beside = lax.ppermute(packed, "tcol", [(k, k ^ 1) for k in range(N_TCOL)])
-    across = lax.ppermute(packed, "tcol", [(k, k ^ 2) for k in range(N_TCOL)])
-    corner = lax.ppermute(across, "tcol", [(k, k ^ 1) for k in range(N_TCOL)])
+        size=3 << 19,
+    )(arrived.reshape(4 * CYCLES * MESSAGE, LANES))
+    beside = lax.ppermute(packed, "core", [(0, 1), (1, 0)])
     depth = PAIRS * LANES
     sends = call(
         gram_kernel,
         jax.ShapeDtypeStruct((N_TROW, ROWS + 8, LANES), F32),
-        4,
-        scalars=1,
+        2,
+        scalars=2,
         scratch=[pltpu.VMEM((FRAMES, depth), BF16), pltpu.VMEM((COLS, depth), BF16)],
         flops=2 * FRAMES * FRAMES * depth,
         size=3 << 19,
-    )(me, packed, beside, across, corner)
+    )(core, z, packed, beside)
     gets = lax.all_to_all(sends, "trow", 0, 0, tiled=True)
     return call(
         join_kernel,
@@ -352,11 +383,15 @@
 
 
 def solution(mesh):
-    placed = (P(("trow", "tcol"), "pixel"), P("pixel", None), P("pixel"), P("pixel"), P("pixel"))
+    fine = Mesh(
+        mesh.devices.reshape(N_PIXEL, N_TROW, N_Z, 2), ("pixel", "trow", "z", "core")
+    )
+    frames = ("trow", "z", "core")
+    placed = (P(frames, "pixel"), P("pixel", None), P("pixel"), P("pixel"), P("pixel"))
     return jax.shard_map(
         per_device,
-        mesh=mesh,
+        mesh=fine,
         in_specs=placed,
-        out_specs=(P("pixel", "trow", "tcol"), P("pixel", None)),
+        out_specs=(P("pixel", "trow", ("z", "core")), P("pixel", None)),
         check_vma=False,
     )

time: 74.2 us -> 74 us (level)
  starting transfers between devices: 12.6 us -> 5.24 us
  blocking collectives: 52.7 us -> 59.4 us
    all_to_all x1, blocking collectives: 36.9 us -> 44.7 us  [per_device(): lax.all_to_all(payload.reshape(4 * CYCLES, MESSAGE // 2, 2, LANES), ('pix...]
    ppermute x3 -> x1, starting transfers between devices: 12.6 us -> 5.24 us  [per_device(): beside = lax.ppermute(packed, 'core', [(0, 1), (1, 0)])]
    all_to_all x1, blocking collectives: 15.9 us -> 14.7 us  [per_device(): gets = lax.all_to_all(sends, 'trow', 0, 0, tiled=True)]
    ppermute x3 -> x1, waiting for transfers between devices: 1.14 us -> 1.52 us  [per_device(): beside = lax.ppermute(packed, 'core', [(0, 1), (1, 0)])]
  transfers between devices with their start and end apart: 3 -> 1, of which waited for: 1 -> 1; matrix products, arithmetic and copies ran while one was open for 0% -> 0% of each run, Pallas kernels for 0% -> 0%
where the time goes in v5:
time: 74 us; the launch traced here: 73.7 us
  blocking collectives  59.4 us (80%)
  Pallas kernels  6.83 us (9%)
  starting transfers between devices  5.24 us (7%)
  waiting for transfers between devices  1.52 us (2%)
    all_to_all x1, blocking collectives, per_device(): lax.all_to_all(payload.reshape(4 * CYCLES, MESSAGE // 2, 2, LANES), ('pix...  44.7 us
    all_to_all x1, blocking collectives, per_device(): gets = lax.all_to_all(sends, 'trow', 0, 0, tiled=True)  14.7 us
    ppermute x1, starting transfers between devices, per_device(): beside = lax.ppermute(packed, 'core', [(0, 1), (1, 0)])  5.24 us
    pallas_call x1, Pallas kernels, per_device(): call(slot_kernel, jax.ShapeDtypeStruct((4 * CYCLES * MESSAGE, LANES), BF1...  4.05 us
    pallas_call x1, Pallas kernels, per_device(): call(gram_kernel, jax.ShapeDtypeStruct((N_TROW, ROWS + 8, LANES), F32), 2...  1.77 us
    ppermute x1, waiting for transfers between devices, per_device(): beside = lax.ppermute(packed, 'core', [(0, 1), (1, 0)])  1.52 us
  transfers between devices with their start and end apart: 1, of which 1 were waited for; matrix products, arithmetic and copies ran while one was open for 0% of the time, Pallas kernels for 0%

profile of v5, /device:TPU:1, one launch (start us, length us, event | category | flops | bytes accessed | tf_op | source)
XLA Modules:
  0.0 73.7 jit_solution(18214904842023548352)
XLA Ops:
  0.6 4.0 %shard_map.68 = bf16[2560,128]{1,0:T(8,128)(2,1)} custom-call(s32[1]{0:T(128)} %bitcast.2.turn_ref, s32[1,4096]{1,0:T(1,128)} %bitcast.11, s32[1,4096]{1,0:T(1,128)} %bitcast.12, f32[1,4096]{1,0:T(1,128)} %bitcast.13, f32[1,4096]{1,0:T(1,128)} %bitcast.14, s32[16,4096]{1,0:T(8,128)} %counts_hbm.1), custom_call_target="tpu_custom_call" | custom-call | flops 1073741824 | bytes 1048576 | tf_op jit(solution)/shard_map/pallas_call | solution.py:322
  4.7 44.7 %all_to_all.10 = bf16[256,5,2,128]{3,2,1,0:T(2,128)(2,1)S(1)} all-to-all(bf16[256,5,2,128]{3,2,1,0:T(2,128)(2,1)} %bitcast.10), channel_id=1, replica_groups=mesh['pixel'=16,'trow'=8,'z'=2,'core'=2] {'pixel','trow','z'}, dimensions={0} | all-to-all | bytes 1310720 | tf_op jit(solution)/shard_map/all_to_all | solution.py:347
  49.4 0.3 shard_map.69.x0_ref
  49.8 5.2 %collective-permute-start = (bf16[2064,128]{1,0:T(8,128)(2,1)S(1)}, bf16[2064,128]{1,0:T(8,128)(2,1)S(1)}, u32[]{:S(2)}, u32[]{:S(2)}) collective-permute-start(bf16[2064,128]{1,0:T(8,128)(2,1)S(1)} %shard_map.69.x0_ref), channel_id=1, source_target_pairs={{0,1},{1,0},{2,3},{3,2},{4,5},{5,4},{6,7},{7,6},{8,9},{9,8},{10,11... | collective-permute-start | bytes 1585160 | tf_op jit(solution)/shard_map/ppermute | solution.py:361
  55.0 1.5 %collective-permute-done.x1_ref = bf16[2064,128]{1,0:T(8,128)(2,1)S(1)} collective-permute-done((bf16[2064,128]{1,0:T(8,128)(2,1)S(1)}, bf16[2064,128]{1,0:T(8,128)(2,1)S(1)}, u32[]{:S(2)}, u32[]{:S(2)}) %collective-permute-start) | collective-permute-done | bytes 528416 | tf_op jit(solution)/shard_map/ppermute | solution.py:361
  56.6 1.8 %shard_map.70 = f32[8,72,128]{2,1,0:T(8,128)S(1)} custom-call(s32[1]{0:T(128)} %bitcast.core_ref, s32[1]{0:T(128)} %bitcast.1.z_ref, bf16[2064,128]{1,0:T(8,128)(2,1)S(1)} %shard_map.69.x0_ref, bf16[2064,128]{1,0:T(8,128)(2,1)S(1)} %collective-permute-done.x1_ref), custom_call_target="tpu_custom_call" | custom-call | flops 536870912 | bytes 1572864 | tf_op jit(solution)/shard_map/pallas_call | solution.py:363
  58.3 14.7 %all_to_all.11.in_ref = f32[8,72,128]{2,1,0:T(8,128)S(1)} all-to-all(f32[8,72,128]{2,1,0:T(8,128)S(1)} %shard_map.70), channel_id=1, replica_groups=mesh['pixel'=16,'trow'=8,'z'=2,'core'=2] {'trow'}, dimensions={0} | all-to-all | bytes 589824 | tf_op jit(solution)/shard_map/all_to_all | solution.py:372
  73.0 0.7 shard_map.71
Async XLA Ops:
  49.8 6.8 %collective-permute-start = (bf16[2064,128]{1,0:T(8,128)(2,1)S(1)}, bf16[2064,128]{1,0:T(8,128)(2,1)S(1)}, u32[]{:S(2)}, u32[]{:S(2)}) collective-permute-start(bf16[2064,128]{1,0:T(8,128)(2,1)S(1)} %shard_map.69.x0_ref), channel_id=1, source_target_pairs={{0,1},{1,0},{2,3},{3,2},{4,5},{5,4},{6,7},{7,6},{8,9},{9,8},{10,11... | collective-permute-start | bytes 1585160 | tf_op jit(solution)/shard_map/ppermute | solution.py:361

commit v6 on v4

--- a/solution.py
+++ b/solution.py
@@ -20,6 +20,7 @@
 ROWS = N_TCOL * SUB
 LANES = 128
 MESSAGE = 10
+FILLED = CYCLES // 2 * SUB
 CHUNK = 512
 RANK = 256
 F32 = jnp.float32
@@ -89,7 +90,6 @@
     rank = jnp.concatenate(ranks, axis=1).astype(jnp.int32)
     slot = ((rank + turn * HALF) & (CAP - 1)) + (labels & 1) * CAP
     slot16 = slot.astype(F32).astype(BF16)
-    label16 = labels.astype(F32).astype(BF16)
     pair16 = (labels >> 1).astype(F32).astype(BF16)
 
     get_dark.wait()
@@ -98,21 +98,25 @@
     frames = (
         flat_ref[...] * live * (counts_ref[...].astype(F32) - dark_ref[...])
     ).astype(BF16)
-    live16 = jnp.broadcast_to(live, (SUB, PIX)).astype(BF16)
-
-    slots = jnp.zeros((CYCLES // 2 * SUB, 2 * CAP), F32)
-    sums = jnp.zeros((CYCLES, LANES), F32)
+    live16 = live.astype(BF16)
+
+    slots = jnp.zeros((FILLED + CYCLES // 2, 2 * CAP), F32)
     slot_of_row = lax.broadcasted_iota(jnp.int32, (2 * CAP, CHUNK), 0).astype(F32).astype(BF16)
-    row = lax.broadcasted_iota(jnp.int32, (CYCLES, CHUNK), 0)
-    even_first = ((row & (CYCLES // 2 - 1)) * 2 + row // (CYCLES // 2)).astype(F32).astype(BF16)
+    pairs = lax.broadcasted_iota(jnp.int32, (CYCLES // 2, CHUNK), 0).astype(F32).astype(BF16)
     one = jnp.ones((2 * CAP, CHUNK), BF16)
     none = jnp.zeros((SUB, CHUNK), BF16)
     for c in range(PIX // CHUNK):
         span = slice(c * CHUNK, (c + 1) * CHUNK)
         here = jnp.broadcast_to(pair16[:, span], (SUB, CHUNK))
         chunk = frames[:, span]
+        usable = jnp.where(
+            jnp.broadcast_to(pair16[:, span], (CYCLES // 2, CHUNK)) == pairs,
+            jnp.broadcast_to(live16[:, span], (CYCLES // 2, CHUNK)),
+            jnp.zeros((CYCLES // 2, CHUNK), BF16),
+        )
         left = jnp.concatenate(
-            [jnp.where(here == jnp.array(r, BF16), chunk, none) for r in range(CYCLES // 2)],
+            [jnp.where(here == jnp.array(r, BF16), chunk, none) for r in range(CYCLES // 2)]
+            + [usable],
             axis=0,
         )
         right = jnp.where(
@@ -121,25 +125,26 @@
             jnp.zeros_like(one),
         )
         slots = slots + dot_t(left, right)
-        member = jnp.where(
-            jnp.broadcast_to(label16[:, span], (CYCLES, CHUNK)) == even_first,
-            one[:CYCLES],
-            jnp.zeros_like(one[:CYCLES]),
-        )
-        stack = jnp.concatenate([chunk, chunk, chunk, live16[:, span]] * 2, axis=0)
-        sums = sums + dot_t(member, stack)
-
-    hi, mid, lo = three_parts(sums)
-    part = lax.broadcasted_iota(jnp.int32, (CYCLES, LANES), 1) // SUB
-    extra = jnp.where(part == 0, hi, jnp.where(part == 1, mid, jnp.where(part == 2, lo, sums)))
+
+    in_row = lax.broadcasted_iota(jnp.int32, (2 * CAP, 2 * CAP), 0) // CAP
+    in_col = lax.broadcasted_iota(jnp.int32, (2 * CAP, 2 * CAP), 1) // CAP
+    same = jnp.where(in_row == in_col, 1.0, 0.0).astype(BF16)
+    sums = dot_n(slots.astype(BF16), same)
+    counted = sums[FILLED:]
+    sums = sums[:FILLED].reshape(CYCLES // 2, SUB, 2 * CAP)
+    lane = lax.broadcasted_iota(jnp.int32, sums.shape, 2) % SUB
+    sums = jnp.where(lane == lax.broadcasted_iota(jnp.int32, sums.shape, 1), sums, 0.0)
+    hi, mid, lo = three_parts(jnp.sum(sums, axis=1))
+    part = lax.broadcasted_iota(jnp.int32, (CYCLES // 2, 2 * CAP), 1) % CAP // SUB
+    extra = jnp.where(part == 0, hi, jnp.where(part == 1, mid, jnp.where(part == 2, lo, counted)))
     shape = (CYCLES // 2, SUB // 2, LANES)
     extras = [
-        jnp.broadcast_to(extra[b * shape[0] : (b + 1) * shape[0]][:, None, :], shape)
+        jnp.broadcast_to(extra[:, b * LANES : (b + 1) * LANES][:, None, :], shape)
         for b in range(2)
     ]
     data = (lax.broadcasted_iota(jnp.int32, shape, 2) >= HALF) == (turn == 1)
     row = lax.broadcasted_iota(jnp.int32, shape, 1)
-    slots = slots.reshape(CYCLES // 2, SUB, 2 * CAP)
+    slots = slots[:FILLED].reshape(CYCLES // 2, SUB, 2 * CAP)
     tiles = []
     for b in range(2):
         early = slots[:, : SUB // 2, b * CAP : (b + 1) * CAP]
@@ -233,26 +238,27 @@
     tile = dot_t(all_ref[...], own_ref[...])
     tile = tile * (inv_col * (own_inv * usable))
 
-    lags = jnp.zeros((1, FRAMES), F32)
-    flip_row = lax.broadcasted_iota(jnp.int32, (LANES, LANES), 0)
-    flip_col = lax.broadcasted_iota(jnp.int32, (LANES, LANES), 1)
-    flip = jnp.where(flip_row + flip_col == LANES - 1, 1.0, 0.0).astype(BF16)
+    group = SUB // 2
+    along = jnp.zeros((group, FRAMES), F32)
+    row = lax.broadcasted_iota(jnp.int32, (LANES, LANES), 0)
+    col = lax.broadcasted_iota(jnp.int32, (LANES, LANES), 1)
     for b in range(FRAMES // LANES):
         start = b * LANES
         width = FRAMES - start
-        back = dot_n(flip, all_ref[start : start + LANES]).astype(BF16)
-        back_stats = dot_n(stats[:, start : start + LANES].astype(BF16), flip)
-        back_sums = back_stats[0:1] + back_stats[1:2] + back_stats[2:3]
-        back_inv = jnp.broadcast_to(1.0 / jnp.maximum(back_sums, 1.0), (LANES, LANES)).T[:, 0:1]
-        block = dot_t(back, all_ref[start:])
-        row = lax.broadcasted_iota(jnp.int32, (LANES, width), 0)
-        col = lax.broadcasted_iota(jnp.int32, (LANES, width), 1)
-        block = jnp.where(row + col >= LANES - 1, block * (back_inv * inv[:, start:]), 0.0)
-        block = pltpu.roll(block, width - LANES + 1, axis=1, stride=1, stride_axis=0)
-        part = jnp.sum(block, axis=0, keepdims=True)
+        block = dot_t(all_ref[start : start + LANES], all_ref[start:])
+        block = block * (inv_col[start : start + LANES, 0:1] * inv[:, start:])
+        corner = jnp.where(col >= row, block[:, :LANES], 0.0)
+        block = corner if width == LANES else jnp.concatenate([corner, block[:, LANES:]], axis=1)
+        part = block[:group]
+        for first in range(group, LANES, group):
+            part = part + pltpu.roll(block[first : first + group], width - first, axis=1)
         if width < FRAMES:
-            part = jnp.concatenate([part, jnp.zeros((1, start), F32)], axis=1)
-        lags = lags + part
+            part = jnp.concatenate([part, jnp.zeros((group, start), F32)], axis=1)
+        along = along + part
+    place = lax.broadcasted_iota(jnp.int32, (group, FRAMES), 0)
+    for step in (1, 2, 4):
+        along = jnp.where((place & step) > 0, pltpu.roll(along, FRAMES - step, axis=1), along)
+    lags = jnp.sum(along, axis=0, keepdims=True)
     remaining = (FRAMES - lax.broadcasted_iota(jnp.int32, (1, FRAMES), 1)).astype(F32)
     lags = lags * usable / remaining
 
@@ -271,7 +277,7 @@
             lag_ref[c : c + 1, b * LANES : (b + 1) * LANES] = both[ROWS + b : ROWS + b + 1]
 
 
-def call(body, out_shape, n_in, scalars=0, scratch=(), flops=0, size=0, source=pltpu.VMEM, limit=32 << 20):
+def call(body, out_shape, n_in, scalars=0, scratch=(), flops=0, size=0, source=pltpu.VMEM):
     vmem = pl.BlockSpec(memory_space=pltpu.VMEM)
     given = pl.BlockSpec(memory_space=source)
     smem = pl.BlockSpec(memory_space=pltpu.SMEM)
@@ -282,7 +288,7 @@
         in_specs=[smem] * scalars + [given] * n_in,
         out_specs=(vmem,) * len(out_shape) if many else vmem,
         scratch_shapes=list(scratch),
-        compiler_params=pltpu.CompilerParams(vmem_limit_bytes=limit),
+        compiler_params=pltpu.CompilerParams(vmem_limit_bytes=32 << 20),
         cost_estimate=pl.CostEstimate(flops=flops, bytes_accessed=size, transcendentals=0),
     )
 
@@ -306,14 +312,18 @@
         flops=2 * CYCLES * SUB * CAP * PIX,
         size=1 << 20,
         source=pltpu.HBM,
-        limit=63 << 20,
     )(
         turn,
-        labels.reshape(1, PIX),
-        pixel_mask.reshape(1, PIX),
-        dark_level.reshape(1, PIX),
-        flat_field.reshape(1, PIX),
-        counts,
+        *(
+            pltpu.with_memory_space_constraint(x, pltpu.HBM)
+            for x in (
+                labels.reshape(1, PIX),
+                pixel_mask.reshape(1, PIX),
+                dark_level.reshape(1, PIX),
+                flat_field.reshape(1, PIX),
+                counts,
+            )
+        ),
     )
     arrived = lax.all_to_all(
         payload.reshape(2 * CYCLES, MESSAGE // 2, 2, LANES), ("pixel", "trow"), 0, 0, tiled=True

time: 74.2 us -> 73.1 us (0.985)
  Pallas kernels: 6.72 us -> 5.76 us
where the time goes in v6:
time: 73.1 us; the launch traced here: 72.7 us
  blocking collectives  52.5 us (72%)
  starting transfers between devices  12.6 us (17%)
  Pallas kernels  5.76 us (8%)
  waiting for transfers between devices  1.14 us (2%)
    all_to_all x1, blocking collectives, per_device(): lax.all_to_all(payload.reshape(2 * CYCLES, MESSAGE // 2, 2, LANES), ('pix...  36.6 us
    all_to_all x1, blocking collectives, per_device(): gets = lax.all_to_all(sends, 'trow', 0, 0, tiled=True)  15.9 us
    ppermute x1, starting transfers between devices, per_device(): corner = lax.ppermute(across, 'tcol', [(k, k ^ 1) for k in range(N_TCOL)])  4.89 us
    ppermute x1, starting transfers between devices, per_device(): beside = lax.ppermute(packed, 'tcol', [(k, k ^ 1) for k in range(N_TCOL)])  4.63 us
    pallas_call x1, Pallas kernels, per_device(): call(slot_kernel, jax.ShapeDtypeStruct((2 * CYCLES * MESSAGE, LANES), BF1...  3.12 us
    ppermute x1, starting transfers between devices, per_device(): across = lax.ppermute(packed, 'tcol', [(k, k ^ 2) for k in range(N_TCOL)])  3.12 us
    pallas_call x1, Pallas kernels, per_device(): call(gram_kernel, jax.ShapeDtypeStruct((N_TROW, ROWS + 8, LANES), F32), 4...  1.76 us
  transfers between devices with their start and end apart: 3, of which 1 were waited for; matrix products, arithmetic and copies ran while one was open for 0% of the time, Pallas kernels for 0%

profile of v6, /device:TPU:1, one launch (start us, length us, event | category | flops | bytes accessed | tf_op | source)
XLA Modules:
  0.0 72.7 jit_solution(1364970398936458713)
XLA Ops:
  0.6 3.1 %shard_map.68 = bf16[1280,128]{1,0:T(8,128)(2,1)S(1)} custom-call(s32[1]{0:T(128)} %bitcast.1.turn_ref, s32[1,4096]{1,0:T(1,128)} %bitcast.10, s32[1,4096]{1,0:T(1,128)} %bitcast.11, f32[1,4096]{1,0:T(1,128)} %bitcast.12, f32[1,4096]{1,0:T(1,128)} %bitcast.13, s32[16,4096]{1,0:T(8,128)} %counts_hbm.1), custom_call_target="tpu_custom_call" | custom-call | flops 1073741824 | bytes 1048576 | tf_op jit(solution)/shard_map/pallas_call | solution.py:299
  3.8 36.6 %all_to_all.10 = bf16[128,5,2,128]{3,2,1,0:T(2,128)(2,1)S(1)} all-to-all(bf16[128,5,2,128]{3,2,1,0:T(2,128)(2,1)S(1)} %bitcast.9), channel_id=1, replica_groups=mesh['pixel'=16,'trow'=8,'tcol'=4] {'pixel','trow'}, dimensions={0} | all-to-all | bytes 655360 | tf_op jit(solution)/shard_map/all_to_all | solution.py:328
  40.4 0.2 shard_map.69.x0_ref
  40.6 3.1 %collective-permute-start.1 = (bf16[1040,128]{1,0:T(8,128)(2,1)S(1)}, bf16[1040,128]{1,0:T(8,128)(2,1)S(1)}, u32[]{:S(2)}, u32[]{:S(2)}) collective-permute-start(bf16[1040,128]{1,0:T(8,128)(2,1)S(1)} %shard_map.69.x0_ref), channel_id=1, source_target_pairs={{0,2},{1,3},{2,0},{3,1},{4,6},{5,7},{6,4},{7,5},{8,10},{9,11},{10,... | collective-permute-start | bytes 798728 | tf_op jit(solution)/shard_map/ppermute | solution.py:339
  43.7 4.6 %collective-permute-start = (bf16[1040,128]{1,0:T(8,128)(2,1)S(1)}, bf16[1040,128]{1,0:T(8,128)(2,1)S(1)}, u32[]{:S(2)}, u32[]{:S(2)}) collective-permute-start(bf16[1040,128]{1,0:T(8,128)(2,1)S(1)} %shard_map.69.x0_ref), channel_id=1, source_target_pairs={{0,1},{1,0},{2,3},{3,2},{4,5},{5,4},{6,7},{7,6},{8,9},{9,8},{10,11... | collective-permute-start | bytes 798728 | tf_op jit(solution)/shard_map/ppermute | solution.py:338
  48.4 0.0 collective-permute-done.1.x2_ref
  48.4 4.9 %collective-permute-start.2 = (bf16[1040,128]{1,0:T(8,128)(2,1)S(1)}, bf16[1040,128]{1,0:T(8,128)(2,1)S(1)}, u32[]{:S(2)}, u32[]{:S(2)}) collective-permute-start(bf16[1040,128]{1,0:T(8,128)(2,1)S(1)} %collective-permute-done.1.x2_ref), channel_id=1, source_target_pairs={{0,1},{1,0},{2,3},{3,2},{4,5},{5,4},{6,7},{7,6},{8,9},{9,8},{10,11... | collective-permute-start | bytes 798728 | tf_op jit(solution)/shard_map/ppermute | solution.py:340
  53.3 0.0 collective-permute-done.x1_ref
  53.3 1.1 %collective-permute-done.2.x3_ref = bf16[1040,128]{1,0:T(8,128)(2,1)S(1)} collective-permute-done((bf16[1040,128]{1,0:T(8,128)(2,1)S(1)}, bf16[1040,128]{1,0:T(8,128)(2,1)S(1)}, u32[]{:S(2)}, u32[]{:S(2)}) %collective-permute-start.2) | collective-permute-done | bytes 266272 | tf_op jit(solution)/shard_map/ppermute | solution.py:340
  54.4 1.8 %shard_map.70 = f32[8,72,128]{2,1,0:T(8,128)S(1)} custom-call(s32[1]{0:T(128)} %bitcast.me_ref, bf16[1040,128]{1,0:T(8,128)(2,1)S(1)} %shard_map.69.x0_ref, bf16[1040,128]{1,0:T(8,128)(2,1)S(1)} %collective-permute-done.x1_ref, bf16[1040,128]{1,0:T(8,128)(2,1)S(1)} %collective-permute-done.1.x2_ref, bf16[1040,128]{1,0:T(8,128)(2,1)S(1)} %collective-permute-done.2.x3_ref), custom_call_target="tpu_custom_call" | custom-call | flops 536870912 | bytes 1572864 | tf_op jit(solution)/shard_map/pallas_call | solution.py:342
  56.2 15.9 %all_to_all.11.in_ref = f32[8,72,128]{2,1,0:T(8,128)S(1)} all-to-all(f32[8,72,128]{2,1,0:T(8,128)S(1)} %shard_map.70), channel_id=1, replica_groups=mesh['pixel'=16,'trow'=8,'tcol'=4] {'trow'}, dimensions={0} | all-to-all | bytes 589824 | tf_op jit(solution)/shard_map/all_to_all | solution.py:351
  72.1 0.7 shard_map.71
Async XLA Ops:
  40.6 7.8 %collective-permute-start.1 = (bf16[1040,128]{1,0:T(8,128)(2,1)S(1)}, bf16[1040,128]{1,0:T(8,128)(2,1)S(1)}, u32[]{:S(2)}, u32[]{:S(2)}) collective-permute-start(bf16[1040,128]{1,0:T(8,128)(2,1)S(1)} %shard_map.69.x0_ref), channel_id=1, source_target_pairs={{0,2},{1,3},{2,0},{3,1},{4,6},{5,7},{6,4},{7,5},{8,10},{9,11},{10,... | collective-permute-start | bytes 798728 | tf_op jit(solution)/shard_map/ppermute | solution.py:339
  43.7 9.6 %collective-permute-start = (bf16[1040,128]{1,0:T(8,128)(2,1)S(1)}, bf16[1040,128]{1,0:T(8,128)(2,1)S(1)}, u32[]{:S(2)}, u32[]{:S(2)}) collective-permute-start(bf16[1040,128]{1,0:T(8,128)(2,1)S(1)} %shard_map.69.x0_ref), channel_id=1, source_target_pairs={{0,1},{1,0},{2,3},{3,2},{4,5},{5,4},{6,7},{7,6},{8,9},{9,8},{10,11... | collective-permute-start | bytes 798728 | tf_op jit(solution)/shard_map/ppermute | solution.py:338
  48.4 6.0 %collective-permute-start.2 = (bf16[1040,128]{1,0:T(8,128)(2,1)S(1)}, bf16[1040,128]{1,0:T(8,128)(2,1)S(1)}, u32[]{:S(2)}, u32[]{:S(2)}) collective-permute-start(bf16[1040,128]{1,0:T(8,128)(2,1)S(1)} %collective-permute-done.1.x2_ref), channel_id=1, source_target_pairs={{0,1},{1,0},{2,3},{3,2},{4,5},{5,4},{6,7},{7,6},{8,9},{9,8},{10,11... | collective-permute-start | bytes 798728 | tf_op jit(solution)/shard_map/ppermute | solution.py:340

commit v7 on v5

--- a/solution.py
+++ b/solution.py
@@ -23,8 +23,9 @@
 ROWS = N_TCOL * SUB
 LANES = 128
 MESSAGE = 10
+FILLED = CYCLES // 2 * SUB
 CHUNK = 512
-RANK = 256
+RANK = 128
 F32 = jnp.float32
 BF16 = jnp.bfloat16
 
@@ -92,7 +93,6 @@
     rank = jnp.concatenate(ranks, axis=1).astype(jnp.int32)
     slot = ((rank + turn * HALF) & (CAP - 1)) + (labels & 1) * CAP
     slot16 = slot.astype(F32).astype(BF16)
-    label16 = labels.astype(F32).astype(BF16)
     pair16 = (labels >> 1).astype(F32).astype(BF16)
 
     get_dark.wait()
@@ -101,21 +101,25 @@
     frames = (
         flat_ref[...] * live * (counts_ref[...].astype(F32) - dark_ref[...])
     ).astype(BF16)
-    live16 = jnp.broadcast_to(live, (SUB, PIX)).astype(BF16)
-
-    slots = jnp.zeros((CYCLES // 2 * SUB, 2 * CAP), F32)
-    sums = jnp.zeros((CYCLES, LANES), F32)
+    live16 = live.astype(BF16)
+
+    slots = jnp.zeros((FILLED + CYCLES // 2, 2 * CAP), F32)
     slot_of_row = lax.broadcasted_iota(jnp.int32, (2 * CAP, CHUNK), 0).astype(F32).astype(BF16)
-    row = lax.broadcasted_iota(jnp.int32, (CYCLES, CHUNK), 0)
-    even_first = ((row & (CYCLES // 2 - 1)) * 2 + row // (CYCLES // 2)).astype(F32).astype(BF16)
+    pairs = lax.broadcasted_iota(jnp.int32, (CYCLES // 2, CHUNK), 0).astype(F32).astype(BF16)
     one = jnp.ones((2 * CAP, CHUNK), BF16)
     none = jnp.zeros((SUB, CHUNK), BF16)
     for c in range(PIX // CHUNK):
         span = slice(c * CHUNK, (c + 1) * CHUNK)
         here = jnp.broadcast_to(pair16[:, span], (SUB, CHUNK))
         chunk = frames[:, span]
+        usable = jnp.where(
+            jnp.broadcast_to(pair16[:, span], (CYCLES // 2, CHUNK)) == pairs,
+            jnp.broadcast_to(live16[:, span], (CYCLES // 2, CHUNK)),
+            jnp.zeros((CYCLES // 2, CHUNK), BF16),
+        )
         left = jnp.concatenate(
-            [jnp.where(here == jnp.array(r, BF16), chunk, none) for r in range(CYCLES // 2)],
+            [jnp.where(here == jnp.array(r, BF16), chunk, none) for r in range(CYCLES // 2)]
+            + [usable],
             axis=0,
         )
         right = jnp.where(
@@ -124,25 +128,26 @@
             jnp.zeros_like(one),
         )
         slots = slots + dot_t(left, right)
-        member = jnp.where(
-            jnp.broadcast_to(label16[:, span], (CYCLES, CHUNK)) == even_first,
-            one[:CYCLES],
-            jnp.zeros_like(one[:CYCLES]),
-        )
-        stack = jnp.concatenate([chunk, chunk, chunk, live16[:, span]] * 2, axis=0)
-        sums = sums + dot_t(member, stack)
-
-    hi, mid, lo = three_parts(sums)
-    part = lax.broadcasted_iota(jnp.int32, (CYCLES, LANES), 1) // SUB
-    extra = jnp.where(part == 0, hi, jnp.where(part == 1, mid, jnp.where(part == 2, lo, sums)))
+
+    in_row = lax.broadcasted_iota(jnp.int32, (2 * CAP, 2 * CAP), 0) // CAP
+    in_col = lax.broadcasted_iota(jnp.int32, (2 * CAP, 2 * CAP), 1) // CAP
+    same = jnp.where(in_row == in_col, 1.0, 0.0).astype(BF16)
+    sums = dot_n(slots.astype(BF16), same)
+    counted = sums[FILLED:]
+    sums = sums[:FILLED].reshape(CYCLES // 2, SUB, 2 * CAP)
+    lane = lax.broadcasted_iota(jnp.int32, sums.shape, 2) % SUB
+    sums = jnp.where(lane == lax.broadcasted_iota(jnp.int32, sums.shape, 1), sums, 0.0)
+    hi, mid, lo = three_parts(jnp.sum(sums, axis=1))
+    part = lax.broadcasted_iota(jnp.int32, (CYCLES // 2, 2 * CAP), 1) % CAP // SUB
+    extra = jnp.where(part == 0, hi, jnp.where(part == 1, mid, jnp.where(part == 2, lo, counted)))
     shape = (CYCLES // 2, SUB // 2, LANES)
     extras = [
-        jnp.broadcast_to(extra[b * shape[0] : (b + 1) * shape[0]][:, None, :], shape)
+        jnp.broadcast_to(extra[:, b * LANES : (b + 1) * LANES][:, None, :], shape)
         for b in range(2)
     ]
     data = (lax.broadcasted_iota(jnp.int32, shape, 2) >= HALF) == (turn == 1)
     row = lax.broadcasted_iota(jnp.int32, shape, 1)
-    slots = slots.reshape(CYCLES // 2, SUB, 2 * CAP)
+    slots = slots[:FILLED].reshape(CYCLES // 2, SUB, 2 * CAP)
     tiles = []
     for b in range(2):
         early = slots[:, : SUB // 2, b * CAP : (b + 1) * CAP]
@@ -243,26 +248,27 @@
     inv_col = jnp.broadcast_to(inv, (LANES, FRAMES)).T
     usable = (stats[3:4] + stats[4:5])[:, 0:1]
 
-    lags = jnp.zeros((1, FRAMES), F32)
-    flip_row = lax.broadcasted_iota(jnp.int32, (LANES, LANES), 0)
-    flip_col = lax.broadcasted_iota(jnp.int32, (LANES, LANES), 1)
-    flip = jnp.where(flip_row + flip_col == LANES - 1, 1.0, 0.0).astype(BF16)
+    group = SUB // 2
+    along = jnp.zeros((group, FRAMES), F32)
+    row = lax.broadcasted_iota(jnp.int32, (LANES, LANES), 0)
+    col = lax.broadcasted_iota(jnp.int32, (LANES, LANES), 1)
     for b in range(FRAMES // LANES):
         start = b * LANES
         width = FRAMES - start
-        back = dot_n(flip, all_ref[start : start + LANES]).astype(BF16)
-        back_stats = dot_n(stats[:, start : start + LANES].astype(BF16), flip)
-        back_sums = back_stats[0:1] + back_stats[1:2] + back_stats[2:3]
-        back_inv = jnp.broadcast_to(1.0 / jnp.maximum(back_sums, 1.0), (LANES, LANES)).T[:, 0:1]
-        block = dot_t(back, all_ref[start:])
-        row = lax.broadcasted_iota(jnp.int32, (LANES, width), 0)
-        col = lax.broadcasted_iota(jnp.int32, (LANES, width), 1)
-        block = jnp.where(row + col >= LANES - 1, block * (back_inv * inv[:, start:]), 0.0)
-        block = pltpu.roll(block, width - LANES + 1, axis=1, stride=1, stride_axis=0)
-        part = jnp.sum(block, axis=0, keepdims=True)
+        block = dot_t(all_ref[start : start + LANES], all_ref[start:])
+        block = block * (inv_col[start : start + LANES, 0:1] * inv[:, start:])
+        corner = jnp.where(col >= row, block[:, :LANES], 0.0)
+        block = corner if width == LANES else jnp.concatenate([corner, block[:, LANES:]], axis=1)
+        part = block[:group]
+        for first in range(group, LANES, group):
+            part = part + pltpu.roll(block[first : first + group], width - first, axis=1)
         if width < FRAMES:
-            part = jnp.concatenate([part, jnp.zeros((1, start), F32)], axis=1)
-        lags = lags + part
+            part = jnp.concatenate([part, jnp.zeros((group, start), F32)], axis=1)
+        along = along + part
+    place = lax.broadcasted_iota(jnp.int32, (group, FRAMES), 0)
+    for step in (1, 2, 4):
+        along = jnp.where((place & step) > 0, pltpu.roll(along, FRAMES - step, axis=1), along)
+    lags = jnp.sum(along, axis=0, keepdims=True)
     remaining = (FRAMES - lax.broadcasted_iota(jnp.int32, (1, FRAMES), 1)).astype(F32)
     lags = lags * usable / remaining
     tail = jnp.concatenate(
@@ -299,7 +305,7 @@
             lag_ref[c : c + 1, b * LANES : (b + 1) * LANES] = both[ROWS + b : ROWS + b + 1]
 
 
-def call(body, out_shape, n_in, scalars=0, scratch=(), flops=0, size=0, source=pltpu.VMEM, limit=32 << 20):
+def call(body, out_shape, n_in, scalars=0, scratch=(), flops=0, size=0, source=pltpu.VMEM):
     vmem = pl.BlockSpec(memory_space=pltpu.VMEM)
     given = pl.BlockSpec(memory_space=source)
     smem = pl.BlockSpec(memory_space=pltpu.SMEM)
@@ -310,7 +316,7 @@
         in_specs=[smem] * scalars + [given] * n_in,
         out_specs=(vmem,) * len(out_shape) if many else vmem,
         scratch_shapes=list(scratch),
-        compiler_params=pltpu.CompilerParams(vmem_limit_bytes=limit),
+        compiler_params=pltpu.CompilerParams(vmem_limit_bytes=32 << 20),
         cost_estimate=pl.CostEstimate(flops=flops, bytes_accessed=size, transcendentals=0),
     )
 
@@ -335,14 +341,18 @@
         flops=2 * CYCLES * SUB * CAP * PIX,
         size=1 << 20,
         source=pltpu.HBM,
-        limit=63 << 20,
     )(
         turn,
-        labels.reshape(1, PIX),
-        pixel_mask.reshape(1, PIX),
-        dark_level.reshape(1, PIX),
-        flat_field.reshape(1, PIX),
-        counts,
+        *(
+            pltpu.with_memory_space_constraint(x, pltpu.HBM)
+            for x in (
+                labels.reshape(1, PIX),
+                pixel_mask.reshape(1, PIX),
+                dark_level.reshape(1, PIX),
+                flat_field.reshape(1, PIX),
+                counts,
+            )
+        ),
     )
     arrived = lax.all_to_all(
         payload.reshape(4 * CYCLES, MESSAGE // 2, 2, LANES),

time: 74 us -> 72.6 us (0.981)
  Pallas kernels: 6.83 us -> 5.6 us
    pallas_call x1, Pallas kernels: 4.05 us -> 3.05 us  [per_device(): call(slot_kernel, jax.ShapeDtypeStruct((4 * CYCLES * MESSAGE, LANES), BF1...]
where the time goes in v7:
time: 72.6 us; the launch traced here: 72.3 us
  blocking collectives  59.2 us (82%)
  Pallas kernels  5.6 us (8%)
  starting transfers between devices  5.25 us (7%)
  waiting for transfers between devices  1.52 us (2%)
    all_to_all x1, blocking collectives, per_device(): lax.all_to_all(payload.reshape(4 * CYCLES, MESSAGE // 2, 2, LANES), ('pix...  44.5 us
    all_to_all x1, blocking collectives, per_device(): gets = lax.all_to_all(sends, 'trow', 0, 0, tiled=True)  14.7 us
    ppermute x1, starting transfers between devices, per_device(): beside = lax.ppermute(packed, 'core', [(0, 1), (1, 0)])  5.25 us
    pallas_call x1, Pallas kernels, per_device(): call(slot_kernel, jax.ShapeDtypeStruct((4 * CYCLES * MESSAGE, LANES), BF1...  3.05 us
    pallas_call x1, Pallas kernels, per_device(): call(gram_kernel, jax.ShapeDtypeStruct((N_TROW, ROWS + 8, LANES), F32), 2...  1.53 us
    ppermute x1, waiting for transfers between devices, per_device(): beside = lax.ppermute(packed, 'core', [(0, 1), (1, 0)])  1.52 us
  transfers between devices with their start and end apart: 1, of which 1 were waited for; matrix products, arithmetic and copies ran while one was open for 0% of the time, Pallas kernels for 0%

profile of v7, /device:TPU:1, one launch (start us, length us, event | category | flops | bytes accessed | tf_op | source)
XLA Modules:
  0.0 72.3 jit_solution(17852780666058659334)
XLA Ops:
  0.6 3.1 %shard_map.68 = bf16[2560,128]{1,0:T(8,128)(2,1)S(1)} custom-call(s32[1]{0:T(128)} %bitcast.2.turn_ref, s32[1,4096]{1,0:T(1,128)} %bitcast.11, s32[1,4096]{1,0:T(1,128)} %bitcast.12, f32[1,4096]{1,0:T(1,128)} %bitcast.13, f32[1,4096]{1,0:T(1,128)} %bitcast.14, s32[16,4096]{1,0:T(8,128)} %counts_hbm.1), custom_call_target="tpu_custom_call" | custom-call | flops 1073741824 | bytes 1048576 | tf_op jit(solution)/shard_map/pallas_call | solution.py:328
  3.7 44.5 %all_to_all.10 = bf16[256,5,2,128]{3,2,1,0:T(2,128)(2,1)S(1)} all-to-all(bf16[256,5,2,128]{3,2,1,0:T(2,128)(2,1)S(1)} %bitcast.10), channel_id=1, replica_groups=mesh['pixel'=16,'trow'=8,'z'=2,'core'=2] {'pixel','trow','z'}, dimensions={0} | all-to-all | bytes 1310720 | tf_op jit(solution)/shard_map/all_to_all | solution.py:357
  48.2 0.3 shard_map.69.x0_ref
  48.6 5.2 %collective-permute-start = (bf16[2064,128]{1,0:T(8,128)(2,1)S(1)}, bf16[2064,128]{1,0:T(8,128)(2,1)S(1)}, u32[]{:S(2)}, u32[]{:S(2)}) collective-permute-start(bf16[2064,128]{1,0:T(8,128)(2,1)S(1)} %shard_map.69.x0_ref), channel_id=1, source_target_pairs={{0,1},{1,0},{2,3},{3,2},{4,5},{5,4},{6,7},{7,6},{8,9},{9,8},{10,11... | collective-permute-start | bytes 1585160 | tf_op jit(solution)/shard_map/ppermute | solution.py:371
  53.8 1.5 %collective-permute-done.x1_ref = bf16[2064,128]{1,0:T(8,128)(2,1)S(1)} collective-permute-done((bf16[2064,128]{1,0:T(8,128)(2,1)S(1)}, bf16[2064,128]{1,0:T(8,128)(2,1)S(1)}, u32[]{:S(2)}, u32[]{:S(2)}) %collective-permute-start) | collective-permute-done | bytes 528416 | tf_op jit(solution)/shard_map/ppermute | solution.py:371
  55.3 1.5 %shard_map.70 = f32[8,72,128]{2,1,0:T(8,128)S(1)} custom-call(s32[1]{0:T(128)} %bitcast.core_ref, s32[1]{0:T(128)} %bitcast.1.z_ref, bf16[2064,128]{1,0:T(8,128)(2,1)S(1)} %shard_map.69.x0_ref, bf16[2064,128]{1,0:T(8,128)(2,1)S(1)} %collective-permute-done.x1_ref), custom_call_target="tpu_custom_call" | custom-call | flops 536870912 | bytes 1572864 | tf_op jit(solution)/shard_map/pallas_call | solution.py:373
  56.9 14.7 %all_to_all.11.in_ref = f32[8,72,128]{2,1,0:T(8,128)S(1)} all-to-all(f32[8,72,128]{2,1,0:T(8,128)S(1)} %shard_map.70), channel_id=1, replica_groups=mesh['pixel'=16,'trow'=8,'z'=2,'core'=2] {'trow'}, dimensions={0} | all-to-all | bytes 589824 | tf_op jit(solution)/shard_map/all_to_all | solution.py:382
  71.6 0.7 shard_map.71
Async XLA Ops:
  48.6 6.8 %collective-permute-start = (bf16[2064,128]{1,0:T(8,128)(2,1)S(1)}, bf16[2064,128]{1,0:T(8,128)(2,1)S(1)}, u32[]{:S(2)}, u32[]{:S(2)}) collective-permute-start(bf16[2064,128]{1,0:T(8,128)(2,1)S(1)} %shard_map.69.x0_ref), channel_id=1, source_target_pairs={{0,1},{1,0},{2,3},{3,2},{4,5},{5,4},{6,7},{7,6},{8,9},{9,8},{10,11... | collective-permute-start | bytes 1585160 | tf_op jit(solution)/shard_map/ppermute | solution.py:371

commit v8 on v7

--- a/solution.py
+++ b/solution.py
@@ -23,9 +23,12 @@
 ROWS = N_TCOL * SUB
 LANES = 128
 MESSAGE = 10
+BLOCK = N_PIXEL * MESSAGE
+FOUR = 4
 FILLED = CYCLES // 2 * SUB
 CHUNK = 512
 RANK = 128
+Y_ORDER = [4, 3, 5, 2, 6, 1, 7, 0]
 F32 = jnp.float32
 BF16 = jnp.bfloat16
 
@@ -36,6 +39,10 @@
 
 def dot_n(a, b):
     return jnp.dot(a, b, preferred_element_type=F32)
+
+
+def block_of(y, z):
+    return ((N_TROW - 1 - y) * N_Z + N_Z - 1 - z) * BLOCK
 
 
 def three_parts(x):
@@ -93,7 +100,8 @@
     rank = jnp.concatenate(ranks, axis=1).astype(jnp.int32)
     slot = ((rank + turn * HALF) & (CAP - 1)) + (labels & 1) * CAP
     slot16 = slot.astype(F32).astype(BF16)
-    pair16 = (labels >> 1).astype(F32).astype(BF16)
+    pair = ((labels >> 1) & 1) * N_PIXEL + N_PIXEL - 1 - labels // OWNED
+    pair16 = pair.astype(F32).astype(BF16)
 
     get_dark.wait()
     get_flat.wait()
@@ -146,66 +154,69 @@
         for b in range(2)
     ]
     data = (lax.broadcasted_iota(jnp.int32, shape, 2) >= HALF) == (turn == 1)
-    row = lax.broadcasted_iota(jnp.int32, shape, 1)
+    row = lax.broadcasted_iota(jnp.int32, (FOUR, SUB // 2, LANES), 1)
     slots = slots[:FILLED].reshape(CYCLES // 2, SUB, 2 * CAP)
-    tiles = []
     for b in range(2):
         early = slots[:, : SUB // 2, b * CAP : (b + 1) * CAP]
         late = slots[:, SUB // 2 :, b * CAP : (b + 1) * CAP]
-        tiles.append(jnp.where(data, early, pltpu.roll(late, HALF, axis=2)))
-        tiles.append(jnp.where(data, pltpu.roll(early, HALF, axis=2), late))
-    groups = []
-    for b in range(2):
-        extra, (lower, upper) = extras[b], tiles[2 * b : 2 * b + 2]
-        second, third, fourth = (
-            pltpu.roll(x, 2 * m, axis=1) for m, x in ((1, lower), (2, upper), (3, upper))
-        )
-        groups += [
-            lower,
-            jnp.where(row < 2, extra, second),
-            jnp.where(row < 2, second, jnp.where(row < 4, extra, third)),
-            jnp.where(row < 4, third, jnp.where(row < 6, extra, fourth)),
-            jnp.where(row < 6, fourth, extra),
-        ]
-    out_ref[...] = (
-        jnp.concatenate(groups, axis=1).reshape(4 * CYCLES * MESSAGE, LANES).astype(BF16)
-    )
+        lower = jnp.where(data, early, pltpu.roll(late, HALF, axis=2))
+        upper = jnp.where(data, pltpu.roll(early, HALF, axis=2), late)
+        for high in range(2):
+            mine = slice(high * N_PIXEL, (high + 1) * N_PIXEL)
+            extra = extras[b][mine].reshape(FOUR, FOUR, SUB // 2, LANES)
+            for half, tile in enumerate((lower, upper)):
+                tile = tile[mine].reshape(FOUR, FOUR, SUB // 2, LANES)
+                first = tile[:, 0]
+                second, third, fourth = (pltpu.roll(tile[:, m], 2 * m, axis=1) for m in (1, 2, 3))
+                groups = [
+                    first,
+                    jnp.where(row < 2, extra[:, 0], second),
+                    jnp.where(row < 2, second, jnp.where(row < 4, extra[:, 1], third)),
+                    jnp.where(row < 4, third, jnp.where(row < 6, extra[:, 2], fourth)),
+                    jnp.where(row < 6, fourth, extra[:, 3]),
+                ]
+                block = jnp.concatenate(groups, axis=1).reshape(BLOCK, LANES).astype(BF16)
+                y = (high * 2 + b) * 2 + half
+                for z in range(N_Z):
+                    at = block_of(y, z)
+                    out_ref[at : at + BLOCK] = block
 
 
 def pack_kernel(in_ref, out_ref):
-    per_shard = N_TROW * N_Z * MESSAGE
-    shape = (N_TROW * N_Z, SUB // 2, LANES)
-    low = lax.broadcasted_iota(jnp.int32, shape, 2) < HALF
+    low = lax.broadcasted_iota(jnp.int32, (PAIRS, SUB // 2, LANES), 2) < HALF
     row = lax.broadcasted_iota(jnp.int32, (SUB // 2, LANES), 0)
     lane = lax.broadcasted_iota(jnp.int32, (SUB // 2, LANES), 1)
-    total = jnp.zeros((per_shard, LANES), F32)
-    for pair in range(PAIRS):
-        halves = []
-        for shard in (2 * pair, 2 * pair + 1):
-            rows = in_ref[shard * per_shard : (shard + 1) * per_shard].astype(F32)
-            total = total + rows
-            group = [rows[8 * i : 8 * i + 8] for i in range(per_shard // 8)]
+    totals = []
+    for j in range(N_TROW):
+        for z in range(N_Z):
+            at = block_of(j, z)
+            rows = in_ref[at : at + BLOCK].astype(F32)
             tiles = []
-            for first in range(0, len(group), 5):
-                g = group[first : first + 5]
+            total = jnp.zeros((FOUR * MESSAGE, LANES), F32)
+            for first in range(0, BLOCK, FOUR * MESSAGE):
+                part = rows[first : first + FOUR * MESSAGE]
+                total = total + part
+                g = [part[8 * i : 8 * i + 8] for i in range(5)]
                 tiles.append(g[0])
                 tiles.append(pltpu.roll(jnp.where(row < 2, g[2], g[1]), 6, axis=0))
                 tiles.append(pltpu.roll(jnp.where(row < 4, g[3], g[2]), 4, axis=0))
                 tiles.append(pltpu.roll(jnp.where(row < 6, g[4], g[3]), 2, axis=0))
-            halves.append(jnp.concatenate(tiles, axis=0).reshape(shape))
-        even, odd = halves
-        early = jnp.where(low, even, odd)
-        late = pltpu.roll(jnp.where(low, odd, even), HALF, axis=2)
-        out_ref[pair * SEEN : (pair + 1) * SEEN] = (
-            jnp.concatenate([early, late], axis=1).reshape(SEEN, LANES).astype(BF16)
-        )
+            totals.append(sum(total[i : i + 1] for i in range(8, FOUR * MESSAGE, MESSAGE)))
+            tiles = tiles[::-1]
+            even = jnp.concatenate(tiles[0::2], axis=0).reshape(low.shape)
+            odd = jnp.concatenate(tiles[1::2], axis=0).reshape(low.shape)
+            early = jnp.where(low, even, odd)
+            late = pltpu.roll(jnp.where(low, odd, even), HALF, axis=2)
+            both = jnp.concatenate([early, late], axis=1).astype(BF16)
+            for pair in range(PAIRS):
+                to = pair * SEEN + (j * N_Z + z) * SUB
+                out_ref[to : to + SUB] = both[pair]
     tails = []
     for half in range(SEEN // LANES):
         sums = jnp.zeros((SUB // 2, LANES), F32)
         usable = jnp.zeros((SUB // 2, LANES), F32)
         for i in range(LANES // SUB):
-            at = (half * LANES // SUB + i) * MESSAGE + SUB // 2
-            extra = jnp.broadcast_to(total[at : at + 1], (SUB // 2, LANES))
+            extra = jnp.broadcast_to(totals[half * LANES // SUB + i], (SUB // 2, LANES))
             added = extra + pltpu.roll(extra, LANES - SUB, axis=1)
             added = added + pltpu.roll(extra, LANES - 2 * SUB, axis=1)
             here = lane // SUB == i
@@ -293,13 +304,14 @@
             own_ref[j * SUB : (j + 1) * SUB, pair * LANES : (pair + 1) * LANES] = x0_ref[at]
     tile = dot_t(all_ref[...], own_ref[...]) * (inv_col * own_inv)
     for i in range(N_TROW):
-        out_ref[i, :ROWS] = tile[i * ROWS : (i + 1) * ROWS]
-        out_ref[i, ROWS:] = tail
+        at = Y_ORDER.index(i)
+        out_ref[at, :ROWS] = tile[i * ROWS : (i + 1) * ROWS]
+        out_ref[at, ROWS:] = tail
 
 
 def join_kernel(in_ref, tile_ref, lag_ref):
     for c in range(OWNED):
-        both = in_ref[2 * c] + in_ref[2 * c + 1]
+        both = in_ref[Y_ORDER.index(2 * c)] + in_ref[Y_ORDER.index(2 * c + 1)]
         tile_ref[c] = both[:ROWS]
         for b in range(FRAMES // LANES):
             lag_ref[c : c + 1, b * LANES : (b + 1) * LANES] = both[ROWS + b : ROWS + b + 1]
@@ -354,12 +366,19 @@
             )
         ),
     )
+    order = [
+        (p * N_TROW + y) * N_Z + z
+        for y in range(N_TROW)[::-1]
+        for z in range(N_Z)[::-1]
+        for p in range(N_PIXEL)[::-1]
+    ]
     arrived = lax.all_to_all(
         payload.reshape(4 * CYCLES, MESSAGE // 2, 2, LANES),
         ("pixel", "trow", "z"),
         0,
         0,
         tiled=True,
+        axis_index_groups=[order],
     )
     packed = call(
         pack_kernel,
@@ -379,7 +398,9 @@
         flops=2 * FRAMES * FRAMES * depth,
         size=3 << 19,
     )(core, z, packed, beside)
-    gets = lax.all_to_all(sends, "trow", 0, 0, tiled=True)
+    gets = lax.all_to_all(
+        sends, "trow", 0, 0, tiled=True, axis_index_groups=[Y_ORDER]
+    )
     return call(
         join_kernel,
         (

time: 72.6 us -> 66 us (0.909)
  blocking collectives: 59.2 us -> 53.2 us
    all_to_all x1, blocking collectives: 44.5 us -> 39.3 us  [per_device(): lax.all_to_all(payload.reshape(4 * CYCLES, MESSAGE // 2, 2, LANES), ('pix...]
    all_to_all x1, blocking collectives: 14.7 us -> 13.8 us  [per_device(): lax.all_to_all(sends, 'trow', 0, 0, tiled=True, axis_index_groups=[Y_ORDER])]
where the time goes in v8:
time: 66 us; the launch traced here: 65.7 us
  blocking collectives  53.2 us (81%)
  Pallas kernels  5.56 us (8%)
  starting transfers between devices  4.84 us (7%)
  waiting for transfers between devices  1.52 us (2%)
  between operations  0.67 us (1%)
    all_to_all x1, blocking collectives, per_device(): lax.all_to_all(payload.reshape(4 * CYCLES, MESSAGE // 2, 2, LANES), ('pix...  39.3 us
    all_to_all x1, blocking collectives, per_device(): lax.all_to_all(sends, 'trow', 0, 0, tiled=True, axis_index_groups=[Y_ORDER])  13.8 us
    ppermute x1, starting transfers between devices, per_device(): beside = lax.ppermute(packed, 'core', [(0, 1), (1, 0)])  4.84 us
    pallas_call x1, Pallas kernels, per_device(): call(slot_kernel, jax.ShapeDtypeStruct((4 * CYCLES * MESSAGE, LANES), BF1...  3 us
    pallas_call x1, Pallas kernels, per_device(): call(gram_kernel, jax.ShapeDtypeStruct((N_TROW, ROWS + 8, LANES), F32), 2...  1.53 us
    ppermute x1, waiting for transfers between devices, per_device(): beside = lax.ppermute(packed, 'core', [(0, 1), (1, 0)])  1.52 us
  transfers between devices with their start and end apart: 1, of which 1 were waited for; matrix products, arithmetic and copies ran while one was open for 0% of the time, Pallas kernels for 0%

profile of v8, /device:TPU:1, one launch (start us, length us, event | category | flops | bytes accessed | tf_op | source)
XLA Modules:
  0.0 65.7 jit_solution(16707048828780463718)
XLA Ops:
  0.6 3.0 %shard_map.68 = bf16[2560,128]{1,0:T(8,128)(2,1)S(1)} custom-call(s32[1]{0:T(128)} %bitcast.2.turn_ref, s32[1,4096]{1,0:T(1,128)} %bitcast.11, s32[1,4096]{1,0:T(1,128)} %bitcast.12, f32[1,4096]{1,0:T(1,128)} %bitcast.13, f32[1,4096]{1,0:T(1,128)} %bitcast.14, s32[16,4096]{1,0:T(8,128)} %counts_hbm.1), custom_call_target="tpu_custom_call" | custom-call | flops 1073741824 | bytes 1048576 | tf_op jit(solution)/shard_map/pallas_call | solution.py:340
  3.6 39.3 %all_to_all.10 = bf16[256,5,2,128]{3,2,1,0:T(2,128)(2,1)S(1)} all-to-all(bf16[256,5,2,128]{3,2,1,0:T(2,128)(2,1)S(1)} %bitcast.10), channel_id=1, replica_groups={{510,478,446,414,382,350,318,286,254,222,190,158,126,94,62,30,508,476,4..., dimensions={0} | all-to-all | bytes 1310720 | tf_op jit(solution)/shard_map/all_to_all | solution.py:375
  43.0 0.3 shard_map.69.x0_ref
  43.3 4.8 %collective-permute-start = (bf16[2064,128]{1,0:T(8,128)(2,1)S(1)}, bf16[2064,128]{1,0:T(8,128)(2,1)S(1)}, u32[]{:S(2)}, u32[]{:S(2)}) collective-permute-start(bf16[2064,128]{1,0:T(8,128)(2,1)S(1)} %shard_map.69.x0_ref), channel_id=1, source_target_pairs={{0,1},{1,0},{2,3},{3,2},{4,5},{5,4},{6,7},{7,6},{8,9},{9,8},{10,11... | collective-permute-start | bytes 1585160 | tf_op jit(solution)/shard_map/ppermute | solution.py:390
  48.2 1.5 %collective-permute-done.x1_ref = bf16[2064,128]{1,0:T(8,128)(2,1)S(1)} collective-permute-done((bf16[2064,128]{1,0:T(8,128)(2,1)S(1)}, bf16[2064,128]{1,0:T(8,128)(2,1)S(1)}, u32[]{:S(2)}, u32[]{:S(2)}) %collective-permute-start) | collective-permute-done | bytes 528416 | tf_op jit(solution)/shard_map/ppermute | solution.py:390
  49.7 1.5 %shard_map.70 = f32[8,72,128]{2,1,0:T(8,128)S(1)} custom-call(s32[1]{0:T(128)} %bitcast.core_ref, s32[1]{0:T(128)} %bitcast.1.z_ref, bf16[2064,128]{1,0:T(8,128)(2,1)S(1)} %shard_map.69.x0_ref, bf16[2064,128]{1,0:T(8,128)(2,1)S(1)} %collective-permute-done.x1_ref), custom_call_target="tpu_custom_call" | custom-call | flops 536870912 | bytes 1572864 | tf_op jit(solution)/shard_map/pallas_call | solution.py:392
  51.2 13.8 %all_to_all.11.in_ref = f32[8,72,128]{2,1,0:T(8,128)S(1)} all-to-all(f32[8,72,128]{2,1,0:T(8,128)S(1)} %shard_map.70), channel_id=1, replica_groups={{16,12,20,8,24,4,28,0},{17,13,21,9,25,5,29,1},{18,14,22,10,26,6,30,2},{..., dimensions={0} | all-to-all | bytes 589824 | tf_op jit(solution)/shard_map/all_to_all | solution.py:401
  65.1 0.7 %shard_map.71 = (f32[4,64,128]{2,1,0:T(8,128)}, f32[4,512]{1,0:T(4,128)}) custom-call(f32[8,72,128]{2,1,0:T(8,128)S(1)} %all_to_all.11.in_ref), custom_call_target="tpu_custom_call" | custom-call | flops 65536 | bytes 524288 | tf_op jit(solution)/shard_map/pallas_call | solution.py:404
Async XLA Ops:
  43.3 6.4 %collective-permute-start = (bf16[2064,128]{1,0:T(8,128)(2,1)S(1)}, bf16[2064,128]{1,0:T(8,128)(2,1)S(1)}, u32[]{:S(2)}, u32[]{:S(2)}) collective-permute-start(bf16[2064,128]{1,0:T(8,128)(2,1)S(1)} %shard_map.69.x0_ref), channel_id=1, source_target_pairs={{0,1},{1,0},{2,3},{3,2},{4,5},{5,4},{6,7},{7,6},{8,9},{9,8},{10,11... | collective-permute-start | bytes 1585160 | tf_op jit(solution)/shard_map/ppermute | solution.py:390

commit v9 on v6

--- a/solution.py
+++ b/solution.py
@@ -22,7 +22,8 @@
 MESSAGE = 10
 FILLED = CYCLES // 2 * SUB
 CHUNK = 512
-RANK = 256
+RANK = 128
+Y_ORDER = [4, 3, 5, 2, 6, 1, 7, 0]
 F32 = jnp.float32
 BF16 = jnp.bfloat16
 
@@ -88,9 +89,10 @@
         ranks.append(jnp.sum(member * place, axis=0, keepdims=True))
         offset = offset + counted[:, RANK:]
     rank = jnp.concatenate(ranks, axis=1).astype(jnp.int32)
-    slot = ((rank + turn * HALF) & (CAP - 1)) + (labels & 1) * CAP
+    back = CYCLES - 1 - labels
+    slot = ((rank + turn * HALF) & (CAP - 1)) + (back & 1) * CAP
     slot16 = slot.astype(F32).astype(BF16)
-    pair16 = (labels >> 1).astype(F32).astype(BF16)
+    pair16 = (back >> 1).astype(F32).astype(BF16)
 
     get_dark.wait()
     get_flat.wait()
@@ -149,8 +151,8 @@
     for b in range(2):
         early = slots[:, : SUB // 2, b * CAP : (b + 1) * CAP]
         late = slots[:, SUB // 2 :, b * CAP : (b + 1) * CAP]
+        tiles.append(jnp.where(data, pltpu.roll(early, HALF, axis=2), late))
         tiles.append(jnp.where(data, early, pltpu.roll(late, HALF, axis=2)))
-        tiles.append(jnp.where(data, pltpu.roll(early, HALF, axis=2), late))
     second, third, fourth = (pltpu.roll(tiles[m], 2 * m, axis=1) for m in (1, 2, 3))
     groups = [
         tiles[0],
@@ -173,7 +175,7 @@
     total = jnp.zeros((per_shard, LANES), F32)
     for pair in range(PAIRS):
         halves = []
-        for shard in (2 * pair, 2 * pair + 1):
+        for shard in (N_PIXEL - 1 - 2 * pair, N_PIXEL - 2 - 2 * pair):
             rows = in_ref[shard * per_shard : (shard + 1) * per_shard].astype(F32)
             total = total + rows
             group = [rows[8 * i : 8 * i + 8] for i in range(per_shard // 8)]
@@ -184,7 +186,7 @@
                 tiles.append(pltpu.roll(jnp.where(row < 2, g[2], g[1]), 6, axis=0))
                 tiles.append(pltpu.roll(jnp.where(row < 4, g[3], g[2]), 4, axis=0))
                 tiles.append(pltpu.roll(jnp.where(row < 6, g[4], g[3]), 2, axis=0))
-            halves.append(jnp.concatenate(tiles, axis=0).reshape(shape))
+            halves.append(jnp.concatenate(tiles[::-1], axis=0).reshape(shape))
         even, odd = halves
         early = jnp.where(low, even, odd)
         late = pltpu.roll(jnp.where(low, odd, even), HALF, axis=2)
@@ -194,7 +196,7 @@
     sums = jnp.zeros((SUB // 2, LANES), F32)
     usable = jnp.zeros((SUB // 2, LANES), F32)
     for j in range(N_TROW):
-        at = j * MESSAGE + SUB // 2
+        at = (N_TROW - 1 - j) * MESSAGE + SUB // 2
         extra = jnp.broadcast_to(total[at : at + 1], (SUB // 2, LANES))
         added = extra + pltpu.roll(extra, LANES - SUB, axis=1)
         added = added + pltpu.roll(extra, LANES - 2 * SUB, axis=1)
@@ -263,15 +265,16 @@
     lags = lags * usable / remaining
 
     for i in range(N_TROW):
-        out_ref[i, :ROWS] = tile[i * ROWS : (i + 1) * ROWS]
+        at = Y_ORDER.index(i)
+        out_ref[at, :ROWS] = tile[i * ROWS : (i + 1) * ROWS]
         for b in range(FRAMES // LANES):
-            out_ref[i, ROWS + b : ROWS + b + 1] = lags[:, b * LANES : (b + 1) * LANES]
-        out_ref[i, ROWS + 4 :] = jnp.zeros((4, LANES), F32)
+            out_ref[at, ROWS + b : ROWS + b + 1] = lags[:, b * LANES : (b + 1) * LANES]
+        out_ref[at, ROWS + 4 :] = jnp.zeros((4, LANES), F32)
 
 
 def join_kernel(in_ref, tile_ref, lag_ref):
     for c in range(OWNED):
-        both = in_ref[2 * c] + in_ref[2 * c + 1]
+        both = in_ref[Y_ORDER.index(2 * c)] + in_ref[Y_ORDER.index(2 * c + 1)]
         tile_ref[c] = both[:ROWS]
         for b in range(FRAMES // LANES):
             lag_ref[c : c + 1, b * LANES : (b + 1) * LANES] = both[ROWS + b : ROWS + b + 1]
@@ -326,7 +329,12 @@
         ),
     )
     arrived = lax.all_to_all(
-        payload.reshape(2 * CYCLES, MESSAGE // 2, 2, LANES), ("pixel", "trow"), 0, 0, tiled=True
+        payload.reshape(2 * CYCLES, MESSAGE // 2, 2, LANES),
+        ("pixel", "trow"),
+        0,
+        0,
+        tiled=True,
+        axis_index_groups=[list(range(N_PIXEL * N_TROW))[::-1]],
     )
     packed = call(
         pack_kernel,
@@ -348,7 +356,7 @@
         flops=2 * FRAMES * FRAMES * depth,
         size=3 << 19,
     )(me, packed, beside, across, corner)
-    gets = lax.all_to_all(sends, "trow", 0, 0, tiled=True)
+    gets = lax.all_to_all(sends, "trow", 0, 0, tiled=True, axis_index_groups=[Y_ORDER])
     return call(
         join_kernel,
         (

time: 73.1 us -> 65.9 us (0.902)
  blocking collectives: 52.5 us -> 45.3 us
    all_to_all x1, blocking collectives: 36.6 us -> 30.2 us  [per_device(): lax.all_to_all(payload.reshape(2 * CYCLES, MESSAGE // 2, 2, LANES), ('pix...]
    all_to_all x1, blocking collectives: 15.9 us -> 15.1 us  [per_device(): lax.all_to_all(sends, 'trow', 0, 0, tiled=True, axis_index_groups=[Y_ORDER])]
where the time goes in v9:
time: 65.9 us; the launch traced here: 65.6 us
  blocking collectives  45.3 us (69%)
  starting transfers between devices  12.8 us (19%)
  Pallas kernels  5.62 us (9%)
  waiting for transfers between devices  1.14 us (2%)
  between operations  0.7 us (1%)
    all_to_all x1, blocking collectives, per_device(): lax.all_to_all(payload.reshape(2 * CYCLES, MESSAGE // 2, 2, LANES), ('pix...  30.2 us
    all_to_all x1, blocking collectives, per_device(): lax.all_to_all(sends, 'trow', 0, 0, tiled=True, axis_index_groups=[Y_ORDER])  15.1 us
    ppermute x1, starting transfers between devices, per_device(): corner = lax.ppermute(across, 'tcol', [(k, k ^ 1) for k in range(N_TCOL)])  4.93 us
    ppermute x1, starting transfers between devices, per_device(): beside = lax.ppermute(packed, 'tcol', [(k, k ^ 1) for k in range(N_TCOL)])  4.81 us
    ppermute x1, starting transfers between devices, per_device(): across = lax.ppermute(packed, 'tcol', [(k, k ^ 2) for k in range(N_TCOL)])  3.1 us
    pallas_call x1, Pallas kernels, per_device(): call(slot_kernel, jax.ShapeDtypeStruct((2 * CYCLES * MESSAGE, LANES), BF1...  2.99 us
    pallas_call x1, Pallas kernels, per_device(): call(gram_kernel, jax.ShapeDtypeStruct((N_TROW, ROWS + 8, LANES), F32), 4...  1.75 us
  transfers between devices with their start and end apart: 3, of which 1 were waited for; matrix products, arithmetic and copies ran while one was open for 0% of the time, Pallas kernels for 0%

profile of v9, /device:TPU:1, one launch (start us, length us, event | category | flops | bytes accessed | tf_op | source)
XLA Modules:
  0.0 65.6 jit_solution(14127947838473593371)
XLA Ops:
  0.6 3.0 %shard_map.68 = bf16[1280,128]{1,0:T(8,128)(2,1)S(1)} custom-call(s32[1]{0:T(128)} %bitcast.1.turn_ref, s32[1,4096]{1,0:T(1,128)} %bitcast.10, s32[1,4096]{1,0:T(1,128)} %bitcast.11, f32[1,4096]{1,0:T(1,128)} %bitcast.12, f32[1,4096]{1,0:T(1,128)} %bitcast.13, s32[16,4096]{1,0:T(8,128)} %counts_hbm.1), custom_call_target="tpu_custom_call" | custom-call | flops 1073741824 | bytes 1048576 | tf_op jit(solution)/shard_map/pallas_call | solution.py:302
  3.6 30.2 %all_to_all.10 = bf16[128,5,2,128]{3,2,1,0:T(2,128)(2,1)S(1)} all-to-all(bf16[128,5,2,128]{3,2,1,0:T(2,128)(2,1)S(1)} %bitcast.9), channel_id=1, replica_groups={{508,504,500,496,492,488,484,480,476,472,468,464,460,456,452,448,444,44..., dimensions={0} | all-to-all | bytes 655360 | tf_op jit(solution)/shard_map/all_to_all | solution.py:331
  33.8 0.2 shard_map.69.x0_ref
  34.0 3.1 %collective-permute-start.1 = (bf16[1040,128]{1,0:T(8,128)(2,1)S(1)}, bf16[1040,128]{1,0:T(8,128)(2,1)S(1)}, u32[]{:S(2)}, u32[]{:S(2)}) collective-permute-start(bf16[1040,128]{1,0:T(8,128)(2,1)S(1)} %shard_map.69.x0_ref), channel_id=1, source_target_pairs={{0,2},{1,3},{2,0},{3,1},{4,6},{5,7},{6,4},{7,5},{8,10},{9,11},{10,... | collective-permute-start | bytes 798728 | tf_op jit(solution)/shard_map/ppermute | solution.py:347
  37.1 4.8 %collective-permute-start = (bf16[1040,128]{1,0:T(8,128)(2,1)S(1)}, bf16[1040,128]{1,0:T(8,128)(2,1)S(1)}, u32[]{:S(2)}, u32[]{:S(2)}) collective-permute-start(bf16[1040,128]{1,0:T(8,128)(2,1)S(1)} %shard_map.69.x0_ref), channel_id=1, source_target_pairs={{0,1},{1,0},{2,3},{3,2},{4,5},{5,4},{6,7},{7,6},{8,9},{9,8},{10,11... | collective-permute-start | bytes 798728 | tf_op jit(solution)/shard_map/ppermute | solution.py:346
  42.0 0.0 collective-permute-done.1.x2_ref
  42.0 4.9 %collective-permute-start.2 = (bf16[1040,128]{1,0:T(8,128)(2,1)S(1)}, bf16[1040,128]{1,0:T(8,128)(2,1)S(1)}, u32[]{:S(2)}, u32[]{:S(2)}) collective-permute-start(bf16[1040,128]{1,0:T(8,128)(2,1)S(1)} %collective-permute-done.1.x2_ref), channel_id=1, source_target_pairs={{0,1},{1,0},{2,3},{3,2},{4,5},{5,4},{6,7},{7,6},{8,9},{9,8},{10,11... | collective-permute-start | bytes 798728 | tf_op jit(solution)/shard_map/ppermute | solution.py:348
  46.9 0.0 collective-permute-done.x1_ref
  46.9 1.1 %collective-permute-done.2.x3_ref = bf16[1040,128]{1,0:T(8,128)(2,1)S(1)} collective-permute-done((bf16[1040,128]{1,0:T(8,128)(2,1)S(1)}, bf16[1040,128]{1,0:T(8,128)(2,1)S(1)}, u32[]{:S(2)}, u32[]{:S(2)}) %collective-permute-start.2) | collective-permute-done | bytes 266272 | tf_op jit(solution)/shard_map/ppermute | solution.py:348
  48.1 1.8 %shard_map.70 = f32[8,72,128]{2,1,0:T(8,128)S(1)} custom-call(s32[1]{0:T(128)} %bitcast.me_ref, bf16[1040,128]{1,0:T(8,128)(2,1)S(1)} %shard_map.69.x0_ref, bf16[1040,128]{1,0:T(8,128)(2,1)S(1)} %collective-permute-done.x1_ref, bf16[1040,128]{1,0:T(8,128)(2,1)S(1)} %collective-permute-done.1.x2_ref, bf16[1040,128]{1,0:T(8,128)(2,1)S(1)} %collective-permute-done.2.x3_ref), custom_call_target="tpu_custom_call" | custom-call | flops 536870912 | bytes 1572864 | tf_op jit(solution)/shard_map/pallas_call | solution.py:350
  49.8 15.1 %all_to_all.11.in_ref = f32[8,72,128]{2,1,0:T(8,128)S(1)} all-to-all(f32[8,72,128]{2,1,0:T(8,128)S(1)} %shard_map.70), channel_id=1, replica_groups={{16,12,20,8,24,4,28,0},{17,13,21,9,25,5,29,1},{18,14,22,10,26,6,30,2},{..., dimensions={0} | all-to-all | bytes 589824 | tf_op jit(solution)/shard_map/all_to_all | solution.py:359
  64.9 0.7 %shard_map.71 = (f32[4,64,128]{2,1,0:T(8,128)}, f32[4,512]{1,0:T(4,128)}) custom-call(f32[8,72,128]{2,1,0:T(8,128)S(1)} %all_to_all.11.in_ref), custom_call_target="tpu_custom_call" | custom-call | flops 65536 | bytes 524288 | tf_op jit(solution)/shard_map/pallas_call | solution.py:360
Async XLA Ops:
  34.0 7.9 %collective-permute-start.1 = (bf16[1040,128]{1,0:T(8,128)(2,1)S(1)}, bf16[1040,128]{1,0:T(8,128)(2,1)S(1)}, u32[]{:S(2)}, u32[]{:S(2)}) collective-permute-start(bf16[1040,128]{1,0:T(8,128)(2,1)S(1)} %shard_map.69.x0_ref), channel_id=1, source_target_pairs={{0,2},{1,3},{2,0},{3,1},{4,6},{5,7},{6,4},{7,5},{8,10},{9,11},{10,... | collective-permute-start | bytes 798728 | tf_op jit(solution)/shard_map/ppermute | solution.py:347
  37.1 9.8 %collective-permute-start = (bf16[1040,128]{1,0:T(8,128)(2,1)S(1)}, bf16[1040,128]{1,0:T(8,128)(2,1)S(1)}, u32[]{:S(2)}, u32[]{:S(2)}) collective-permute-start(bf16[1040,128]{1,0:T(8,128)(2,1)S(1)} %shard_map.69.x0_ref), channel_id=1, source_target_pairs={{0,1},{1,0},{2,3},{3,2},{4,5},{5,4},{6,7},{7,6},{8,9},{9,8},{10,11... | collective-permute-start | bytes 798728 | tf_op jit(solution)/shard_map/ppermute | solution.py:346
  42.0 6.1 %collective-permute-start.2 = (bf16[1040,128]{1,0:T(8,128)(2,1)S(1)}, bf16[1040,128]{1,0:T(8,128)(2,1)S(1)}, u32[]{:S(2)}, u32[]{:S(2)}) collective-permute-start(bf16[1040,128]{1,0:T(8,128)(2,1)S(1)} %collective-permute-done.1.x2_ref), channel_id=1, source_target_pairs={{0,1},{1,0},{2,3},{3,2},{4,5},{5,4},{6,7},{7,6},{8,9},{9,8},{10,11... | collective-permute-start | bytes 798728 | tf_op jit(solution)/shard_map/ppermute | solution.py:348

commit v10 on v9

--- a/solution.py
+++ b/solution.py
@@ -24,6 +24,8 @@
 CHUNK = 512
 RANK = 128
 Y_ORDER = [4, 3, 5, 2, 6, 1, 7, 0]
+FIRST_PIXEL, FIRST_Y = 10, 5
+FIRST = FIRST_PIXEL * N_TROW + FIRST_Y
 F32 = jnp.float32
 BF16 = jnp.bfloat16
 
@@ -89,7 +91,7 @@
         ranks.append(jnp.sum(member * place, axis=0, keepdims=True))
         offset = offset + counted[:, RANK:]
     rank = jnp.concatenate(ranks, axis=1).astype(jnp.int32)
-    back = CYCLES - 1 - labels
+    back = labels ^ (FIRST // 2)
     slot = ((rank + turn * HALF) & (CAP - 1)) + (back & 1) * CAP
     slot16 = slot.astype(F32).astype(BF16)
     pair16 = (back >> 1).astype(F32).astype(BF16)
@@ -151,8 +153,9 @@
     for b in range(2):
         early = slots[:, : SUB // 2, b * CAP : (b + 1) * CAP]
         late = slots[:, SUB // 2 :, b * CAP : (b + 1) * CAP]
-        tiles.append(jnp.where(data, pltpu.roll(early, HALF, axis=2), late))
-        tiles.append(jnp.where(data, early, pltpu.roll(late, HALF, axis=2)))
+        lower = jnp.where(data, early, pltpu.roll(late, HALF, axis=2))
+        upper = jnp.where(data, pltpu.roll(early, HALF, axis=2), late)
+        tiles += [lower, upper] if FIRST % 2 == 0 else [upper, lower]
     second, third, fourth = (pltpu.roll(tiles[m], 2 * m, axis=1) for m in (1, 2, 3))
     groups = [
         tiles[0],
@@ -175,7 +178,7 @@
     total = jnp.zeros((per_shard, LANES), F32)
     for pair in range(PAIRS):
         halves = []
-        for shard in (N_PIXEL - 1 - 2 * pair, N_PIXEL - 2 - 2 * pair):
+        for shard in ((2 * pair) ^ FIRST_PIXEL, (2 * pair + 1) ^ FIRST_PIXEL):
             rows = in_ref[shard * per_shard : (shard + 1) * per_shard].astype(F32)
             total = total + rows
             group = [rows[8 * i : 8 * i + 8] for i in range(per_shard // 8)]
@@ -186,7 +189,8 @@
                 tiles.append(pltpu.roll(jnp.where(row < 2, g[2], g[1]), 6, axis=0))
                 tiles.append(pltpu.roll(jnp.where(row < 4, g[3], g[2]), 4, axis=0))
                 tiles.append(pltpu.roll(jnp.where(row < 6, g[4], g[3]), 2, axis=0))
-            halves.append(jnp.concatenate(tiles[::-1], axis=0).reshape(shape))
+            tiles = [tiles[j ^ FIRST_Y] for j in range(N_TROW)]
+            halves.append(jnp.concatenate(tiles, axis=0).reshape(shape))
         even, odd = halves
         early = jnp.where(low, even, odd)
         late = pltpu.roll(jnp.where(low, odd, even), HALF, axis=2)
@@ -196,7 +200,7 @@
     sums = jnp.zeros((SUB // 2, LANES), F32)
     usable = jnp.zeros((SUB // 2, LANES), F32)
     for j in range(N_TROW):
-        at = (N_TROW - 1 - j) * MESSAGE + SUB // 2
+        at = (j ^ FIRST_Y) * MESSAGE + SUB // 2
         extra = jnp.broadcast_to(total[at : at + 1], (SUB // 2, LANES))
         added = extra + pltpu.roll(extra, LANES - SUB, axis=1)
         added = added + pltpu.roll(extra, LANES - 2 * SUB, axis=1)
@@ -334,7 +338,7 @@
         0,
         0,
         tiled=True,
-        axis_index_groups=[list(range(N_PIXEL * N_TROW))[::-1]],
+        axis_index_groups=[[m ^ FIRST for m in range(N_PIXEL * N_TROW)]],
     )
     packed = call(
         pack_kernel,

time: 65.9 us -> 64.6 us (0.980)
  blocking collectives: 45.3 us -> 44.2 us
    all_to_all x1, blocking collectives: 15.1 us -> 14.1 us  [per_device(): lax.all_to_all(sends, 'trow', 0, 0, tiled=True, axis_index_groups=[Y_ORDER])]
  transfers between devices with their start and end apart: 3 -> 3, of which waited for: 1 -> 2; matrix products, arithmetic and copies ran while one was open for 0% -> 0% of each run, Pallas kernels for 0% -> 0%
where the time goes in v10:
time: 64.6 us; the launch traced here: 64.2 us
  blocking collectives  44.2 us (68%)
  starting transfers between devices  12.2 us (19%)
  Pallas kernels  5.63 us (9%)
  waiting for transfers between devices  1.52 us (2%)
  between operations  0.69 us (1%)
    all_to_all x1, blocking collectives, per_device(): lax.all_to_all(payload.reshape(2 * CYCLES, MESSAGE // 2, 2, LANES), ('pix...  30.1 us
    all_to_all x1, blocking collectives, per_device(): lax.all_to_all(sends, 'trow', 0, 0, tiled=True, axis_index_groups=[Y_ORDER])  14.1 us
    ppermute x1, starting transfers between devices, per_device(): corner = lax.ppermute(across, 'tcol', [(k, k ^ 1) for k in range(N_TCOL)])  4.86 us
    ppermute x1, starting transfers between devices, per_device(): beside = lax.ppermute(packed, 'tcol', [(k, k ^ 1) for k in range(N_TCOL)])  4.23 us
    ppermute x1, starting transfers between devices, per_device(): across = lax.ppermute(packed, 'tcol', [(k, k ^ 2) for k in range(N_TCOL)])  3.1 us
    pallas_call x1, Pallas kernels, per_device(): call(slot_kernel, jax.ShapeDtypeStruct((2 * CYCLES * MESSAGE, LANES), BF1...  2.99 us
    pallas_call x1, Pallas kernels, per_device(): call(gram_kernel, jax.ShapeDtypeStruct((N_TROW, ROWS + 8, LANES), F32), 4...  1.75 us
  transfers between devices with their start and end apart: 3, of which 2 were waited for; matrix products, arithmetic and copies ran while one was open for 0% of the time, Pallas kernels for 0%

profile of v10, /device:TPU:1, one launch (start us, length us, event | category | flops | bytes accessed | tf_op | source)
XLA Modules:
  0.0 64.2 jit_solution(1833809791027418549)
XLA Ops:
  0.6 3.0 %shard_map.68 = bf16[1280,128]{1,0:T(8,128)(2,1)S(1)} custom-call(s32[1]{0:T(128)} %bitcast.1.turn_ref, s32[1,4096]{1,0:T(1,128)} %bitcast.10, s32[1,4096]{1,0:T(1,128)} %bitcast.11, f32[1,4096]{1,0:T(1,128)} %bitcast.12, f32[1,4096]{1,0:T(1,128)} %bitcast.13, s32[16,4096]{1,0:T(8,128)} %counts_hbm.1), custom_call_target="tpu_custom_call" | custom-call | flops 1073741824 | bytes 1048576 | tf_op jit(solution)/shard_map/pallas_call | solution.py:306
  3.6 30.1 %all_to_all.10 = bf16[128,5,2,128]{3,2,1,0:T(2,128)(2,1)S(1)} all-to-all(bf16[128,5,2,128]{3,2,1,0:T(2,128)(2,1)S(1)} %bitcast.9), channel_id=1, replica_groups={{340,336,348,344,324,320,332,328,372,368,380,376,356,352,364,360,276,27..., dimensions={0} | all-to-all | bytes 655360 | tf_op jit(solution)/shard_map/all_to_all | solution.py:335
  33.7 0.2 shard_map.69.x0_ref
  33.9 3.1 %collective-permute-start.1 = (bf16[1040,128]{1,0:T(8,128)(2,1)S(1)}, bf16[1040,128]{1,0:T(8,128)(2,1)S(1)}, u32[]{:S(2)}, u32[]{:S(2)}) collective-permute-start(bf16[1040,128]{1,0:T(8,128)(2,1)S(1)} %shard_map.69.x0_ref), channel_id=1, source_target_pairs={{0,2},{1,3},{2,0},{3,1},{4,6},{5,7},{6,4},{7,5},{8,10},{9,11},{10,... | collective-permute-start | bytes 798728 | tf_op jit(solution)/shard_map/ppermute | solution.py:351
  37.0 4.2 %collective-permute-start = (bf16[1040,128]{1,0:T(8,128)(2,1)S(1)}, bf16[1040,128]{1,0:T(8,128)(2,1)S(1)}, u32[]{:S(2)}, u32[]{:S(2)}) collective-permute-start(bf16[1040,128]{1,0:T(8,128)(2,1)S(1)} %shard_map.69.x0_ref), channel_id=1, source_target_pairs={{0,1},{1,0},{2,3},{3,2},{4,5},{5,4},{6,7},{7,6},{8,9},{9,8},{10,11... | collective-permute-start | bytes 798728 | tf_op jit(solution)/shard_map/ppermute | solution.py:350
  41.3 0.4 collective-permute-done.1.x2_ref
  41.7 4.9 %collective-permute-start.2 = (bf16[1040,128]{1,0:T(8,128)(2,1)S(1)}, bf16[1040,128]{1,0:T(8,128)(2,1)S(1)}, u32[]{:S(2)}, u32[]{:S(2)}) collective-permute-start(bf16[1040,128]{1,0:T(8,128)(2,1)S(1)} %collective-permute-done.1.x2_ref), channel_id=1, source_target_pairs={{0,1},{1,0},{2,3},{3,2},{4,5},{5,4},{6,7},{7,6},{8,9},{9,8},{10,11... | collective-permute-start | bytes 798728 | tf_op jit(solution)/shard_map/ppermute | solution.py:352
  46.6 0.0 collective-permute-done.x1_ref
  46.6 1.1 %collective-permute-done.2.x3_ref = bf16[1040,128]{1,0:T(8,128)(2,1)S(1)} collective-permute-done((bf16[1040,128]{1,0:T(8,128)(2,1)S(1)}, bf16[1040,128]{1,0:T(8,128)(2,1)S(1)}, u32[]{:S(2)}, u32[]{:S(2)}) %collective-permute-start.2) | collective-permute-done | bytes 266272 | tf_op jit(solution)/shard_map/ppermute | solution.py:352
  47.7 1.8 %shard_map.70 = f32[8,72,128]{2,1,0:T(8,128)S(1)} custom-call(s32[1]{0:T(128)} %bitcast.me_ref, bf16[1040,128]{1,0:T(8,128)(2,1)S(1)} %shard_map.69.x0_ref, bf16[1040,128]{1,0:T(8,128)(2,1)S(1)} %collective-permute-done.x1_ref, bf16[1040,128]{1,0:T(8,128)(2,1)S(1)} %collective-permute-done.1.x2_ref, bf16[1040,128]{1,0:T(8,128)(2,1)S(1)} %collective-permute-done.2.x3_ref), custom_call_target="tpu_custom_call" | custom-call | flops 536870912 | bytes 1572864 | tf_op jit(solution)/shard_map/pallas_call | solution.py:354
  49.5 14.1 %all_to_all.11.in_ref = f32[8,72,128]{2,1,0:T(8,128)S(1)} all-to-all(f32[8,72,128]{2,1,0:T(8,128)S(1)} %shard_map.70), channel_id=1, replica_groups={{16,12,20,8,24,4,28,0},{17,13,21,9,25,5,29,1},{18,14,22,10,26,6,30,2},{..., dimensions={0} | all-to-all | bytes 589824 | tf_op jit(solution)/shard_map/all_to_all | solution.py:363
  63.5 0.7 %shard_map.71 = (f32[4,64,128]{2,1,0:T(8,128)}, f32[4,512]{1,0:T(4,128)}) custom-call(f32[8,72,128]{2,1,0:T(8,128)S(1)} %all_to_all.11.in_ref), custom_call_target="tpu_custom_call" | custom-call | flops 65536 | bytes 524288 | tf_op jit(solution)/shard_map/pallas_call | solution.py:364
Async XLA Ops:
  33.9 7.7 %collective-permute-start.1 = (bf16[1040,128]{1,0:T(8,128)(2,1)S(1)}, bf16[1040,128]{1,0:T(8,128)(2,1)S(1)}, u32[]{:S(2)}, u32[]{:S(2)}) collective-permute-start(bf16[1040,128]{1,0:T(8,128)(2,1)S(1)} %shard_map.69.x0_ref), channel_id=1, source_target_pairs={{0,2},{1,3},{2,0},{3,1},{4,6},{5,7},{6,4},{7,5},{8,10},{9,11},{10,... | collective-permute-start | bytes 798728 | tf_op jit(solution)/shard_map/ppermute | solution.py:351
  37.0 9.5 %collective-permute-start = (bf16[1040,128]{1,0:T(8,128)(2,1)S(1)}, bf16[1040,128]{1,0:T(8,128)(2,1)S(1)}, u32[]{:S(2)}, u32[]{:S(2)}) collective-permute-start(bf16[1040,128]{1,0:T(8,128)(2,1)S(1)} %shard_map.69.x0_ref), channel_id=1, source_target_pairs={{0,1},{1,0},{2,3},{3,2},{4,5},{5,4},{6,7},{7,6},{8,9},{9,8},{10,11... | collective-permute-start | bytes 798728 | tf_op jit(solution)/shard_map/ppermute | solution.py:350
  41.7 6.0 %collective-permute-start.2 = (bf16[1040,128]{1,0:T(8,128)(2,1)S(1)}, bf16[1040,128]{1,0:T(8,128)(2,1)S(1)}, u32[]{:S(2)}, u32[]{:S(2)}) collective-permute-start(bf16[1040,128]{1,0:T(8,128)(2,1)S(1)} %collective-permute-done.1.x2_ref), channel_id=1, source_target_pairs={{0,1},{1,0},{2,3},{3,2},{4,5},{5,4},{6,7},{7,6},{8,9},{9,8},{10,11... | collective-permute-start | bytes 798728 | tf_op jit(solution)/shard_map/ppermute | solution.py:352

commit v11 on v8

--- a/solution.py
+++ b/solution.py
@@ -29,6 +29,7 @@
 CHUNK = 512
 RANK = 128
 Y_ORDER = [4, 3, 5, 2, 6, 1, 7, 0]
+FIRST_PIXEL, FIRST_Y = 10, 5
 F32 = jnp.float32
 BF16 = jnp.bfloat16
 
@@ -42,7 +43,7 @@
 
 
 def block_of(y, z):
-    return ((N_TROW - 1 - y) * N_Z + N_Z - 1 - z) * BLOCK
+    return ((y ^ FIRST_Y) * N_Z + z) * BLOCK
 
 
 def three_parts(x):
@@ -100,7 +101,7 @@
     rank = jnp.concatenate(ranks, axis=1).astype(jnp.int32)
     slot = ((rank + turn * HALF) & (CAP - 1)) + (labels & 1) * CAP
     slot16 = slot.astype(F32).astype(BF16)
-    pair = ((labels >> 1) & 1) * N_PIXEL + N_PIXEL - 1 - labels // OWNED
+    pair = ((labels >> 1) & 1) * N_PIXEL + ((labels // OWNED) ^ FIRST_PIXEL)
     pair16 = pair.astype(F32).astype(BF16)
 
     get_dark.wait()
@@ -202,7 +203,7 @@
                 tiles.append(pltpu.roll(jnp.where(row < 4, g[3], g[2]), 4, axis=0))
                 tiles.append(pltpu.roll(jnp.where(row < 6, g[4], g[3]), 2, axis=0))
             totals.append(sum(total[i : i + 1] for i in range(8, FOUR * MESSAGE, MESSAGE)))
-            tiles = tiles[::-1]
+            tiles = [tiles[p ^ FIRST_PIXEL] for p in range(N_PIXEL)]
             even = jnp.concatenate(tiles[0::2], axis=0).reshape(low.shape)
             odd = jnp.concatenate(tiles[1::2], axis=0).reshape(low.shape)
             early = jnp.where(low, even, odd)
@@ -367,10 +368,10 @@
         ),
     )
     order = [
-        (p * N_TROW + y) * N_Z + z
-        for y in range(N_TROW)[::-1]
-        for z in range(N_Z)[::-1]
-        for p in range(N_PIXEL)[::-1]
+        ((p ^ FIRST_PIXEL) * N_TROW + (y ^ FIRST_Y)) * N_Z + z
+        for y in range(N_TROW)
+        for z in range(N_Z)
+        for p in range(N_PIXEL)
     ]
     arrived = lax.all_to_all(
         payload.reshape(4 * CYCLES, MESSAGE // 2, 2, LANES),

time: 66 us -> 65 us (0.985)
  starting transfers between devices: 4.84 us -> 3.28 us
    ppermute x1, starting transfers between devices: 4.84 us -> 3.28 us  [per_device(): beside = lax.ppermute(packed, 'core', [(0, 1), (1, 0)])]
where the time goes in v11:
time: 65 us; the launch traced here: 64.7 us
  blocking collectives  53.7 us (83%)
  Pallas kernels  5.54 us (9%)
  starting transfers between devices  3.28 us (5%)
  waiting for transfers between devices  1.52 us (2%)
  between operations  0.67 us (1%)
    all_to_all x1, blocking collectives, per_device(): lax.all_to_all(payload.reshape(4 * CYCLES, MESSAGE // 2, 2, LANES), ('pix...  39.4 us
    all_to_all x1, blocking collectives, per_device(): lax.all_to_all(sends, 'trow', 0, 0, tiled=True, axis_index_groups=[Y_ORDER])  14.3 us
    ppermute x1, starting transfers between devices, per_device(): beside = lax.ppermute(packed, 'core', [(0, 1), (1, 0)])  3.28 us
    pallas_call x1, Pallas kernels, per_device(): call(slot_kernel, jax.ShapeDtypeStruct((4 * CYCLES * MESSAGE, LANES), BF1...  2.99 us
    pallas_call x1, Pallas kernels, per_device(): call(gram_kernel, jax.ShapeDtypeStruct((N_TROW, ROWS + 8, LANES), F32), 2...  1.53 us
    ppermute x1, waiting for transfers between devices, per_device(): beside = lax.ppermute(packed, 'core', [(0, 1), (1, 0)])  1.52 us
  transfers between devices with their start and end apart: 1, of which 1 were waited for; matrix products, arithmetic and copies ran while one was open for 0% of the time, Pallas kernels for 0%

profile of v11, /device:TPU:1, one launch (start us, length us, event | category | flops | bytes accessed | tf_op | source)
XLA Modules:
  0.0 64.7 jit_solution(2038686864162370666)
XLA Ops:
  0.6 3.0 %shard_map.68 = bf16[2560,128]{1,0:T(8,128)(2,1)S(1)} custom-call(s32[1]{0:T(128)} %bitcast.2.turn_ref, s32[1,4096]{1,0:T(1,128)} %bitcast.11, s32[1,4096]{1,0:T(1,128)} %bitcast.12, f32[1,4096]{1,0:T(1,128)} %bitcast.13, f32[1,4096]{1,0:T(1,128)} %bitcast.14, s32[16,4096]{1,0:T(8,128)} %counts_hbm.1), custom_call_target="tpu_custom_call" | custom-call | flops 1073741824 | bytes 1048576 | tf_op jit(solution)/shard_map/pallas_call | solution.py:341
  3.6 39.4 %all_to_all.10 = bf16[256,5,2,128]{3,2,1,0:T(2,128)(2,1)S(1)} all-to-all(bf16[256,5,2,128]{3,2,1,0:T(2,128)(2,1)S(1)} %bitcast.10), channel_id=1, replica_groups={{340,372,276,308,468,500,404,436,84,116,20,52,212,244,148,180,342,374,2..., dimensions={0} | all-to-all | bytes 1310720 | tf_op jit(solution)/shard_map/all_to_all | solution.py:376
  43.0 0.4 shard_map.69.x0_ref
  43.4 3.3 %collective-permute-start = (bf16[2064,128]{1,0:T(8,128)(2,1)S(1)}, bf16[2064,128]{1,0:T(8,128)(2,1)S(1)}, u32[]{:S(2)}, u32[]{:S(2)}) collective-permute-start(bf16[2064,128]{1,0:T(8,128)(2,1)S(1)} %shard_map.69.x0_ref), channel_id=1, source_target_pairs={{0,1},{1,0},{2,3},{3,2},{4,5},{5,4},{6,7},{7,6},{8,9},{9,8},{10,11... | collective-permute-start | bytes 1585160 | tf_op jit(solution)/shard_map/ppermute | solution.py:391
  46.7 1.5 %collective-permute-done.x1_ref = bf16[2064,128]{1,0:T(8,128)(2,1)S(1)} collective-permute-done((bf16[2064,128]{1,0:T(8,128)(2,1)S(1)}, bf16[2064,128]{1,0:T(8,128)(2,1)S(1)}, u32[]{:S(2)}, u32[]{:S(2)}) %collective-permute-start) | collective-permute-done | bytes 528416 | tf_op jit(solution)/shard_map/ppermute | solution.py:391
  48.2 1.5 %shard_map.70 = f32[8,72,128]{2,1,0:T(8,128)S(1)} custom-call(s32[1]{0:T(128)} %bitcast.core_ref, s32[1]{0:T(128)} %bitcast.1.z_ref, bf16[2064,128]{1,0:T(8,128)(2,1)S(1)} %shard_map.69.x0_ref, bf16[2064,128]{1,0:T(8,128)(2,1)S(1)} %collective-permute-done.x1_ref), custom_call_target="tpu_custom_call" | custom-call | flops 536870912 | bytes 1572864 | tf_op jit(solution)/shard_map/pallas_call | solution.py:393
  49.7 14.3 %all_to_all.11.in_ref = f32[8,72,128]{2,1,0:T(8,128)S(1)} all-to-all(f32[8,72,128]{2,1,0:T(8,128)S(1)} %shard_map.70), channel_id=1, replica_groups={{16,12,20,8,24,4,28,0},{17,13,21,9,25,5,29,1},{18,14,22,10,26,6,30,2},{..., dimensions={0} | all-to-all | bytes 589824 | tf_op jit(solution)/shard_map/all_to_all | solution.py:402
  64.0 0.7 %shard_map.71 = (f32[4,64,128]{2,1,0:T(8,128)}, f32[4,512]{1,0:T(4,128)}) custom-call(f32[8,72,128]{2,1,0:T(8,128)S(1)} %all_to_all.11.in_ref), custom_call_target="tpu_custom_call" | custom-call | flops 65536 | bytes 524288 | tf_op jit(solution)/shard_map/pallas_call | solution.py:405
Async XLA Ops:
  43.4 4.8 %collective-permute-start = (bf16[2064,128]{1,0:T(8,128)(2,1)S(1)}, bf16[2064,128]{1,0:T(8,128)(2,1)S(1)}, u32[]{:S(2)}, u32[]{:S(2)}) collective-permute-start(bf16[2064,128]{1,0:T(8,128)(2,1)S(1)} %shard_map.69.x0_ref), channel_id=1, source_target_pairs={{0,1},{1,0},{2,3},{3,2},{4,5},{5,4},{6,7},{7,6},{8,9},{9,8},{10,11... | collective-permute-start | bytes 1585160 | tf_op jit(solution)/shard_map/ppermute | solution.py:391

commit v12 on v10

--- a/solution.py
+++ b/solution.py
@@ -276,15 +276,21 @@
         out_ref[at, ROWS + 4 :] = jnp.zeros((4, LANES), F32)
 
 
-def join_kernel(in_ref, tile_ref, lag_ref):
+def join_kernel(in_ref, tile_hbm, lag_ref, tile_ref, sems):
+    puts = []
     for c in range(OWNED):
         both = in_ref[Y_ORDER.index(2 * c)] + in_ref[Y_ORDER.index(2 * c + 1)]
         tile_ref[c] = both[:ROWS]
+        put = pltpu.make_async_copy(tile_ref.at[c], tile_hbm.at[c], sems.at[c])
+        put.start()
+        puts.append(put)
         for b in range(FRAMES // LANES):
             lag_ref[c : c + 1, b * LANES : (b + 1) * LANES] = both[ROWS + b : ROWS + b + 1]
-
-
-def call(body, out_shape, n_in, scalars=0, scratch=(), flops=0, size=0, source=pltpu.VMEM):
+    for put in puts:
+        put.wait()
+
+
+def call(body, out_shape, n_in, scalars=0, scratch=(), flops=0, size=0, source=pltpu.VMEM, first_out=pltpu.VMEM):
     vmem = pl.BlockSpec(memory_space=pltpu.VMEM)
     given = pl.BlockSpec(memory_space=source)
     smem = pl.BlockSpec(memory_space=pltpu.SMEM)
@@ -293,7 +299,7 @@
         body,
         out_shape=out_shape,
         in_specs=[smem] * scalars + [given] * n_in,
-        out_specs=(vmem,) * len(out_shape) if many else vmem,
+        out_specs=(pl.BlockSpec(memory_space=first_out), vmem) if many else vmem,
         scratch_shapes=list(scratch),
         compiler_params=pltpu.CompilerParams(vmem_limit_bytes=32 << 20),
         cost_estimate=pl.CostEstimate(flops=flops, bytes_accessed=size, transcendentals=0),
@@ -368,6 +374,8 @@
             jax.ShapeDtypeStruct((OWNED, FRAMES), F32),
         ),
         1,
+        scratch=[pltpu.VMEM((OWNED, ROWS, COLS), F32), pltpu.SemaphoreType.DMA((OWNED,))],
+        first_out=pltpu.HBM,
         flops=1 << 16,
         size=1 << 19,
     )(gets)

time: 64.6 us -> 65.2 us (level)
  no operation moved by 1% of the time
where the time goes in v12:
time: 65.2 us; the launch traced here: 64.8 us
  blocking collectives  44.2 us (68%)
  starting transfers between devices  12.2 us (19%)
  Pallas kernels  6.23 us (10%)
  waiting for transfers between devices  1.52 us (2%)
  between operations  0.69 us (1%)
    all_to_all x1, blocking collectives, per_device(): lax.all_to_all(payload.reshape(2 * CYCLES, MESSAGE // 2, 2, LANES), ('pix...  30.1 us
    all_to_all x1, blocking collectives, per_device(): lax.all_to_all(sends, 'trow', 0, 0, tiled=True, axis_index_groups=[Y_ORDER])  14.1 us
    ppermute x1, starting transfers between devices, per_device(): corner = lax.ppermute(across, 'tcol', [(k, k ^ 1) for k in range(N_TCOL)])  4.86 us
    ppermute x1, starting transfers between devices, per_device(): beside = lax.ppermute(packed, 'tcol', [(k, k ^ 1) for k in range(N_TCOL)])  4.23 us
    ppermute x1, starting transfers between devices, per_device(): across = lax.ppermute(packed, 'tcol', [(k, k ^ 2) for k in range(N_TCOL)])  3.1 us
    pallas_call x1, Pallas kernels, per_device(): call(slot_kernel, jax.ShapeDtypeStruct((2 * CYCLES * MESSAGE, LANES), BF1...  2.99 us
    pallas_call x1, Pallas kernels, per_device(): call(gram_kernel, jax.ShapeDtypeStruct((N_TROW, ROWS + 8, LANES), F32), 4...  1.75 us
  transfers between devices with their start and end apart: 3, of which 2 were waited for; matrix products, arithmetic and copies ran while one was open for 0% of the time, Pallas kernels for 0%

profile of v12, /device:TPU:1, one launch (start us, length us, event | category | flops | bytes accessed | tf_op | source)
XLA Modules:
  0.0 64.8 jit_solution(1767195294144237024)
XLA Ops:
  0.6 3.0 %shard_map.68 = bf16[1280,128]{1,0:T(8,128)(2,1)S(1)} custom-call(s32[1]{0:T(128)} %bitcast.1.turn_ref, s32[1,4096]{1,0:T(1,128)} %bitcast.10, s32[1,4096]{1,0:T(1,128)} %bitcast.11, f32[1,4096]{1,0:T(1,128)} %bitcast.12, f32[1,4096]{1,0:T(1,128)} %bitcast.13, s32[16,4096]{1,0:T(8,128)} %counts_hbm.1), custom_call_target="tpu_custom_call" | custom-call | flops 1073741824 | bytes 1048576 | tf_op jit(solution)/shard_map/pallas_call | solution.py:312
  3.6 30.1 %all_to_all.10 = bf16[128,5,2,128]{3,2,1,0:T(2,128)(2,1)S(1)} all-to-all(bf16[128,5,2,128]{3,2,1,0:T(2,128)(2,1)S(1)} %bitcast.9), channel_id=1, replica_groups={{340,336,348,344,324,320,332,328,372,368,380,376,356,352,364,360,276,27..., dimensions={0} | all-to-all | bytes 655360 | tf_op jit(solution)/shard_map/all_to_all | solution.py:341
  33.7 0.2 shard_map.69.x0_ref
  33.9 3.1 %collective-permute-start.1 = (bf16[1040,128]{1,0:T(8,128)(2,1)S(1)}, bf16[1040,128]{1,0:T(8,128)(2,1)S(1)}, u32[]{:S(2)}, u32[]{:S(2)}) collective-permute-start(bf16[1040,128]{1,0:T(8,128)(2,1)S(1)} %shard_map.69.x0_ref), channel_id=1, source_target_pairs={{0,2},{1,3},{2,0},{3,1},{4,6},{5,7},{6,4},{7,5},{8,10},{9,11},{10,... | collective-permute-start | bytes 798728 | tf_op jit(solution)/shard_map/ppermute | solution.py:357
  37.0 4.2 %collective-permute-start = (bf16[1040,128]{1,0:T(8,128)(2,1)S(1)}, bf16[1040,128]{1,0:T(8,128)(2,1)S(1)}, u32[]{:S(2)}, u32[]{:S(2)}) collective-permute-start(bf16[1040,128]{1,0:T(8,128)(2,1)S(1)} %shard_map.69.x0_ref), channel_id=1, source_target_pairs={{0,1},{1,0},{2,3},{3,2},{4,5},{5,4},{6,7},{7,6},{8,9},{9,8},{10,11... | collective-permute-start | bytes 798728 | tf_op jit(solution)/shard_map/ppermute | solution.py:356
  41.3 0.4 collective-permute-done.1.x2_ref
  41.7 4.9 %collective-permute-start.2 = (bf16[1040,128]{1,0:T(8,128)(2,1)S(1)}, bf16[1040,128]{1,0:T(8,128)(2,1)S(1)}, u32[]{:S(2)}, u32[]{:S(2)}) collective-permute-start(bf16[1040,128]{1,0:T(8,128)(2,1)S(1)} %collective-permute-done.1.x2_ref), channel_id=1, source_target_pairs={{0,1},{1,0},{2,3},{3,2},{4,5},{5,4},{6,7},{7,6},{8,9},{9,8},{10,11... | collective-permute-start | bytes 798728 | tf_op jit(solution)/shard_map/ppermute | solution.py:358
  46.6 0.0 collective-permute-done.x1_ref
  46.6 1.1 %collective-permute-done.2.x3_ref = bf16[1040,128]{1,0:T(8,128)(2,1)S(1)} collective-permute-done((bf16[1040,128]{1,0:T(8,128)(2,1)S(1)}, bf16[1040,128]{1,0:T(8,128)(2,1)S(1)}, u32[]{:S(2)}, u32[]{:S(2)}) %collective-permute-start.2) | collective-permute-done | bytes 266272 | tf_op jit(solution)/shard_map/ppermute | solution.py:358
  47.7 1.8 %shard_map.70 = f32[8,72,128]{2,1,0:T(8,128)S(1)} custom-call(s32[1]{0:T(128)} %bitcast.me_ref, bf16[1040,128]{1,0:T(8,128)(2,1)S(1)} %shard_map.69.x0_ref, bf16[1040,128]{1,0:T(8,128)(2,1)S(1)} %collective-permute-done.x1_ref, bf16[1040,128]{1,0:T(8,128)(2,1)S(1)} %collective-permute-done.1.x2_ref, bf16[1040,128]{1,0:T(8,128)(2,1)S(1)} %collective-permute-done.2.x3_ref), custom_call_target="tpu_custom_call" | custom-call | flops 536870912 | bytes 1572864 | tf_op jit(solution)/shard_map/pallas_call | solution.py:360
  49.5 14.1 %all_to_all.11.in_ref = f32[8,72,128]{2,1,0:T(8,128)S(1)} all-to-all(f32[8,72,128]{2,1,0:T(8,128)S(1)} %shard_map.70), channel_id=1, replica_groups={{16,12,20,8,24,4,28,0},{17,13,21,9,25,5,29,1},{18,14,22,10,26,6,30,2},{..., dimensions={0} | all-to-all | bytes 589824 | tf_op jit(solution)/shard_map/all_to_all | solution.py:369
  63.5 1.3 %shard_map.71 = (f32[4,64,128]{2,1,0:T(8,128)}, f32[4,512]{1,0:T(4,128)}) custom-call(f32[8,72,128]{2,1,0:T(8,128)S(1)} %all_to_all.11.in_ref), custom_call_target="tpu_custom_call" | custom-call | flops 65536 | bytes 524288 | tf_op jit(solution)/shard_map/pallas_call | solution.py:370
Async XLA Ops:
  33.9 7.7 %collective-permute-start.1 = (bf16[1040,128]{1,0:T(8,128)(2,1)S(1)}, bf16[1040,128]{1,0:T(8,128)(2,1)S(1)}, u32[]{:S(2)}, u32[]{:S(2)}) collective-permute-start(bf16[1040,128]{1,0:T(8,128)(2,1)S(1)} %shard_map.69.x0_ref), channel_id=1, source_target_pairs={{0,2},{1,3},{2,0},{3,1},{4,6},{5,7},{6,4},{7,5},{8,10},{9,11},{10,... | collective-permute-start | bytes 798728 | tf_op jit(solution)/shard_map/ppermute | solution.py:357
  37.0 9.5 %collective-permute-start = (bf16[1040,128]{1,0:T(8,128)(2,1)S(1)}, bf16[1040,128]{1,0:T(8,128)(2,1)S(1)}, u32[]{:S(2)}, u32[]{:S(2)}) collective-permute-start(bf16[1040,128]{1,0:T(8,128)(2,1)S(1)} %shard_map.69.x0_ref), channel_id=1, source_target_pairs={{0,1},{1,0},{2,3},{3,2},{4,5},{5,4},{6,7},{7,6},{8,9},{9,8},{10,11... | collective-permute-start | bytes 798728 | tf_op jit(solution)/shard_map/ppermute | solution.py:356
  41.7 6.0 %collective-permute-start.2 = (bf16[1040,128]{1,0:T(8,128)(2,1)S(1)}, bf16[1040,128]{1,0:T(8,128)(2,1)S(1)}, u32[]{:S(2)}, u32[]{:S(2)}) collective-permute-start(bf16[1040,128]{1,0:T(8,128)(2,1)S(1)} %collective-permute-done.1.x2_ref), channel_id=1, source_target_pairs={{0,1},{1,0},{2,3},{3,2},{4,5},{5,4},{6,7},{7,6},{8,9},{9,8},{10,11... | collective-permute-start | bytes 798728 | tf_op jit(solution)/shard_map/ppermute | solution.py:358
